TPU v7x, 32 devices: a whole 2x2x4 slice. The times are simulated.
32 devices in a mesh: sub: 16 (over z, y, x), coarse: 2 (over core).
Axes of the slice: x: 2, y: 2, z: 4, core: 2. Of those that a mesh axis runs over, the one named last changes fastest.
Arguments:
- right_side: float32 [16, 64, 256], P('sub', None, 'coarse'), may hold values from -6 to 6
- local_blocks: bfloat16 [16, 2, 64, 64, 256], P('sub', None, None, None, 'coarse'), may hold values from -0.5 to 0.5
- diag_blocks: bfloat16 [16, 64, 64, 256], P('sub', None, None, 'coarse'), as said below
- iface_blocks: bfloat16 [16, 64, 64, 192], P('sub', None, None, 'coarse'), may hold values from -0.75 to 0.75
- block_cols: int32 [16, 2, 256], P('sub', None, 'coarse'), may hold values from 0 to 255
- basis: bfloat16 [16, 32, 64, 256], P('sub', None, None, 'coarse'), may hold values from -0.09375 to 0.09375
- coarse_inverse: float32 [512, 512], P('sub'), as said below
Outputs:
- solution_field: float32 [16, 64, 256], P('sub', None, 'coarse')
- residual: float32 [16, 64, 256], P('sub', None, 'coarse')
Inputs may be any that keep to these rules, and one draw needn't show every extreme that they name: `diag_blocks`: each diagonal block is 4 times the identity plus entries of magnitude at most 0.5. `coarse_inverse`: the matrix is the identity plus entries of magnitude at most 4 / sqrt(512).
All inputs are finite; a program needn't handle non-finite values.
Results may differ from a plain program's by a relative error of at most 0.0003.
Values sent between devices are 32-bit elements; how exact they have to be, the bound alone decides.
No kernel may reach another device: no remote copies, remote signals or barrier semaphores. Data moves between devices by JAX's collectives and lax.ppermute only.
A program may use at most 64 MiB of HBM per device.

v0:
```python
import functools

import jax
import jax.numpy as jnp
from jax import lax
from jax.experimental import pallas as pl
from jax.experimental.pallas import tpu as pltpu
from jax.sharding import PartitionSpec as P

SWEEPS = 3
ITERS = 2
BITS = 3
ROWS = 8
WIDE = 3
SCOPED = 6 << 20
HIGH = lax.Precision.HIGHEST


def kernel(body, outs, near, far=(), scratch=()):
    near = [pltpu.with_memory_space_constraint(a, pltpu.VMEM) for a in near]
    far = [pltpu.with_memory_space_constraint(a, pltpu.HBM) for a in far]
    there, here = pl.BlockSpec(memory_space=pl.ANY), pl.BlockSpec(memory_space=pltpu.VMEM)
    return pl.pallas_call(
        body,
        out_shape=outs,
        in_specs=[here] * len(near) + [there] * len(far),
        out_specs=[there if o.memory_space == pltpu.HBM else here for o in outs],
        scratch_shapes=scratch,
        cost_estimate=pl.CostEstimate(flops=0, bytes_accessed=0, transcendentals=0),
        compiler_params=pltpu.CompilerParams(vmem_limit_bytes=SCOPED),
    )(*near, *far)


def vmem(shape, dtype=jnp.float32):
    return pltpu.VMEM(tuple(shape), dtype)


def start_all(sources, targets, done, first=0):
    copies = [
        pltpu.make_async_copy(source, target, done.at[first + at])
        for at, (source, target) in enumerate(zip(sources, targets))
    ]
    for copy in copies:
        copy.start()
    return copies


def wait_all(copies):
    for copy in copies:
        copy.wait()


def by_rows(count, body, step=ROWS):
    def turn(at, carry):
        body(pl.multiple_of(at * step, step))
        return carry

    lax.fori_loop(0, count // step, turn, 0)


def rows_times(blocks, vec, start):
    chunk = blocks[pl.ds(start, ROWS)].astype(jnp.float32)
    return jnp.sum(chunk * vec[None], axis=1)


def block_product(blocks, vec, out):
    def body(start):
        out[pl.ds(start, ROWS), :] = rows_times(blocks, vec, start)

    by_rows(blocks.shape[0], body)


def relaxed(dblock, vec, out, base=None):
    whole = vec[...]

    def body(start):
        here = pl.ds(start, ROWS)
        part = 0.25 * (2.0 * vec[here, :] - 0.25 * rows_times(dblock, whole, start))
        out[here, :] = part if base is None else base[here, :] + part

    by_rows(dblock.shape[0], body)


def restricted(zvec, vec, scratch):
    block_product(zvec, vec, scratch)
    sums = jnp.broadcast_to(jnp.sum(scratch[...], axis=1, keepdims=True), scratch.shape)
    lane = lax.broadcasted_iota(jnp.int32, sums.shape, 1)
    row = lax.broadcasted_iota(jnp.int32, sums.shape, 0)
    return jnp.sum(jnp.where(lax.rem(lane, sums.shape[0]) == row, sums, 0.0), axis=0, keepdims=True)


def post(message, nvec, sums, cross, square):
    sub = lax.axis_index("sub")
    lanes = message.shape[-1]
    lane = lax.broadcasted_iota(jnp.int32, (ROWS, lanes), 1)
    groups = lanes // nvec
    group, place = lane // nvec, lax.rem(lane, nvec)
    pair = jnp.where(place == 0, cross, jnp.where(place == 1, square, 0.0))
    row = jnp.where(group == lax.rem(sub + 1, groups), pair, 0.0)
    row = jnp.where(group == lax.rem(sub, groups), sums, row)
    if len(message.shape) == 3:
        message[...] = jnp.broadcast_to(row[None, : message.shape[1]], message.shape)
    else:
        for at in range(message.shape[0] // ROWS):
            message[at * ROWS : (at + 1) * ROWS, :] = row


def total(x):
    return jnp.sum(x, keepdims=True)


def step_size(arrived, nvec, count):
    lane = lax.broadcasted_iota(jnp.int32, arrived.shape, 1)
    sender = lax.broadcasted_iota(jnp.int32, arrived.shape, 0)
    groups = arrived.shape[1] // nvec
    values = jnp.where(lane // nvec == lax.rem(sender // count + 1, groups), arrived[...], 0.0)
    place = lax.rem(lane, nvec)
    cross = total(jnp.where(place == 0, values, 0.0))
    square = total(jnp.where(place == 1, values, 0.0))
    return cross / (square + 1e-06)


def restriction_rows(arrived, nvec, count):
    lanes = arrived.shape[1]
    each = count * (lanes // nvec)
    lane = lax.broadcasted_iota(jnp.int32, (each, lanes), 1)
    sender = lax.broadcasted_iota(jnp.int32, (each, lanes), 0)
    keep = lane // nvec == sender // count
    return [
        jnp.sum(jnp.where(keep, arrived[at : at + each, :], 0.0), axis=0, keepdims=True)
        for at in range(0, arrived.shape[0], each)
    ]


def weights_here(inverse, rows):
    lanes = rows[0].shape[1]
    acc = inverse[:, :lanes] * rows[0]
    for at in range(1, len(rows)):
        acc = acc + inverse[:, at * lanes : (at + 1) * lanes] * rows[at]
    return jnp.broadcast_to(jnp.sum(acc, axis=1, keepdims=True), acc.shape)


def combined(weights, zvec, value):
    for at in range(weights.shape[0]):
        value = value + weights[at : at + 1, :] * zvec[at].astype(jnp.float32)
    return value


def picked(vec, others, cols, part):
    me = lax.axis_index("coarse")
    width = vec.shape[1]
    index = jnp.broadcast_to(cols[pl.ds(part, 1), :], vec.shape)
    owner = index // width
    place = lax.rem(index, width)

    def lanes(block):
        return jnp.take_along_axis(block, place, axis=1, mode="promise_in_bounds")

    if others.shape[0] == 1:
        return jnp.where(owner == me, lanes(vec[...]), lanes(others[0]))
    value = lanes(others[0])
    for at in range(1, others.shape[0]):
        value = jnp.where(owner == at, lanes(others[at]), value)
    return value


def off_rows(lblocks, chosen, start):
    value = rows_times(lblocks.at[0], chosen[0], start)
    for part in range(1, len(chosen)):
        value = value + rows_times(lblocks.at[part], chosen[part], start)
    return value


def with_interface(known, vec, fblock, out):
    width = fblock.shape[2]
    vec = vec[:, :width]

    def body(start):
        here = pl.ds(start, ROWS)
        add = rows_times(fblock, vec, start)
        pad = jnp.zeros((ROWS, out.shape[1] - width), jnp.float32)
        out[here, :] = known[here, :] + jnp.concatenate([add, pad], axis=1)

    by_rows(out.shape[0], body)


def first_kernel(resid_far, zvec_far, dblock_far, resid, dblock, message_far, zvec, scratch, message, done):
    copies = start_all((resid_far, zvec_far, dblock_far), (resid, zvec, dblock), done)
    wait_all(copies[:2])
    zero = jnp.zeros((1, message.shape[-1]), jnp.float32)
    post(message, zvec.shape[0], restricted(zvec, resid[...], scratch), zero, zero)
    wait_all(copies[2:] + start_all((message,), (message_far,), done, 3))


def relax_kernel(vec, dblock, out):
    relaxed(dblock, vec, out)


def diag_kernel(vec, dblock, *refs):
    count = (len(refs) - 2) // 2
    copies = start_all(refs[:count], refs[count + 1 : -1], refs[-1])
    block_product(dblock, vec[...], refs[count])
    wait_all(copies)


def diag_from_far_kernel(vec, dblock_far, out, dblock, done):
    wait_all(start_all((dblock_far,), (dblock,), done))
    block_product(dblock, vec[...], out)


def apply_kernel(diag_near, vec, others, cols, here, there, fblock_far, out, fblock, arrived, done):
    copies = start_all((there, fblock_far), (arrived, fblock), done)
    dblock, lblocks = (here, arrived) if diag_near else (arrived, here)
    chosen = [picked(vec, others, cols, part) for part in range(lblocks.shape[0])]
    whole = vec[...]

    def own(start):
        return rows_times(dblock, whole, start)

    def off(start):
        return off_rows(lblocks, chosen, start)

    first, second = (own, off) if diag_near else (off, own)

    def begin(start):
        out[pl.ds(start, ROWS), :] = first(start)

    def finish(start):
        rows = pl.ds(start, ROWS)
        out[rows, :] = out[rows, :] + second(start)

    by_rows(out.shape[0], begin)
    copies[0].wait()
    by_rows(out.shape[0], finish)
    copies[1].wait()


def sweep_kernel(state, others, own, resid, dblock, lblocks, cols, out, rest):
    chosen = [picked(state, others, cols, part) for part in range(lblocks.shape[0])]

    def body(start):
        here = pl.ds(start, ROWS)
        rest[here, :] = resid[here, :] - (own[here, :] + off_rows(lblocks, chosen, start))

    by_rows(dblock.shape[0], body)
    relaxed(dblock, rest, out, state)


def direction_kernel(count, state, arrived, zvec, inverse, out):
    rows = restriction_rows(arrived, zvec.shape[0], count)
    out[...] = combined(weights_here(inverse, rows), zvec, state[...])


def near_lanes(parts, inner):
    group = lax.broadcasted_iota(jnp.int32, parts[0].shape, 1) // inner
    value = parts[0][...]
    for at in range(1, len(parts)):
        value = jnp.where(group == at, parts[at][...], value)
    return value


def image_kernel(known, near0, near1, near2, fblock, resid, zvec, dblock, image, state, message_far, scratch, message, done):
    with_interface(known, near_lanes((near0, near1, near2), fblock.shape[2] // BITS), fblock, image)
    value = image[...]
    sums = restricted(zvec, value, scratch)
    post(message, zvec.shape[0], sums, total(resid[...] * value), total(value * value))
    copies = start_all((message,), (message_far,), done)
    relaxed(dblock, image, state)
    wait_all(copies)


def next_direction_kernel(count, state, arrived, zvec, inverse, first, resid, image, out, rest, alpha):
    size = step_size(arrived, zvec.shape[0], count)
    rows = restriction_rows(arrived, zvec.shape[0], count)
    out[...] = first[...] - size * combined(weights_here(inverse, rows), zvec, state[...])
    rest[...] = resid[...] - size * image[...]
    alpha[...] = jnp.broadcast_to(size, alpha.shape)


def last_image_kernel(nvec, known, near0, near1, near2, fblock, resid, image, message):
    with_interface(known, near_lanes((near0, near1, near2), fblock.shape[2] // BITS), fblock, image)
    value = image[...]
    zero = jnp.zeros((1, message.shape[-1]), jnp.float32)
    post(message, nvec, zero, total(resid[...] * value), total(value * value))


def final_kernel(nvec, count, arrived, alpha, first, second, resid, image, field, rest):
    size = step_size(arrived, nvec, count)
    field[0] = alpha[0:1, :] * first[...] + size * second[...]
    rest[0] = resid[...] - size * image[...]


def swap(count, apart):
    return [(low, low ^ apart) for low in range(count) if low ^ apart < count]


def gathered(array, count):
    if count == 2:
        return lax.ppermute(array, "coarse", swap(2, 1))[None]
    return lax.all_gather(array, "coarse", axis=0)


def local(subs, count, right_side, local_blocks, diag_blocks, iface_blocks, block_cols, basis, coarse_inverse):
    lfar, dfar, ffar = local_blocks[0], diag_blocks[0], iface_blocks[0]
    cfar, zfar = block_cols[0], basis[0]
    shape = right_side.shape[1:]
    nvec, lanes = zfar.shape[0], shape[1]
    flat, small, parcel = vmem(shape), vmem((nvec, lanes)), vmem((subs * count, lanes))
    wide = vmem((subs * count, WIDE, lanes))

    def sems(number):
        return pltpu.SemaphoreType.DMA((number,))

    def like(array, space=vmem):
        return space(array.shape, array.dtype)

    def everywhere(message):
        return lax.all_to_all(message, ("sub", "coarse"), 0, 0, tiled=len(message.shape) == 2)

    def sweep(state, others, own, resid, dblock, lblocks, cols):
        (out,) = kernel(sweep_kernel, [flat], [state, others, own, resid, dblock, lblocks, cols], (), [flat])
        return out

    def diag(vec, dblock, *far):
        return kernel(diag_kernel, [flat, *map(like, far)], [vec, dblock], far, [sems(max(len(far), 1))])

    def middle(state, resid, dblock, lblocks, cols):
        for _ in range(SWEEPS - 3):
            others = gathered(state, count)
            (own,) = diag(state, dblock)
            state = sweep(state, others, own, resid, dblock, lblocks, cols)
        return state

    def last_sweep(state, resid, dblock, lblocks, cols):
        others = gathered(state, count)
        own, *held = diag(state, dblock, zfar, coarse_inverse)
        return sweep(state, others, own, resid, dblock, lblocks, cols), held

    def apply(vec, cols, here, there, last=False):
        others = gathered(vec, count)
        near = [lax.ppermute(vec, "sub", swap(subs, 1 << bit)) for bit in range(BITS)]
        outs, scratch = [flat, like(ffar)], [like(there)]
        if not last:
            outs, scratch = outs + scratch, []
        known, fblock, *brought = kernel(
            functools.partial(apply_kernel, len(here.shape) < len(there.shape)),
            outs,
            [vec, others, cols, here],
            [there, ffar],
            [*scratch, sems(2)],
        )
        return [known, *near, fblock], brought

    wide_far = pltpu.HBM(wide.shape, jnp.float32)
    resid, dblock, message = kernel(
        first_kernel,
        [flat, like(dfar), wide_far],
        [],
        [right_side[0], zfar, dfar],
        [like(zfar), small, wide, sems(4)],
    )
    arrived = everywhere(message)[:, 0, :]
    (state,) = kernel(relax_kernel, [flat], [resid, dblock])
    others = gathered(state, count)
    own, lblocks, cols = diag(state, dblock, lfar, cfar)
    state = sweep(state, others, own, resid, dblock, lblocks, cols)
    state = middle(state, resid, dblock, lblocks, cols)
    state, held = last_sweep(state, resid, dblock, lblocks, cols)
    (first,) = kernel(functools.partial(direction_kernel, count), [flat], [state, arrived, *held])
    terms, (lblocks,) = apply(first, cols, dblock, lfar)
    first_image, state, message = kernel(
        image_kernel, [flat, flat, wide_far], [*terms, resid, held[0], dblock], [], [small, wide, sems(1)]
    )
    arrived = everywhere(message)[:, 0, :]
    others = gathered(state, count)
    own, dblock = kernel(diag_from_far_kernel, [flat, like(dfar)], [state], [dfar], [sems(1)])
    state = sweep(state, others, own, first_image, dblock, lblocks, cols)
    state = middle(state, first_image, dblock, lblocks, cols)
    state, held = last_sweep(state, first_image, dblock, lblocks, cols)
    second, rest, alpha = kernel(
        functools.partial(next_direction_kernel, count),
        [flat, flat, vmem((ROWS, lanes))],
        [state, arrived, *held, first, resid, first_image],
    )
    terms, _ = apply(second, cols, lblocks, dfar, True)
    image, message = kernel(functools.partial(last_image_kernel, nvec), [flat, parcel], [*terms, rest])
    arrived = everywhere(message)
    return pl.pallas_call(
        functools.partial(final_kernel, nvec, count),
        out_shape=[jax.ShapeDtypeStruct((1, *shape), jnp.float32)] * 2,
        in_specs=[pl.BlockSpec(memory_space=pltpu.VMEM)] * 6,
        compiler_params=pltpu.CompilerParams(vmem_limit_bytes=SCOPED),
    )(*[pltpu.with_memory_space_constraint(a, pltpu.VMEM) for a in (arrived, alpha, first, second, rest, image)])


def solution(mesh):
    placed = (
        P("sub", None, "coarse"),
        P("sub", None, None, None, "coarse"),
        P("sub", None, None, "coarse"),
        P("sub", None, None, "coarse"),
        P("sub", None, "coarse"),
        P("sub", None, None, "coarse"),
        P("sub", None),
    )
    return jax.shard_map(
        functools.partial(local, mesh.shape["sub"], mesh.shape["coarse"]),
        mesh=mesh,
        in_specs=placed,
        out_specs=(P("sub", None, "coarse"), P("sub", None, "coarse")),
        check_vma=False,
    )
```

profile of v0, /device:TPU:0, one launch (start us, length us, event | category | flops | bytes accessed | tf_op | source)
XLA Modules:
  0.0 53.4 jit_solution(10358382788938410651)
XLA Ops:
  0.6 2.0 %shard_map.86 = (f32[64,128]{1,0:T(8,128)S(1)}, bf16[64,64,128]{2,1,0:T(8,128)(2,1)S(1)}, f32[32,3,128]{2,1,0:T(4,128)}) custom-call(f32[64,128]{1,0:T(8,128)} %bitcast.42, bf16[32,64,128]{2,1,0:T(8,128)(2,1)} %bitcast.37, bf16[64,64,128]{2,1,0:T(8,128)(2,1)} %bitcast.32), custom_call_target="tpu_custom_call" | custom-call | tf_op jit(solution)/shard_map/pallas_call | solution.py:23
  2.6 7.3 %all-to-all-start = ((f32[32,3,128]{2,1,0:T(4,128)}), f32[32,3,128]{2,1,0:T(4,128)S(1)}, u32[]{:S(2)}, u32[]{:S(2)}) async-start(f32[32,3,128]{2,1,0:T(4,128)} %get-tuple-element.35), calls=%async_computation | async-start | bytes 131072 | tf_op jit(solution)/shard_map/all_to_all | solution.py:318
  9.9 0.3 shard_map.87.vec.state
  10.3 0.3 collective-permute-start
  10.6 1.6 %shard_map.88 = (f32[64,128]{1,0:T(8,128)S(1)}, bf16[2,64,64,128]{3,2,1,0:T(8,128)(2,1)S(1)}, s32[2,128]{1,0:T(2,128)S(1)}) custom-call(f32[64,128]{1,0:T(8,128)S(1)} %shard_map.87.vec.state, bf16[64,64,128]{2,1,0:T(8,128)(2,1)S(1)} %get-tuple-element.30.dblock.here, bf16[2,64,64,128]{3,2,1,0:T(8,128)(2,1)} %bitcast.35, s32[2,128]{1,0:T(2,128)} %bitcast.43), custom_call_target="tpu_custom_call" | custom-call | tf_op jit(solution)/shard_map/pallas_call | solution.py:23
  12.2 0.0 collective-permute-done
  12.2 1.0 %shard_map.89.vec.state = f32[64,128]{1,0:T(8,128)S(1)} custom-call(f32[64,128]{1,0:T(8,128)S(1)} %shard_map.87.vec.state, f32[1,64,128]{2,1,0:T(8,128)S(1)} %bitcast.28, f32[64,128]{1,0:T(8,128)S(1)} %get-tuple-element.31.own, f32[64,128]{1,0:T(8,128)S(1)} %get-tuple-element.29.vec.resid, bf16[64,64,128]{2,1,0:T(8,128)(2,1)S(1)} %get-tuple-element.30.dblock.here, ...), custom_call_target="tpu_custom_call" | custom-call | tf_op jit(solution)/shard_map/pallas_call | solution.py:23
  13.3 0.3 collective-permute-start.1
  13.6 1.1 %shard_map.90 = (f32[64,128]{1,0:T(8,128)S(1)}, bf16[32,64,128]{2,1,0:T(8,128)(2,1)S(1)}, f32[32,512]{1,0:T(8,128)S(1)}) custom-call(f32[64,128]{1,0:T(8,128)S(1)} %shard_map.89.vec.state, bf16[64,64,128]{2,1,0:T(8,128)(2,1)S(1)} %get-tuple-element.30.dblock.here, bf16[32,64,128]{2,1,0:T(8,128)(2,1)} %bitcast.38, f32[32,512]{1,0:T(8,128)} %refs_1_.3), custom_call_target="tpu_custom_call" | custom-call | tf_op jit(solution)/shard_map/pallas_call | solution.py:23
  14.7 0.0 copy-start
  14.7 0.0 collective-permute-done.1
  14.7 1.0 %shard_map.91.state = f32[64,128]{1,0:T(8,128)S(1)} custom-call(f32[64,128]{1,0:T(8,128)S(1)} %shard_map.89.vec.state, f32[1,64,128]{2,1,0:T(8,128)S(1)} %bitcast.29, f32[64,128]{1,0:T(8,128)S(1)} %get-tuple-element.34.own, f32[64,128]{1,0:T(8,128)S(1)} %get-tuple-element.29.vec.resid, bf16[64,64,128]{2,1,0:T(8,128)(2,1)S(1)} %get-tuple-element.30.dblock.here, ...), custom_call_target="tpu_custom_call" | custom-call | tf_op jit(solution)/shard_map/pallas_call | solution.py:23
  15.7 1.6 %all-to-all-done = f32[32,3,128]{2,1,0:T(4,128)S(1)} async-done(((f32[32,3,128]{2,1,0:T(4,128)}), f32[32,3,128]{2,1,0:T(4,128)S(1)}, u32[]{:S(2)}, u32[]{:S(2)}) %all-to-all-start) | async-done | bytes 49184 | tf_op jit(solution)/shard_map/all_to_all | solution.py:318
  17.4 0.2 shard_map.92.vec.first
  17.6 0.2 collective-permute-start.2
  17.8 0.6 %collective-permute-start.5 = (f32[64,128]{1,0:T(8,128)S(1)}, f32[64,128]{1,0:T(8,128)S(1)}, u32[]{:S(2)}, u32[]{:S(2)}) collective-permute-start(f32[64,128]{1,0:T(8,128)S(1)} %shard_map.92.vec.first), channel_id=1, source_target_pairs={{0,8},{2,10},{4,12},{6,14},{8,0},{10,2},{12,4},{14,6},{16,24},{18,... | collective-permute-start | bytes 98312 | tf_op jit(solution)/shard_map/ppermute | solution.py:341
  18.3 1.1 %collective-permute-start.4 = (f32[64,128]{1,0:T(8,128)S(1)}, f32[64,128]{1,0:T(8,128)S(1)}, u32[]{:S(2)}, u32[]{:S(2)}) collective-permute-start(f32[64,128]{1,0:T(8,128)S(1)} %shard_map.92.vec.first), channel_id=1, source_target_pairs={{0,4},{2,6},{4,0},{6,2},{8,12},{10,14},{12,8},{14,10},{16,20},{18,... | collective-permute-start | bytes 98312 | tf_op jit(solution)/shard_map/ppermute | solution.py:341
  19.4 1.5 %collective-permute-start.3 = (f32[64,128]{1,0:T(8,128)S(1)}, f32[64,128]{1,0:T(8,128)S(1)}, u32[]{:S(2)}, u32[]{:S(2)}) collective-permute-start(f32[64,128]{1,0:T(8,128)S(1)} %shard_map.92.vec.first), channel_id=1, source_target_pairs={{0,2},{2,0},{4,6},{6,4},{8,10},{10,8},{12,14},{14,12},{16,18},{18,... | collective-permute-start | bytes 98312 | tf_op jit(solution)/shard_map/ppermute | solution.py:341
  20.9 0.0 collective-permute-done.2
  20.9 2.2 %shard_map.93 = (f32[64,128]{1,0:T(8,128)S(1)}, bf16[64,64,96]{2,1,0:T(8,128)(2,1)S(1)}, bf16[2,64,64,128]{3,2,1,0:T(8,128)(2,1)S(1)}) custom-call(f32[64,128]{1,0:T(8,128)S(1)} %shard_map.92.vec.first, f32[1,64,128]{2,1,0:T(8,128)S(1)} %bitcast.26, s32[2,128]{1,0:T(2,128)S(1)} %get-tuple-element.33.cols, ...), custom_call_target="tpu_custom_call" | custom-call | tf_op jit(solution)/shard_map/pallas_call | solution.py:23
  23.1 0.0 collective-permute-done.5.near2
  23.2 0.0 collective-permute-done.4.near1
  23.2 0.2 collective-permute-done.3.near0
  23.3 0.0 copy-done.1
  23.3 1.3 %shard_map.94 = (f32[64,128]{1,0:T(8,128)S(1)}, f32[64,128]{1,0:T(8,128)S(1)}, f32[32,3,128]{2,1,0:T(4,128)}) custom-call(f32[64,128]{1,0:T(8,128)S(1)} %get-tuple-element.38.known, f32[64,128]{1,0:T(8,128)S(1)} %collective-permute-done.3.near0, f32[64,128]{1,0:T(8,128)S(1)} %collective-permute-done.4.near1, f32[64,128]{1,0:T(8,128)S(1)} %collective-permute-done.5.near2, ...), custom_call_target="tpu_custom_call" | custom-call | tf_op jit(solution)/shard_map/pallas_call | solution.py:23
  24.7 3.7 %all-to-all-start.1 = ((f32[32,3,128]{2,1,0:T(4,128)}), f32[32,3,128]{2,1,0:T(4,128)S(1)}, u32[]{:S(2)}, u32[]{:S(2)}) async-start(f32[32,3,128]{2,1,0:T(4,128)} %get-tuple-element.46), calls=%async_computation.1 | async-start | bytes 131072 | tf_op jit(solution)/shard_map/all_to_all | solution.py:318
  28.4 0.3 collective-permute-start.6
  28.7 1.5 %shard_map.95 = (f32[64,128]{1,0:T(8,128)S(1)}, bf16[64,64,128]{2,1,0:T(8,128)(2,1)S(1)}) custom-call(f32[64,128]{1,0:T(8,128)S(1)} %get-tuple-element.40.vec.state, bf16[64,64,128]{2,1,0:T(8,128)(2,1)} %bitcast.33), custom_call_target="tpu_custom_call" | custom-call | tf_op jit(solution)/shard_map/pallas_call | solution.py:23
  30.3 0.0 collective-permute-done.6
  30.3 1.0 %shard_map.96.vec.state = f32[64,128]{1,0:T(8,128)S(1)} custom-call(f32[64,128]{1,0:T(8,128)S(1)} %get-tuple-element.40.vec.state, f32[1,64,128]{2,1,0:T(8,128)S(1)} %bitcast.27, f32[64,128]{1,0:T(8,128)S(1)} %get-tuple-element.41.own, f32[64,128]{1,0:T(8,128)S(1)} %get-tuple-element.42.resid.image, bf16[64,64,128]{2,1,0:T(8,128)(2,1)S(1)} %get-tuple-element.43.dblock, ...), custom_call_target="tpu_custom_call" | custom-call | tf_op jit(solution)/shard_map/pallas_call | solution.py:23
  31.3 0.3 collective-permute-start.7
  31.6 1.1 %shard_map.97 = (f32[64,128]{1,0:T(8,128)S(1)}, bf16[32,64,128]{2,1,0:T(8,128)(2,1)S(1)}, f32[32,512]{1,0:T(8,128)S(1)}) custom-call(f32[64,128]{1,0:T(8,128)S(1)} %shard_map.96.vec.state, bf16[64,64,128]{2,1,0:T(8,128)(2,1)S(1)} %get-tuple-element.43.dblock, bf16[32,64,128]{2,1,0:T(8,128)(2,1)} %bitcast.39, f32[32,512]{1,0:T(8,128)} %refs_1_.3), custom_call_target="tpu_custom_call" | custom-call | tf_op jit(solution)/shard_map/pallas_call | solution.py:23
  32.7 0.0 collective-permute-done.7
  32.7 1.0 %shard_map.98.state = f32[64,128]{1,0:T(8,128)S(1)} custom-call(f32[64,128]{1,0:T(8,128)S(1)} %shard_map.96.vec.state, f32[1,64,128]{2,1,0:T(8,128)S(1)} %bitcast.30, f32[64,128]{1,0:T(8,128)S(1)} %get-tuple-element.45.own, f32[64,128]{1,0:T(8,128)S(1)} %get-tuple-element.42.resid.image, bf16[64,64,128]{2,1,0:T(8,128)(2,1)S(1)} %get-tuple-element.43.dblock, ...), custom_call_target="tpu_custom_call" | custom-call | tf_op jit(solution)/shard_map/pallas_call | solution.py:23
  33.7 2.1 %all-to-all-done.1 = f32[32,3,128]{2,1,0:T(4,128)S(1)} async-done(((f32[32,3,128]{2,1,0:T(4,128)}), f32[32,3,128]{2,1,0:T(4,128)S(1)}, u32[]{:S(2)}, u32[]{:S(2)}) %all-to-all-start.1) | async-done | bytes 49184 | tf_op jit(solution)/shard_map/all_to_all | solution.py:318
  35.8 0.2 shard_map.99
  36.0 0.2 collective-permute-start.8
  36.2 0.6 %collective-permute-start.11 = (f32[64,128]{1,0:T(8,128)S(1)}, f32[64,128]{1,0:T(8,128)S(1)}, u32[]{:S(2)}, u32[]{:S(2)}) collective-permute-start(f32[64,128]{1,0:T(8,128)S(1)} %get-tuple-element.49.vec.second), channel_id=1, source_target_pairs={{0,8},{2,10},{4,12},{6,14},{8,0},{10,2},{12,4},{14,6},{16,24},{18,... | collective-permute-start | bytes 98312 | tf_op jit(solution)/shard_map/ppermute | solution.py:341
  36.8 0.7 %collective-permute-start.10 = (f32[64,128]{1,0:T(8,128)S(1)}, f32[64,128]{1,0:T(8,128)S(1)}, u32[]{:S(2)}, u32[]{:S(2)}) collective-permute-start(f32[64,128]{1,0:T(8,128)S(1)} %get-tuple-element.49.vec.second), channel_id=1, source_target_pairs={{0,4},{2,6},{4,0},{6,2},{8,12},{10,14},{12,8},{14,10},{16,20},{18,... | collective-permute-start | bytes 98312 | tf_op jit(solution)/shard_map/ppermute | solution.py:341
  37.5 1.4 %collective-permute-start.9 = (f32[64,128]{1,0:T(8,128)S(1)}, f32[64,128]{1,0:T(8,128)S(1)}, u32[]{:S(2)}, u32[]{:S(2)}) collective-permute-start(f32[64,128]{1,0:T(8,128)S(1)} %get-tuple-element.49.vec.second), channel_id=1, source_target_pairs={{0,2},{2,0},{4,6},{6,4},{8,10},{10,8},{12,14},{14,12},{16,18},{18,... | collective-permute-start | bytes 98312 | tf_op jit(solution)/shard_map/ppermute | solution.py:341
  38.9 0.0 collective-permute-done.8
  38.9 1.6 %shard_map.100 = (f32[64,128]{1,0:T(8,128)S(1)}, bf16[64,64,96]{2,1,0:T(8,128)(2,1)S(1)}) custom-call(f32[64,128]{1,0:T(8,128)S(1)} %get-tuple-element.49.vec.second, f32[1,64,128]{2,1,0:T(8,128)S(1)} %bitcast.25, s32[2,128]{1,0:T(2,128)S(1)} %get-tuple-element.33.cols, bf16[2,64,64,128]{3,2,1,0:T(8,128)(2,1)S(1)} %get-tuple-element.44.lblocks.here, ...), custom_call_target="tpu_custom_call" | custom-call | tf_op jit(solution)/shard_map/pallas_call | solution.py:23
  40.5 0.0 collective-permute-done.11.near2
  40.5 0.2 collective-permute-done.10.near1
  40.7 0.7 %collective-permute-done.9.near0 = f32[64,128]{1,0:T(8,128)S(1)} collective-permute-done((f32[64,128]{1,0:T(8,128)S(1)}, f32[64,128]{1,0:T(8,128)S(1)}, u32[]{:S(2)}, u32[]{:S(2)}) %collective-permute-start.9) | collective-permute-done | bytes 32800 | tf_op jit(solution)/shard_map/ppermute | solution.py:341
  41.4 0.5 %shard_map.101 = (f32[64,128]{1,0:T(8,128)S(1)}, f32[32,128]{1,0:T(8,128)S(1)}) custom-call(f32[64,128]{1,0:T(8,128)S(1)} %get-tuple-element.50.known, f32[64,128]{1,0:T(8,128)S(1)} %collective-permute-done.9.near0, f32[64,128]{1,0:T(8,128)S(1)} %collective-permute-done.10.near1, f32[64,128]{1,0:T(8,128)S(1)} %collective-permute-done.11.near2, ...), custom_call_target="tpu_custom_call" | custom-call | tf_op jit(solution)/shard_map/pallas_call | solution.py:23
  41.9 10.7 %all_to_all.21 = f32[32,1,128]{2,1,0:T(1,128)S(1)} all-to-all(f32[32,1,128]{2,1,0:T(1,128)S(1)} %bitcast.31), channel_id=1, replica_groups=mesh['sub'=16,'coarse'=2] {'sub','coarse'}, dimensions={0} | all-to-all | bytes 32768 | tf_op jit(solution)/shard_map/all_to_all | solution.py:318
  52.6 0.8 %shard_map.102 = (f32[1,64,128]{2,1,0:T(8,128)}, f32[1,64,128]{2,1,0:T(8,128)}) custom-call(f32[32,128]{1,0:T(8,128)S(1)} %bitcast.23, f32[8,128]{1,0:T(8,128)S(1)} %get-tuple-element.54.alpha, f32[64,128]{1,0:T(8,128)S(1)} %shard_map.92.vec.first, f32[64,128]{1,0:T(8,128)S(1)} %get-tuple-element.49.vec.second, f32[64,128]{1,0:T(8,128)S(1)} %get-tuple-element.52.resid, ...), custom_call_target="tpu_custom_call" | custom-call | tf_op jit(solution)/shard_map/pallas_call | solution.py:388
  (4 shorter events, 0.0 us)
Async XLA Ops:
  2.6 14.7 %all-to-all-start = ((f32[32,3,128]{2,1,0:T(4,128)}), f32[32,3,128]{2,1,0:T(4,128)S(1)}, u32[]{:S(2)}, u32[]{:S(2)}) async-start(f32[32,3,128]{2,1,0:T(4,128)} %get-tuple-element.35), calls=%async_computation | async-start | bytes 131072 | tf_op jit(solution)/shard_map/all_to_all | solution.py:318
  10.3 1.9 %collective-permute-start = (f32[64,128]{1,0:T(8,128)S(1)}, f32[64,128]{1,0:T(8,128)S(1)}, u32[]{:S(2)}, u32[]{:S(2)}) collective-permute-start(f32[64,128]{1,0:T(8,128)S(1)} %shard_map.87.vec.state), channel_id=1, source_target_pairs={{0,1},{1,0},{2,3},{3,2},{4,5},{5,4},{6,7},{7,6},{8,9},{9,8},{10,11... | collective-permute-start | bytes 98312 | tf_op jit(solution)/shard_map/ppermute | solution.py:299
  13.3 1.4 %collective-permute-start.1 = (f32[64,128]{1,0:T(8,128)S(1)}, f32[64,128]{1,0:T(8,128)S(1)}, u32[]{:S(2)}, u32[]{:S(2)}) collective-permute-start(f32[64,128]{1,0:T(8,128)S(1)} %shard_map.89.vec.state), channel_id=1, source_target_pairs={{0,1},{1,0},{2,3},{3,2},{4,5},{5,4},{6,7},{7,6},{8,9},{9,8},{10,11... | collective-permute-start | bytes 98312 | tf_op jit(solution)/shard_map/ppermute | solution.py:299
  14.7 6.2 %copy-start = (bf16[32,64,128]{2,1,0:T(8,128)(2,1)}, bf16[32,64,128]{2,1,0:T(8,128)(2,1)S(1)}, u32[]{:S(2)}) copy-start(bf16[32,64,128]{2,1,0:T(8,128)(2,1)S(1)} %get-tuple-element.36.zvec) | copy-start | bytes 1572868
  17.6 3.3 %collective-permute-start.2 = (f32[64,128]{1,0:T(8,128)S(1)}, f32[64,128]{1,0:T(8,128)S(1)}, u32[]{:S(2)}, u32[]{:S(2)}) collective-permute-start(f32[64,128]{1,0:T(8,128)S(1)} %shard_map.92.vec.first), channel_id=1, source_target_pairs={{0,1},{1,0},{2,3},{3,2},{4,5},{5,4},{6,7},{7,6},{8,9},{9,8},{10,11... | collective-permute-start | bytes 98312 | tf_op jit(solution)/shard_map/ppermute | solution.py:299
  17.8 5.4 %collective-permute-start.5 = (f32[64,128]{1,0:T(8,128)S(1)}, f32[64,128]{1,0:T(8,128)S(1)}, u32[]{:S(2)}, u32[]{:S(2)}) collective-permute-start(f32[64,128]{1,0:T(8,128)S(1)} %shard_map.92.vec.first), channel_id=1, source_target_pairs={{0,8},{2,10},{4,12},{6,14},{8,0},{10,2},{12,4},{14,6},{16,24},{18,... | collective-permute-start | bytes 98312 | tf_op jit(solution)/shard_map/ppermute | solution.py:341
  18.3 4.8 %collective-permute-start.4 = (f32[64,128]{1,0:T(8,128)S(1)}, f32[64,128]{1,0:T(8,128)S(1)}, u32[]{:S(2)}, u32[]{:S(2)}) collective-permute-start(f32[64,128]{1,0:T(8,128)S(1)} %shard_map.92.vec.first), channel_id=1, source_target_pairs={{0,4},{2,6},{4,0},{6,2},{8,12},{10,14},{12,8},{14,10},{16,20},{18,... | collective-permute-start | bytes 98312 | tf_op jit(solution)/shard_map/ppermute | solution.py:341
  19.4 3.9 %collective-permute-start.3 = (f32[64,128]{1,0:T(8,128)S(1)}, f32[64,128]{1,0:T(8,128)S(1)}, u32[]{:S(2)}, u32[]{:S(2)}) collective-permute-start(f32[64,128]{1,0:T(8,128)S(1)} %shard_map.92.vec.first), channel_id=1, source_target_pairs={{0,2},{2,0},{4,6},{6,4},{8,10},{10,8},{12,14},{14,12},{16,18},{18,... | collective-permute-start | bytes 98312 | tf_op jit(solution)/shard_map/ppermute | solution.py:341
  20.9 2.4 %copy-start.1 = (bf16[32,64,128]{2,1,0:T(8,128)(2,1)S(1)}, bf16[32,64,128]{2,1,0:T(8,128)(2,1)}, u32[]{:S(2)}) copy-start(bf16[32,64,128]{2,1,0:T(8,128)(2,1)} %copy-done) | copy-start | bytes 1572868
  24.7 11.1 %all-to-all-start.1 = ((f32[32,3,128]{2,1,0:T(4,128)}), f32[32,3,128]{2,1,0:T(4,128)S(1)}, u32[]{:S(2)}, u32[]{:S(2)}) async-start(f32[32,3,128]{2,1,0:T(4,128)} %get-tuple-element.46), calls=%async_computation.1 | async-start | bytes 131072 | tf_op jit(solution)/shard_map/all_to_all | solution.py:318
  28.4 1.9 %collective-permute-start.6 = (f32[64,128]{1,0:T(8,128)S(1)}, f32[64,128]{1,0:T(8,128)S(1)}, u32[]{:S(2)}, u32[]{:S(2)}) collective-permute-start(f32[64,128]{1,0:T(8,128)S(1)} %get-tuple-element.40.vec.state), channel_id=1, source_target_pairs={{0,1},{1,0},{2,3},{3,2},{4,5},{5,4},{6,7},{7,6},{8,9},{9,8},{10,11... | collective-permute-start | bytes 98312 | tf_op jit(solution)/shard_map/ppermute | solution.py:299
  31.3 1.4 %collective-permute-start.7 = (f32[64,128]{1,0:T(8,128)S(1)}, f32[64,128]{1,0:T(8,128)S(1)}, u32[]{:S(2)}, u32[]{:S(2)}) collective-permute-start(f32[64,128]{1,0:T(8,128)S(1)} %shard_map.96.vec.state), channel_id=1, source_target_pairs={{0,1},{1,0},{2,3},{3,2},{4,5},{5,4},{6,7},{7,6},{8,9},{9,8},{10,11... | collective-permute-start | bytes 98312 | tf_op jit(solution)/shard_map/ppermute | solution.py:299
  36.0 2.9 %collective-permute-start.8 = (f32[64,128]{1,0:T(8,128)S(1)}, f32[64,128]{1,0:T(8,128)S(1)}, u32[]{:S(2)}, u32[]{:S(2)}) collective-permute-start(f32[64,128]{1,0:T(8,128)S(1)} %get-tuple-element.49.vec.second), channel_id=1, source_target_pairs={{0,1},{1,0},{2,3},{3,2},{4,5},{5,4},{6,7},{7,6},{8,9},{9,8},{10,11... | collective-permute-start | bytes 98312 | tf_op jit(solution)/shard_map/ppermute | solution.py:299
  36.2 4.3 %collective-permute-start.11 = (f32[64,128]{1,0:T(8,128)S(1)}, f32[64,128]{1,0:T(8,128)S(1)}, u32[]{:S(2)}, u32[]{:S(2)}) collective-permute-start(f32[64,128]{1,0:T(8,128)S(1)} %get-tuple-element.49.vec.second), channel_id=1, source_target_pairs={{0,8},{2,10},{4,12},{6,14},{8,0},{10,2},{12,4},{14,6},{16,24},{18,... | collective-permute-start | bytes 98312 | tf_op jit(solution)/shard_map/ppermute | solution.py:341
  36.8 3.9 %collective-permute-start.10 = (f32[64,128]{1,0:T(8,128)S(1)}, f32[64,128]{1,0:T(8,128)S(1)}, u32[]{:S(2)}, u32[]{:S(2)}) collective-permute-start(f32[64,128]{1,0:T(8,128)S(1)} %get-tuple-element.49.vec.second), channel_id=1, source_target_pairs={{0,4},{2,6},{4,0},{6,2},{8,12},{10,14},{12,8},{14,10},{16,20},{18,... | collective-permute-start | bytes 98312 | tf_op jit(solution)/shard_map/ppermute | solution.py:341
  37.5 3.9 %collective-permute-start.9 = (f32[64,128]{1,0:T(8,128)S(1)}, f32[64,128]{1,0:T(8,128)S(1)}, u32[]{:S(2)}, u32[]{:S(2)}) collective-permute-start(f32[64,128]{1,0:T(8,128)S(1)} %get-tuple-element.49.vec.second), channel_id=1, source_target_pairs={{0,2},{2,0},{4,6},{6,4},{8,10},{10,8},{12,14},{14,12},{16,18},{18,... | collective-permute-start | bytes 98312 | tf_op jit(solution)/shard_map/ppermute | solution.py:341
where the time goes:
time: 53.8 us; the launch traced here: 53.4 us
  Pallas kernels  18.6 us (35%)
  starting transfers between devices  18.5 us (34%)
  blocking collectives  10.7 us (20%)
  waiting for transfers between devices  4.77 us (9%)
  between operations  0.85 us (2%)
    pallas_call x16, Pallas kernels, kernel(): pl.pallas_call(body, out_shape=outs, in_specs=[here] * len(near) + [there...  17.8 us
    all_to_all x2, starting transfers between devices, everywhere(): lax.all_to_all(message, ('sub', 'coarse'), 0, 0, tiled=len(message.shape)...  11 us
    all_to_all x1, blocking collectives, everywhere(): lax.all_to_all(message, ('sub', 'coarse'), 0, 0, tiled=len(message.shape)...  10.7 us
    ppermute x6, starting transfers between devices, apply(): lax.ppermute(vec, 'sub', swap(subs, 1 << bit))  5.81 us
    all_to_all x2, waiting for transfers between devices, everywhere(): lax.all_to_all(message, ('sub', 'coarse'), 0, 0, tiled=len(message.shape)...  3.71 us
    ppermute x6, starting transfers between devices, gathered(): return lax.ppermute(array, 'coarse', swap(2, 1))[None]  1.64 us
  transfers between devices with their start and end apart: 14, of which 5 were waited for; matrix products, arithmetic and copies ran while one was open for 0% of the time, Pallas kernels for 25%

commit v1 on v0

--- a/solution.py
+++ b/solution.py
@@ -51,11 +51,8 @@
 
 
 def by_rows(count, body, step=ROWS):
-    def turn(at, carry):
-        body(pl.multiple_of(at * step, step))
-        return carry
-
-    lax.fori_loop(0, count // step, turn, 0)
+    for start in range(0, count, step):
+        body(start)
 
 
 def rows_times(blocks, vec, start):
@@ -81,28 +78,31 @@
     by_rows(dblock.shape[0], body)
 
 
-def restricted(zvec, vec, scratch):
-    block_product(zvec, vec, scratch)
+def dot_rows(left, right):
+    return jnp.sum(left * right, axis=0, keepdims=True)
+
+
+def post(message, scratch):
+    sub = lax.axis_index("sub")
+    lanes = scratch.shape[1]
+    nvec = scratch.shape[0] - ROWS
+    groups = lanes // nvec
     sums = jnp.broadcast_to(jnp.sum(scratch[...], axis=1, keepdims=True), scratch.shape)
-    lane = lax.broadcasted_iota(jnp.int32, sums.shape, 1)
-    row = lax.broadcasted_iota(jnp.int32, sums.shape, 0)
-    return jnp.sum(jnp.where(lax.rem(lane, sums.shape[0]) == row, sums, 0.0), axis=0, keepdims=True)
-
-
-def post(message, nvec, sums, cross, square):
-    sub = lax.axis_index("sub")
-    lanes = message.shape[-1]
-    lane = lax.broadcasted_iota(jnp.int32, (ROWS, lanes), 1)
-    groups = lanes // nvec
-    group, place = lane // nvec, lax.rem(lane, nvec)
-    pair = jnp.where(place == 0, cross, jnp.where(place == 1, square, 0.0))
-    row = jnp.where(group == lax.rem(sub + 1, groups), pair, 0.0)
-    row = jnp.where(group == lax.rem(sub, groups), sums, row)
+    lane = lax.broadcasted_iota(jnp.int32, scratch.shape, 1)
+    row = lax.broadcasted_iota(jnp.int32, scratch.shape, 0)
+    place = lax.rem(sub + row // nvec, groups) * nvec + lax.rem(row, nvec)
+    line = jnp.sum(jnp.where(lane == place, sums, 0.0), axis=0, keepdims=True)
     if len(message.shape) == 3:
-        message[...] = jnp.broadcast_to(row[None, : message.shape[1]], message.shape)
+        message[...] = jnp.broadcast_to(line[None], message.shape)
     else:
-        for at in range(message.shape[0] // ROWS):
-            message[at * ROWS : (at + 1) * ROWS, :] = row
+        message[...] = jnp.broadcast_to(line, message.shape)
+
+
+def inner_products(scratch, resid, image):
+    nvec = scratch.shape[0] - ROWS
+    scratch[nvec:, :] = jnp.concatenate(
+        [dot_rows(resid, image), dot_rows(image, image), jnp.zeros((ROWS - 2, image.shape[1]), jnp.float32)], axis=0
+    )
 
 
 def total(x):
@@ -184,16 +184,24 @@
     by_rows(out.shape[0], body)
 
 
-def first_kernel(resid_far, zvec_far, dblock_far, resid, dblock, message_far, zvec, scratch, message, done):
-    copies = start_all((resid_far, zvec_far, dblock_far), (resid, zvec, dblock), done)
-    wait_all(copies[:2])
-    zero = jnp.zeros((1, message.shape[-1]), jnp.float32)
-    post(message, zvec.shape[0], restricted(zvec, resid[...], scratch), zero, zero)
-    wait_all(copies[2:] + start_all((message,), (message_far,), done, 3))
-
-
-def relax_kernel(vec, dblock, out):
-    relaxed(dblock, vec, out)
+def first_kernel(resid_far, zvec_far, dblock_far, resid, dblock, state, message_far, zvec, scratch, message, done):
+    pieces = [pl.ds(at, ROWS) for at in range(0, zvec.shape[0], ROWS)]
+    copies = start_all(
+        [resid_far, *[zvec_far.at[piece] for piece in pieces], dblock_far],
+        [resid, *[zvec.at[piece] for piece in pieces], dblock],
+        done,
+    )
+    copies[0].wait()
+    vec = resid[...]
+    for copy, piece in zip(copies[1:-1], pieces):
+        copy.wait()
+        scratch[piece, :] = rows_times(zvec, vec, piece.start)
+    scratch[zvec.shape[0] :, :] = jnp.zeros((ROWS, vec.shape[1]), jnp.float32)
+    post(message, scratch)
+    sent = start_all((message,), (message_far,), done, len(copies))
+    copies[-1].wait()
+    relaxed(dblock, resid, state)
+    wait_all(sent)
 
 
 def diag_kernel(vec, dblock, *refs):
@@ -203,35 +211,36 @@
     wait_all(copies)
 
 
-def diag_from_far_kernel(vec, dblock_far, out, dblock, done):
-    wait_all(start_all((dblock_far,), (dblock,), done))
-    block_product(dblock, vec[...], out)
-
-
-def apply_kernel(diag_near, vec, others, cols, here, there, fblock_far, out, fblock, arrived, done):
-    copies = start_all((there, fblock_far), (arrived, fblock), done)
-    dblock, lblocks = (here, arrived) if diag_near else (arrived, here)
+def diag_copy_kernel(vec, dblock, *refs):
+    count = (len(refs) - 3) // 2
+    copies = start_all(refs[:count], refs[count + 2 : -1], refs[-1])
+    out, copied = refs[count : count + 2]
+    whole = vec[...]
+
+    def body(start):
+        rows = pl.ds(start, ROWS)
+        out[rows, :] = rows_times(dblock, whole, start)
+        copied[rows] = dblock[rows]
+
+    by_rows(out.shape[0], body)
+    wait_all(copies)
+
+
+def apply_kernel(vec, others, cols, lblocks, dblock_far, fblock_far, out, fblock, dblock, done):
+    copies = start_all((dblock_far, fblock_far), (dblock, fblock), done)
     chosen = [picked(vec, others, cols, part) for part in range(lblocks.shape[0])]
     whole = vec[...]
 
+    def off(start):
+        out[pl.ds(start, ROWS), :] = off_rows(lblocks, chosen, start)
+
     def own(start):
-        return rows_times(dblock, whole, start)
-
-    def off(start):
-        return off_rows(lblocks, chosen, start)
-
-    first, second = (own, off) if diag_near else (off, own)
-
-    def begin(start):
-        out[pl.ds(start, ROWS), :] = first(start)
-
-    def finish(start):
         rows = pl.ds(start, ROWS)
-        out[rows, :] = out[rows, :] + second(start)
-
-    by_rows(out.shape[0], begin)
+        out[rows, :] = out[rows, :] + rows_times(dblock, whole, start)
+
+    by_rows(out.shape[0], off)
     copies[0].wait()
-    by_rows(out.shape[0], finish)
+    by_rows(out.shape[0], own)
     copies[1].wait()
 
 
@@ -246,42 +255,71 @@
     relaxed(dblock, rest, out, state)
 
 
-def direction_kernel(count, state, arrived, zvec, inverse, out):
+def direction_kernel(count, state, arrived, zvec, inverse, out, *parts):
     rows = restriction_rows(arrived, zvec.shape[0], count)
-    out[...] = combined(weights_here(inverse, rows), zvec, state[...])
-
-
-def near_lanes(parts, inner):
-    group = lax.broadcasted_iota(jnp.int32, parts[0].shape, 1) // inner
-    value = parts[0][...]
-    for at in range(1, len(parts)):
-        value = jnp.where(group == at, parts[at][...], value)
-    return value
+    value = combined(weights_here(inverse, rows), zvec, state[...])
+    out[...] = value
+    pack_lanes(value, parts)
+
+
+def pack_lanes(vec, parts):
+    deep, lanes = vec.shape
+    rows = parts[0].shape[0]
+    groups = deep // rows
+    inner = lanes // groups
+    group = lax.broadcasted_iota(jnp.int32, (rows, lanes), 1) // inner
+    for q, part in enumerate(parts):
+        value = jnp.zeros((rows, lanes), jnp.float32)
+        for g in range(groups):
+            value = jnp.where(group == g, turned(vec[g * rows : (g + 1) * rows, :], (g - q) * inner), value)
+        part[...] = value
+
+
+def turned(value, lanes):
+    lanes %= value.shape[1]
+    return pltpu.roll(value, lanes, 1) if lanes else value
+
+
+def near_lanes(parts, deep):
+    rows, lanes = parts[0].shape
+    groups = deep // rows
+    inner = lanes // groups
+    group = lax.broadcasted_iota(jnp.int32, (rows, lanes), 1) // inner
+    pieces = []
+    for g in range(groups):
+        value = jnp.zeros((rows, lanes), jnp.float32)
+        for q, part in enumerate(parts):
+            value = jnp.where(group == q, turned(part[...], (q - g) * inner), value)
+        pieces.append(value)
+    return jnp.concatenate(pieces, axis=0)
 
 
 def image_kernel(known, near0, near1, near2, fblock, resid, zvec, dblock, image, state, message_far, scratch, message, done):
-    with_interface(known, near_lanes((near0, near1, near2), fblock.shape[2] // BITS), fblock, image)
+    with_interface(known, near_lanes((near0, near1, near2), known.shape[0]), fblock, image)
     value = image[...]
-    sums = restricted(zvec, value, scratch)
-    post(message, zvec.shape[0], sums, total(resid[...] * value), total(value * value))
+    block_product(zvec, value, scratch)
+    inner_products(scratch, resid[...], value)
+    post(message, scratch)
     copies = start_all((message,), (message_far,), done)
     relaxed(dblock, image, state)
     wait_all(copies)
 
 
-def next_direction_kernel(count, state, arrived, zvec, inverse, first, resid, image, out, rest, alpha):
+def next_direction_kernel(count, state, arrived, zvec, inverse, first, resid, image, out, rest, alpha, *parts):
     size = step_size(arrived, zvec.shape[0], count)
     rows = restriction_rows(arrived, zvec.shape[0], count)
-    out[...] = first[...] - size * combined(weights_here(inverse, rows), zvec, state[...])
+    value = first[...] - size * combined(weights_here(inverse, rows), zvec, state[...])
+    out[...] = value
+    pack_lanes(value, parts)
     rest[...] = resid[...] - size * image[...]
     alpha[...] = jnp.broadcast_to(size, alpha.shape)
 
 
-def last_image_kernel(nvec, known, near0, near1, near2, fblock, resid, image, message):
-    with_interface(known, near_lanes((near0, near1, near2), fblock.shape[2] // BITS), fblock, image)
-    value = image[...]
-    zero = jnp.zeros((1, message.shape[-1]), jnp.float32)
-    post(message, nvec, zero, total(resid[...] * value), total(value * value))
+def last_image_kernel(known, near0, near1, near2, fblock, resid, image, message, scratch):
+    with_interface(known, near_lanes((near0, near1, near2), known.shape[0]), fblock, image)
+    scratch[...] = jnp.zeros(scratch.shape, jnp.float32)
+    inner_products(scratch, resid[...], image[...])
+    post(message, scratch)
 
 
 def final_kernel(nvec, count, arrived, alpha, first, second, resid, image, field, rest):
@@ -305,7 +343,7 @@
     cfar, zfar = block_cols[0], basis[0]
     shape = right_side.shape[1:]
     nvec, lanes = zfar.shape[0], shape[1]
-    flat, small, parcel = vmem(shape), vmem((nvec, lanes)), vmem((subs * count, lanes))
+    flat, small, parcel = vmem(shape), vmem((nvec + ROWS, lanes)), vmem((subs * count, lanes))
     wide = vmem((subs * count, WIDE, lanes))
 
     def sems(number):
@@ -324,66 +362,61 @@
     def diag(vec, dblock, *far):
         return kernel(diag_kernel, [flat, *map(like, far)], [vec, dblock], far, [sems(max(len(far), 1))])
 
-    def middle(state, resid, dblock, lblocks, cols):
-        for _ in range(SWEEPS - 3):
+    def smooth(state, resid, dblock, lblocks, cols, *far):
+        others = gathered(state, count)
+        own, dblock, *more = kernel(
+            diag_copy_kernel,
+            [flat, like(dblock), *map(like, far)],
+            [state, dblock],
+            far,
+            [sems(max(len(far), 1))],
+        )
+        lblocks, cols = more or (lblocks, cols)
+        state = sweep(state, others, own, resid, dblock, lblocks, cols)
+        for at in range(SWEEPS - 2):
             others = gathered(state, count)
-            (own,) = diag(state, dblock)
+            own, *held = diag(state, dblock, *((zfar, coarse_inverse) if at == SWEEPS - 3 else ()))
             state = sweep(state, others, own, resid, dblock, lblocks, cols)
-        return state
-
-    def last_sweep(state, resid, dblock, lblocks, cols):
-        others = gathered(state, count)
-        own, *held = diag(state, dblock, zfar, coarse_inverse)
-        return sweep(state, others, own, resid, dblock, lblocks, cols), held
-
-    def apply(vec, cols, here, there, last=False):
+        return state, held, lblocks, cols
+
+    def apply(vec, parts, lblocks, cols, last=False):
         others = gathered(vec, count)
-        near = [lax.ppermute(vec, "sub", swap(subs, 1 << bit)) for bit in range(BITS)]
-        outs, scratch = [flat, like(ffar)], [like(there)]
+        near = [lax.ppermute(part, "sub", swap(subs, 1 << bit)) for bit, part in enumerate(parts)]
+        outs, scratch = [flat, like(ffar)], [like(dfar)]
         if not last:
             outs, scratch = outs + scratch, []
         known, fblock, *brought = kernel(
-            functools.partial(apply_kernel, len(here.shape) < len(there.shape)),
-            outs,
-            [vec, others, cols, here],
-            [there, ffar],
-            [*scratch, sems(2)],
+            apply_kernel, outs, [vec, others, cols, lblocks], [dfar, ffar], [*scratch, sems(2)]
         )
         return [known, *near, fblock], brought
 
     wide_far = pltpu.HBM(wide.shape, jnp.float32)
-    resid, dblock, message = kernel(
+    resid, dblock, state, message = kernel(
         first_kernel,
-        [flat, like(dfar), wide_far],
+        [flat, like(dfar), flat, wide_far],
         [],
         [right_side[0], zfar, dfar],
-        [like(zfar), small, wide, sems(4)],
+        [like(zfar), small, wide, sems(3 + nvec // ROWS)],
     )
     arrived = everywhere(message)[:, 0, :]
-    (state,) = kernel(relax_kernel, [flat], [resid, dblock])
-    others = gathered(state, count)
-    own, lblocks, cols = diag(state, dblock, lfar, cfar)
-    state = sweep(state, others, own, resid, dblock, lblocks, cols)
-    state = middle(state, resid, dblock, lblocks, cols)
-    state, held = last_sweep(state, resid, dblock, lblocks, cols)
-    (first,) = kernel(functools.partial(direction_kernel, count), [flat], [state, arrived, *held])
-    terms, (lblocks,) = apply(first, cols, dblock, lfar)
+    state, held, lblocks, cols = smooth(state, resid, dblock, lfar, cfar)
+    packed = [vmem((shape[0] * ffar.shape[2] // (BITS * lanes), lanes))] * BITS
+    first, *parts = kernel(
+        functools.partial(direction_kernel, count), [flat, *packed], [state, arrived, *held]
+    )
+    terms, (dblock,) = apply(first, parts, lblocks, cols)
     first_image, state, message = kernel(
         image_kernel, [flat, flat, wide_far], [*terms, resid, held[0], dblock], [], [small, wide, sems(1)]
     )
     arrived = everywhere(message)[:, 0, :]
-    others = gathered(state, count)
-    own, dblock = kernel(diag_from_far_kernel, [flat, like(dfar)], [state], [dfar], [sems(1)])
-    state = sweep(state, others, own, first_image, dblock, lblocks, cols)
-    state = middle(state, first_image, dblock, lblocks, cols)
-    state, held = last_sweep(state, first_image, dblock, lblocks, cols)
-    second, rest, alpha = kernel(
+    state, held, _, _ = smooth(state, first_image, dblock, lblocks, cols)
+    second, rest, alpha, *parts = kernel(
         functools.partial(next_direction_kernel, count),
-        [flat, flat, vmem((ROWS, lanes))],
+        [flat, flat, vmem((ROWS, lanes)), *packed],
         [state, arrived, *held, first, resid, first_image],
     )
-    terms, _ = apply(second, cols, lblocks, dfar, True)
-    image, message = kernel(functools.partial(last_image_kernel, nvec), [flat, parcel], [*terms, rest])
+    terms, _ = apply(second, parts, lblocks, cols, True)
+    image, message = kernel(last_image_kernel, [flat, parcel], [*terms, rest], [], [small])
     arrived = everywhere(message)
     return pl.pallas_call(
         functools.partial(final_kernel, nvec, count),

time: 53.8 us -> 51.4 us (0.955)
  waiting for transfers between devices: 4.77 us -> 9.84 us
  Pallas kernels: 18.6 us -> 14.7 us
  starting transfers between devices: 18.5 us -> 15.8 us
  blocking collectives: 10.7 us -> 9.9 us
    pallas_call x16 -> x15, Pallas kernels: 17.8 us -> 13.9 us  [kernel(): pl.pallas_call(body, out_shape=outs, in_specs=[here] * len(near) + [there...]
    all_to_all x2, waiting for transfers between devices: 3.71 us -> 5.86 us  [everywhere(): lax.all_to_all(message, ('sub', 'coarse'), 0, 0, tiled=len(message.shape)...]
    ppermute x6, starting transfers between devices: 5.81 us -> 3.89 us  [apply(): lax.ppermute(part, 'sub', swap(subs, 1 << bit))]
    ppermute x6, waiting for transfers between devices: 1.05 us -> 2.68 us  [apply(): lax.ppermute(part, 'sub', swap(subs, 1 << bit))]
    ppermute x6, waiting for transfers between devices: 0.02 us -> 1.3 us  [gathered(): return lax.ppermute(array, 'coarse', swap(2, 1))[None]]
    all_to_all x2, starting transfers between devices: 11 us -> 10.3 us  [everywhere(): lax.all_to_all(message, ('sub', 'coarse'), 0, 0, tiled=len(message.shape)...]
    all_to_all x1, blocking collectives: 10.7 us -> 9.9 us  [everywhere(): lax.all_to_all(message, ('sub', 'coarse'), 0, 0, tiled=len(message.shape)...]
  transfers between devices with their start and end apart: 14 -> 14, of which waited for: 5 -> 10; matrix products, arithmetic and copies ran while one was open for 0% -> 0% of each run, Pallas kernels for 25% -> 19%
where the time goes in v1:
time: 51.4 us; the launch traced here: 51 us
  starting transfers between devices  15.8 us (31%)
  Pallas kernels  14.7 us (29%)
  blocking collectives  9.9 us (19%)
  waiting for transfers between devices  9.84 us (19%)
  between operations  0.8 us (2%)
    pallas_call x15, Pallas kernels, kernel(): pl.pallas_call(body, out_shape=outs, in_specs=[here] * len(near) + [there...  13.9 us
    all_to_all x2, starting transfers between devices, everywhere(): lax.all_to_all(message, ('sub', 'coarse'), 0, 0, tiled=len(message.shape)...  10.3 us
    all_to_all x1, blocking collectives, everywhere(): lax.all_to_all(message, ('sub', 'coarse'), 0, 0, tiled=len(message.shape)...  9.9 us
    all_to_all x2, waiting for transfers between devices, everywhere(): lax.all_to_all(message, ('sub', 'coarse'), 0, 0, tiled=len(message.shape)...  5.86 us
    ppermute x6, starting transfers between devices, apply(): lax.ppermute(part, 'sub', swap(subs, 1 << bit))  3.89 us
    ppermute x6, waiting for transfers between devices, apply(): lax.ppermute(part, 'sub', swap(subs, 1 << bit))  2.68 us
    ppermute x6, starting transfers between devices, gathered(): return lax.ppermute(array, 'coarse', swap(2, 1))[None]  1.62 us
    ppermute x6, waiting for transfers between devices, gathered(): return lax.ppermute(array, 'coarse', swap(2, 1))[None]  1.3 us
  transfers between devices with their start and end apart: 14, of which 10 were waited for; matrix products, arithmetic and copies ran while one was open for 0% of the time, Pallas kernels for 19%

profile of v1, /device:TPU:0, one launch (start us, length us, event | category | flops | bytes accessed | tf_op | source)
XLA Modules:
  0.0 51.0 jit_solution(3715681708111115726)
XLA Ops:
  0.6 0.0 copy-start.3
  0.6 0.0 copy-start
  0.6 2.1 %shard_map.86 = (f32[64,128]{1,0:T(8,128)S(1)}, bf16[64,64,128]{2,1,0:T(8,128)(2,1)S(1)}, f32[64,128]{1,0:T(8,128)S(1)}, f32[32,3,128]{2,1,0:T(4,128)}) custom-call(f32[64,128]{1,0:T(8,128)} %bitcast.52, bf16[32,64,128]{2,1,0:T(8,128)(2,1)} %bitcast.47, bf16[64,64,128]{2,1,0:T(8,128)(2,1)} %bitcast.44), custom_call_target="tpu_custom_call" | custom-call | tf_op jit(solution)/shard_map/pallas_call | solution.py:23
  2.7 7.3 %all-to-all-start = ((f32[32,3,128]{2,1,0:T(4,128)}), f32[32,3,128]{2,1,0:T(4,128)S(1)}, u32[]{:S(2)}, u32[]{:S(2)}) async-start(f32[32,3,128]{2,1,0:T(4,128)} %get-tuple-element.42), calls=%async_computation | async-start | bytes 131072 | tf_op jit(solution)/shard_map/all_to_all | solution.py:356
  10.0 0.3 collective-permute-start
  10.3 0.3 shard_map.87
  10.7 0.6 %collective-permute-done = f32[64,128]{1,0:T(8,128)S(1)} collective-permute-done((f32[64,128]{1,0:T(8,128)S(1)}, f32[64,128]{1,0:T(8,128)S(1)}, u32[]{:S(2)}, u32[]{:S(2)}) %collective-permute-start) | collective-permute-done | bytes 32800 | tf_op jit(solution)/shard_map/ppermute | solution.py:337
  11.3 0.0 copy-done.3
  11.3 0.9 %shard_map.88.vec.state = f32[64,128]{1,0:T(8,128)S(1)} custom-call(f32[64,128]{1,0:T(8,128)S(1)} %get-tuple-element.36.vec.state, f32[1,64,128]{2,1,0:T(8,128)S(1)} %bitcast.39, f32[64,128]{1,0:T(8,128)S(1)} %get-tuple-element.38.own, f32[64,128]{1,0:T(8,128)S(1)} %get-tuple-element.39.resid, bf16[64,64,128]{2,1,0:T(8,128)(2,1)S(1)} %get-tuple-element.40.dblock, ...), custom_call_target="tpu_custom_call" | custom-call | tf_op jit(solution)/shard_map/pallas_call | solution.py:23
  12.2 0.3 collective-permute-start.1
  12.5 1.1 %shard_map.89 = (f32[64,128]{1,0:T(8,128)S(1)}, bf16[32,64,128]{2,1,0:T(8,128)(2,1)S(1)}, f32[32,512]{1,0:T(8,128)S(1)}) custom-call(f32[64,128]{1,0:T(8,128)S(1)} %shard_map.88.vec.state, bf16[64,64,128]{2,1,0:T(8,128)(2,1)S(1)} %get-tuple-element.40.dblock, bf16[32,64,128]{2,1,0:T(8,128)(2,1)} %bitcast.48, f32[32,512]{1,0:T(8,128)} %refs_1_.3), custom_call_target="tpu_custom_call" | custom-call | tf_op jit(solution)/shard_map/pallas_call | solution.py:23
  13.6 0.0 collective-permute-done.1
  13.6 0.9 %shard_map.90.state = f32[64,128]{1,0:T(8,128)S(1)} custom-call(f32[64,128]{1,0:T(8,128)S(1)} %shard_map.88.vec.state, f32[1,64,128]{2,1,0:T(8,128)S(1)} %bitcast.41, f32[64,128]{1,0:T(8,128)S(1)} %get-tuple-element.41.own, f32[64,128]{1,0:T(8,128)S(1)} %get-tuple-element.39.resid, bf16[64,64,128]{2,1,0:T(8,128)(2,1)S(1)} %get-tuple-element.40.dblock, ...), custom_call_target="tpu_custom_call" | custom-call | tf_op jit(solution)/shard_map/pallas_call | solution.py:23
  14.5 2.9 %all-to-all-done = f32[32,3,128]{2,1,0:T(4,128)S(1)} async-done(((f32[32,3,128]{2,1,0:T(4,128)}), f32[32,3,128]{2,1,0:T(4,128)S(1)}, u32[]{:S(2)}, u32[]{:S(2)}) %all-to-all-start) | async-done | bytes 49184 | tf_op jit(solution)/shard_map/all_to_all | solution.py:356
  17.5 0.3 shard_map.91
  17.7 0.2 collective-permute-start.2
  17.9 0.5 collective-permute-start.3
  18.4 0.8 %collective-permute-start.4 = (f32[16,128]{1,0:T(8,128)S(1)}, f32[16,128]{1,0:T(8,128)S(1)}, u32[]{:S(2)}, u32[]{:S(2)}) collective-permute-start(f32[16,128]{1,0:T(8,128)S(1)} %get-tuple-element.48), channel_id=1, source_target_pairs={{0,4},{2,6},{4,0},{6,2},{8,12},{10,14},{12,8},{14,10},{16,20},{18,... | collective-permute-start | bytes 24584 | tf_op jit(solution)/shard_map/ppermute | solution.py:384
  19.2 0.7 %collective-permute-start.5 = (f32[16,128]{1,0:T(8,128)S(1)}, f32[16,128]{1,0:T(8,128)S(1)}, u32[]{:S(2)}, u32[]{:S(2)}) collective-permute-start(f32[16,128]{1,0:T(8,128)S(1)} %get-tuple-element.49), channel_id=1, source_target_pairs={{0,8},{2,10},{4,12},{6,14},{8,0},{10,2},{12,4},{14,6},{16,24},{18,... | collective-permute-start | bytes 24584 | tf_op jit(solution)/shard_map/ppermute | solution.py:384
  19.9 0.0 collective-permute-done.2
  19.9 1.6 %shard_map.92 = (f32[64,128]{1,0:T(8,128)S(1)}, bf16[64,64,96]{2,1,0:T(8,128)(2,1)S(1)}, bf16[64,64,128]{2,1,0:T(8,128)(2,1)S(1)}) custom-call(f32[64,128]{1,0:T(8,128)S(1)} %get-tuple-element.45.vec.first, f32[1,64,128]{2,1,0:T(8,128)S(1)} %bitcast.37, s32[2,128]{1,0:T(2,128)S(1)} %bitcast.33, bf16[2,64,64,128]{3,2,1,0:T(8,128)(2,1)S(1)} %bitcast.24, ...), custom_call_target="tpu_custom_call" | custom-call | tf_op jit(solution)/shard_map/pallas_call | solution.py:23
  21.5 0.1 collective-permute-done.3.near0
  21.6 0.4 collective-permute-done.4.near1
  22.0 0.8 %collective-permute-done.5.near2 = f32[16,128]{1,0:T(8,128)S(1)} collective-permute-done((f32[16,128]{1,0:T(8,128)S(1)}, f32[16,128]{1,0:T(8,128)S(1)}, u32[]{:S(2)}, u32[]{:S(2)}) %collective-permute-start.5) | collective-permute-done | bytes 8224 | tf_op jit(solution)/shard_map/ppermute | solution.py:384
  22.8 1.3 %shard_map.93 = (f32[64,128]{1,0:T(8,128)S(1)}, f32[64,128]{1,0:T(8,128)S(1)}, f32[32,3,128]{2,1,0:T(4,128)}) custom-call(f32[64,128]{1,0:T(8,128)S(1)} %get-tuple-element.46.known, f32[16,128]{1,0:T(8,128)S(1)} %collective-permute-done.3.near0, f32[16,128]{1,0:T(8,128)S(1)} %collective-permute-done.4.near1, f32[16,128]{1,0:T(8,128)S(1)} %collective-permute-done.5.near2, ...), custom_call_target="tpu_custom_call" | custom-call | tf_op jit(solution)/shard_map/pallas_call | solution.py:23
  24.1 2.9 %all-to-all-start.1 = ((f32[32,3,128]{2,1,0:T(4,128)}), f32[32,3,128]{2,1,0:T(4,128)S(1)}, u32[]{:S(2)}, u32[]{:S(2)}) async-start(f32[32,3,128]{2,1,0:T(4,128)} %get-tuple-element.57), calls=%async_computation.1 | async-start | bytes 131072 | tf_op jit(solution)/shard_map/all_to_all | solution.py:356
  27.1 0.3 collective-permute-start.6
  27.4 0.3 shard_map.94
  27.7 0.6 %collective-permute-done.6 = f32[64,128]{1,0:T(8,128)S(1)} collective-permute-done((f32[64,128]{1,0:T(8,128)S(1)}, f32[64,128]{1,0:T(8,128)S(1)}, u32[]{:S(2)}, u32[]{:S(2)}) %collective-permute-start.6) | collective-permute-done | bytes 32800 | tf_op jit(solution)/shard_map/ppermute | solution.py:337
  28.3 0.9 %shard_map.95.vec.state = f32[64,128]{1,0:T(8,128)S(1)} custom-call(f32[64,128]{1,0:T(8,128)S(1)} %get-tuple-element.52.vec.state, f32[1,64,128]{2,1,0:T(8,128)S(1)} %bitcast.40, f32[64,128]{1,0:T(8,128)S(1)} %get-tuple-element.53.own, f32[64,128]{1,0:T(8,128)S(1)} %get-tuple-element.54.resid.image, bf16[64,64,128]{2,1,0:T(8,128)(2,1)S(1)} %get-tuple-element.55.dblock, ...), custom_call_target="tpu_custom_call" | custom-call | tf_op jit(solution)/shard_map/pallas_call | solution.py:23
  29.2 0.3 collective-permute-start.7
  29.6 1.1 %shard_map.96 = (f32[64,128]{1,0:T(8,128)S(1)}, bf16[32,64,128]{2,1,0:T(8,128)(2,1)S(1)}, f32[32,512]{1,0:T(8,128)S(1)}) custom-call(f32[64,128]{1,0:T(8,128)S(1)} %shard_map.95.vec.state, bf16[64,64,128]{2,1,0:T(8,128)(2,1)S(1)} %get-tuple-element.55.dblock, bf16[32,64,128]{2,1,0:T(8,128)(2,1)} %bitcast.49, f32[32,512]{1,0:T(8,128)} %refs_1_.3), custom_call_target="tpu_custom_call" | custom-call | tf_op jit(solution)/shard_map/pallas_call | solution.py:23
  30.6 0.0 collective-permute-done.7
  30.6 0.9 %shard_map.97.state = f32[64,128]{1,0:T(8,128)S(1)} custom-call(f32[64,128]{1,0:T(8,128)S(1)} %shard_map.95.vec.state, f32[1,64,128]{2,1,0:T(8,128)S(1)} %bitcast.42, f32[64,128]{1,0:T(8,128)S(1)} %get-tuple-element.56.own, f32[64,128]{1,0:T(8,128)S(1)} %get-tuple-element.54.resid.image, bf16[64,64,128]{2,1,0:T(8,128)(2,1)S(1)} %get-tuple-element.55.dblock, ...), custom_call_target="tpu_custom_call" | custom-call | tf_op jit(solution)/shard_map/pallas_call | solution.py:23
  31.5 2.9 %all-to-all-done.1 = f32[32,3,128]{2,1,0:T(4,128)S(1)} async-done(((f32[32,3,128]{2,1,0:T(4,128)}), f32[32,3,128]{2,1,0:T(4,128)S(1)}, u32[]{:S(2)}, u32[]{:S(2)}) %all-to-all-start.1) | async-done | bytes 49184 | tf_op jit(solution)/shard_map/all_to_all | solution.py:356
  34.5 0.3 shard_map.98
  34.8 0.2 collective-permute-start.8
  35.0 0.5 collective-permute-start.9
  35.4 0.8 %collective-permute-start.10 = (f32[16,128]{1,0:T(8,128)S(1)}, f32[16,128]{1,0:T(8,128)S(1)}, u32[]{:S(2)}, u32[]{:S(2)}) collective-permute-start(f32[16,128]{1,0:T(8,128)S(1)} %get-tuple-element.63), channel_id=1, source_target_pairs={{0,4},{2,6},{4,0},{6,2},{8,12},{10,14},{12,8},{14,10},{16,20},{18,... | collective-permute-start | bytes 24584 | tf_op jit(solution)/shard_map/ppermute | solution.py:384
  36.2 0.7 %collective-permute-start.11 = (f32[16,128]{1,0:T(8,128)S(1)}, f32[16,128]{1,0:T(8,128)S(1)}, u32[]{:S(2)}, u32[]{:S(2)}) collective-permute-start(f32[16,128]{1,0:T(8,128)S(1)} %get-tuple-element.64), channel_id=1, source_target_pairs={{0,8},{2,10},{4,12},{6,14},{8,0},{10,2},{12,4},{14,6},{16,24},{18,... | collective-permute-start | bytes 24584 | tf_op jit(solution)/shard_map/ppermute | solution.py:384
  36.9 0.0 collective-permute-done.8
  36.9 1.6 %shard_map.99 = (f32[64,128]{1,0:T(8,128)S(1)}, bf16[64,64,96]{2,1,0:T(8,128)(2,1)S(1)}) custom-call(f32[64,128]{1,0:T(8,128)S(1)} %get-tuple-element.60.vec.second, f32[1,64,128]{2,1,0:T(8,128)S(1)} %bitcast.38, s32[2,128]{1,0:T(2,128)S(1)} %bitcast.36, bf16[2,64,64,128]{3,2,1,0:T(8,128)(2,1)S(1)} %bitcast.27, bf16[64,64,128]{2,1,0:T(8,128)(2,1)} %bitcast.46, ...), custom_call_target="tpu_custom_call" | custom-call | tf_op jit(solution)/shard_map/pallas_call | solution.py:23
  38.5 0.2 collective-permute-done.9.near0
  38.6 0.4 collective-permute-done.10.near1
  39.1 0.8 %collective-permute-done.11.near2 = f32[16,128]{1,0:T(8,128)S(1)} collective-permute-done((f32[16,128]{1,0:T(8,128)S(1)}, f32[16,128]{1,0:T(8,128)S(1)}, u32[]{:S(2)}, u32[]{:S(2)}) %collective-permute-start.11) | collective-permute-done | bytes 8224 | tf_op jit(solution)/shard_map/ppermute | solution.py:384
  39.9 0.5 %shard_map.100 = (f32[64,128]{1,0:T(8,128)S(1)}, f32[32,128]{1,0:T(8,128)S(1)}) custom-call(f32[64,128]{1,0:T(8,128)S(1)} %get-tuple-element.61.known, f32[16,128]{1,0:T(8,128)S(1)} %collective-permute-done.9.near0, f32[16,128]{1,0:T(8,128)S(1)} %collective-permute-done.10.near1, f32[16,128]{1,0:T(8,128)S(1)} %collective-permute-done.11.near2, ...), custom_call_target="tpu_custom_call" | custom-call | tf_op jit(solution)/shard_map/pallas_call | solution.py:23
  40.4 9.9 %all_to_all.21 = f32[32,1,128]{2,1,0:T(1,128)S(1)} all-to-all(f32[32,1,128]{2,1,0:T(1,128)S(1)} %bitcast.43), channel_id=1, replica_groups=mesh['sub'=16,'coarse'=2] {'sub','coarse'}, dimensions={0} | all-to-all | bytes 32768 | tf_op jit(solution)/shard_map/all_to_all | solution.py:356
  50.3 0.8 %shard_map.101 = (f32[1,64,128]{2,1,0:T(8,128)}, f32[1,64,128]{2,1,0:T(8,128)}) custom-call(f32[32,128]{1,0:T(8,128)S(1)} %bitcast.29, f32[8,128]{1,0:T(8,128)S(1)} %get-tuple-element.68.alpha, f32[64,128]{1,0:T(8,128)S(1)} %get-tuple-element.45.vec.first, f32[64,128]{1,0:T(8,128)S(1)} %get-tuple-element.60.vec.second, ...), custom_call_target="tpu_custom_call" | custom-call | tf_op jit(solution)/shard_map/pallas_call | solution.py:421
  (7 shorter events, 0.0 us)
Async XLA Ops:
  0.6 10.7 %copy-start.3 = (s32[1,2,128]{2,1,0:T(2,128)S(1)}, s32[1,2,128]{2,1,0:T(2,128)}, u32[]{:S(2)}) copy-start(s32[1,2,128]{2,1,0:T(2,128)} %param.11) | copy-start | bytes 3076
  0.6 10.7 %copy-start = (bf16[1,2,64,64,128]{4,3,2,1,0:T(8,128)(2,1)S(1)}, bf16[1,2,64,64,128]{4,3,2,1,0:T(8,128)(2,1)}, u32[]{:S(2)}) copy-start(bf16[1,2,64,64,128]{4,3,2,1,0:T(8,128)(2,1)} %param.8) | copy-start | bytes 6291460
  2.7 14.7 %all-to-all-start = ((f32[32,3,128]{2,1,0:T(4,128)}), f32[32,3,128]{2,1,0:T(4,128)S(1)}, u32[]{:S(2)}, u32[]{:S(2)}) async-start(f32[32,3,128]{2,1,0:T(4,128)} %get-tuple-element.42), calls=%async_computation | async-start | bytes 131072 | tf_op jit(solution)/shard_map/all_to_all | solution.py:356
  10.0 1.3 %collective-permute-start = (f32[64,128]{1,0:T(8,128)S(1)}, f32[64,128]{1,0:T(8,128)S(1)}, u32[]{:S(2)}, u32[]{:S(2)}) collective-permute-start(f32[64,128]{1,0:T(8,128)S(1)} %get-tuple-element.36.vec.state), channel_id=1, source_target_pairs={{0,1},{1,0},{2,3},{3,2},{4,5},{5,4},{6,7},{7,6},{8,9},{9,8},{10,11... | collective-permute-start | bytes 98312 | tf_op jit(solution)/shard_map/ppermute | solution.py:337
  12.2 1.4 %collective-permute-start.1 = (f32[64,128]{1,0:T(8,128)S(1)}, f32[64,128]{1,0:T(8,128)S(1)}, u32[]{:S(2)}, u32[]{:S(2)}) collective-permute-start(f32[64,128]{1,0:T(8,128)S(1)} %shard_map.88.vec.state), channel_id=1, source_target_pairs={{0,1},{1,0},{2,3},{3,2},{4,5},{5,4},{6,7},{7,6},{8,9},{9,8},{10,11... | collective-permute-start | bytes 98312 | tf_op jit(solution)/shard_map/ppermute | solution.py:337
  13.6 6.3 %copy-start.1 = (bf16[32,64,128]{2,1,0:T(8,128)(2,1)}, bf16[32,64,128]{2,1,0:T(8,128)(2,1)S(1)}, u32[]{:S(2)}) copy-start(bf16[32,64,128]{2,1,0:T(8,128)(2,1)S(1)} %get-tuple-element.43.zvec) | copy-start | bytes 1572868
  17.7 2.1 %collective-permute-start.2 = (f32[64,128]{1,0:T(8,128)S(1)}, f32[64,128]{1,0:T(8,128)S(1)}, u32[]{:S(2)}, u32[]{:S(2)}) collective-permute-start(f32[64,128]{1,0:T(8,128)S(1)} %get-tuple-element.45.vec.first), channel_id=1, source_target_pairs={{0,1},{1,0},{2,3},{3,2},{4,5},{5,4},{6,7},{7,6},{8,9},{9,8},{10,11... | collective-permute-start | bytes 98312 | tf_op jit(solution)/shard_map/ppermute | solution.py:337
  17.9 3.7 %collective-permute-start.3 = (f32[16,128]{1,0:T(8,128)S(1)}, f32[16,128]{1,0:T(8,128)S(1)}, u32[]{:S(2)}, u32[]{:S(2)}) collective-permute-start(f32[16,128]{1,0:T(8,128)S(1)} %get-tuple-element.47), channel_id=1, source_target_pairs={{0,2},{2,0},{4,6},{6,4},{8,10},{10,8},{12,14},{14,12},{16,18},{18,... | collective-permute-start | bytes 24584 | tf_op jit(solution)/shard_map/ppermute | solution.py:384
  18.4 3.7 %collective-permute-start.4 = (f32[16,128]{1,0:T(8,128)S(1)}, f32[16,128]{1,0:T(8,128)S(1)}, u32[]{:S(2)}, u32[]{:S(2)}) collective-permute-start(f32[16,128]{1,0:T(8,128)S(1)} %get-tuple-element.48), channel_id=1, source_target_pairs={{0,4},{2,6},{4,0},{6,2},{8,12},{10,14},{12,8},{14,10},{16,20},{18,... | collective-permute-start | bytes 24584 | tf_op jit(solution)/shard_map/ppermute | solution.py:384
  19.2 3.7 %collective-permute-start.5 = (f32[16,128]{1,0:T(8,128)S(1)}, f32[16,128]{1,0:T(8,128)S(1)}, u32[]{:S(2)}, u32[]{:S(2)}) collective-permute-start(f32[16,128]{1,0:T(8,128)S(1)} %get-tuple-element.49), channel_id=1, source_target_pairs={{0,8},{2,10},{4,12},{6,14},{8,0},{10,2},{12,4},{14,6},{16,24},{18,... | collective-permute-start | bytes 24584 | tf_op jit(solution)/shard_map/ppermute | solution.py:384
  19.9 2.9 %copy-start.2 = (bf16[32,64,128]{2,1,0:T(8,128)(2,1)S(1)}, bf16[32,64,128]{2,1,0:T(8,128)(2,1)}, u32[]{:S(2)}) copy-start(bf16[32,64,128]{2,1,0:T(8,128)(2,1)} %copy-done.1) | copy-start | bytes 1572868
  24.1 10.4 %all-to-all-start.1 = ((f32[32,3,128]{2,1,0:T(4,128)}), f32[32,3,128]{2,1,0:T(4,128)S(1)}, u32[]{:S(2)}, u32[]{:S(2)}) async-start(f32[32,3,128]{2,1,0:T(4,128)} %get-tuple-element.57), calls=%async_computation.1 | async-start | bytes 131072 | tf_op jit(solution)/shard_map/all_to_all | solution.py:356
  27.1 1.3 %collective-permute-start.6 = (f32[64,128]{1,0:T(8,128)S(1)}, f32[64,128]{1,0:T(8,128)S(1)}, u32[]{:S(2)}, u32[]{:S(2)}) collective-permute-start(f32[64,128]{1,0:T(8,128)S(1)} %get-tuple-element.52.vec.state), channel_id=1, source_target_pairs={{0,1},{1,0},{2,3},{3,2},{4,5},{5,4},{6,7},{7,6},{8,9},{9,8},{10,11... | collective-permute-start | bytes 98312 | tf_op jit(solution)/shard_map/ppermute | solution.py:337
  29.2 1.4 %collective-permute-start.7 = (f32[64,128]{1,0:T(8,128)S(1)}, f32[64,128]{1,0:T(8,128)S(1)}, u32[]{:S(2)}, u32[]{:S(2)}) collective-permute-start(f32[64,128]{1,0:T(8,128)S(1)} %shard_map.95.vec.state), channel_id=1, source_target_pairs={{0,1},{1,0},{2,3},{3,2},{4,5},{5,4},{6,7},{7,6},{8,9},{9,8},{10,11... | collective-permute-start | bytes 98312 | tf_op jit(solution)/shard_map/ppermute | solution.py:337
  34.8 2.1 %collective-permute-start.8 = (f32[64,128]{1,0:T(8,128)S(1)}, f32[64,128]{1,0:T(8,128)S(1)}, u32[]{:S(2)}, u32[]{:S(2)}) collective-permute-start(f32[64,128]{1,0:T(8,128)S(1)} %get-tuple-element.60.vec.second), channel_id=1, source_target_pairs={{0,1},{1,0},{2,3},{3,2},{4,5},{5,4},{6,7},{7,6},{8,9},{9,8},{10,11... | collective-permute-start | bytes 98312 | tf_op jit(solution)/shard_map/ppermute | solution.py:337
  35.0 3.7 %collective-permute-start.9 = (f32[16,128]{1,0:T(8,128)S(1)}, f32[16,128]{1,0:T(8,128)S(1)}, u32[]{:S(2)}, u32[]{:S(2)}) collective-permute-start(f32[16,128]{1,0:T(8,128)S(1)} %get-tuple-element.62), channel_id=1, source_target_pairs={{0,2},{2,0},{4,6},{6,4},{8,10},{10,8},{12,14},{14,12},{16,18},{18,... | collective-permute-start | bytes 24584 | tf_op jit(solution)/shard_map/ppermute | solution.py:384
  35.4 3.7 %collective-permute-start.10 = (f32[16,128]{1,0:T(8,128)S(1)}, f32[16,128]{1,0:T(8,128)S(1)}, u32[]{:S(2)}, u32[]{:S(2)}) collective-permute-start(f32[16,128]{1,0:T(8,128)S(1)} %get-tuple-element.63), channel_id=1, source_target_pairs={{0,4},{2,6},{4,0},{6,2},{8,12},{10,14},{12,8},{14,10},{16,20},{18,... | collective-permute-start | bytes 24584 | tf_op jit(solution)/shard_map/ppermute | solution.py:384
  36.2 3.7 %collective-permute-start.11 = (f32[16,128]{1,0:T(8,128)S(1)}, f32[16,128]{1,0:T(8,128)S(1)}, u32[]{:S(2)}, u32[]{:S(2)}) collective-permute-start(f32[16,128]{1,0:T(8,128)S(1)} %get-tuple-element.64), channel_id=1, source_target_pairs={{0,8},{2,10},{4,12},{6,14},{8,0},{10,2},{12,4},{14,6},{16,24},{18,... | collective-permute-start | bytes 24584 | tf_op jit(solution)/shard_map/ppermute | solution.py:384

commit v2 on v1

--- a/solution.py
+++ b/solution.py
@@ -50,19 +50,41 @@
         copy.wait()
 
 
-def by_rows(count, body, step=ROWS):
-    for start in range(0, count, step):
+def by_rows(count, body):
+    for start in range(0, count, ROWS):
         body(start)
 
 
-def rows_times(blocks, vec, start):
-    chunk = blocks[pl.ds(start, ROWS)].astype(jnp.float32)
-    return jnp.sum(chunk * vec[None], axis=1)
+def folded(terms):
+    row = lax.broadcasted_iota(jnp.int32, terms[0].shape, 0)
+    for step in (4, 2, 1):
+        half = len(terms) // 2
+        keep = (row & step) == 0
+        terms = [
+            jnp.where(keep, a, b)
+            + jnp.where(keep, pltpu.roll(a, ROWS - step, 0), pltpu.roll(b, step, 0))
+            for a, b in zip(terms[:half], terms[half:])
+        ]
+    return terms[0]
+
+
+def rows_times(start, *pairs):
+    terms = []
+    for at in range(start, start + ROWS):
+        term = None
+        for blocks, vec in pairs:
+            for low in range(0, vec.shape[0], 2 * ROWS):
+                chunk = blocks[at, low : low + 2 * ROWS, :].astype(jnp.float32)
+                upper = chunk[:ROWS] * vec[low : low + ROWS]
+                term = upper if term is None else term + upper
+                term = term + chunk[ROWS:] * vec[low + ROWS : low + 2 * ROWS]
+        terms.append(term)
+    return folded(terms)
 
 
 def block_product(blocks, vec, out):
     def body(start):
-        out[pl.ds(start, ROWS), :] = rows_times(blocks, vec, start)
+        out[pl.ds(start, ROWS), :] = rows_times(start, (blocks, vec))
 
     by_rows(blocks.shape[0], body)
 
@@ -72,7 +94,7 @@
 
     def body(start):
         here = pl.ds(start, ROWS)
-        part = 0.25 * (2.0 * vec[here, :] - 0.25 * rows_times(dblock, whole, start))
+        part = 0.25 * (2.0 * vec[here, :] - 0.25 * rows_times(start, (dblock, whole)))
         out[here, :] = part if base is None else base[here, :] + part
 
     by_rows(dblock.shape[0], body)
@@ -165,10 +187,7 @@
 
 
 def off_rows(lblocks, chosen, start):
-    value = rows_times(lblocks.at[0], chosen[0], start)
-    for part in range(1, len(chosen)):
-        value = value + rows_times(lblocks.at[part], chosen[part], start)
-    return value
+    return rows_times(start, *[(lblocks.at[part], vec) for part, vec in enumerate(chosen)])
 
 
 def with_interface(known, vec, fblock, out):
@@ -177,7 +196,7 @@
 
     def body(start):
         here = pl.ds(start, ROWS)
-        add = rows_times(fblock, vec, start)
+        add = rows_times(start, (fblock, vec))
         pad = jnp.zeros((ROWS, out.shape[1] - width), jnp.float32)
         out[here, :] = known[here, :] + jnp.concatenate([add, pad], axis=1)
 
@@ -195,7 +214,7 @@
     vec = resid[...]
     for copy, piece in zip(copies[1:-1], pieces):
         copy.wait()
-        scratch[piece, :] = rows_times(zvec, vec, piece.start)
+        scratch[piece, :] = rows_times(piece.start, (zvec, vec))
     scratch[zvec.shape[0] :, :] = jnp.zeros((ROWS, vec.shape[1]), jnp.float32)
     post(message, scratch)
     sent = start_all((message,), (message_far,), done, len(copies))
@@ -219,7 +238,7 @@
 
     def body(start):
         rows = pl.ds(start, ROWS)
-        out[rows, :] = rows_times(dblock, whole, start)
+        out[rows, :] = rows_times(start, (dblock, whole))
         copied[rows] = dblock[rows]
 
     by_rows(out.shape[0], body)
@@ -236,7 +255,7 @@
 
     def own(start):
         rows = pl.ds(start, ROWS)
-        out[rows, :] = out[rows, :] + rows_times(dblock, whole, start)
+        out[rows, :] = out[rows, :] + rows_times(start, (dblock, whole))
 
     by_rows(out.shape[0], off)
     copies[0].wait()

time: 51.4 us -> 51.1 us (level)
    all_to_all x2, waiting for transfers between devices: 5.86 us -> 6.41 us  [everywhere(): lax.all_to_all(message, ('sub', 'coarse'), 0, 0, tiled=len(message.shape)...]
  transfers between devices with their start and end apart: 14 -> 14, of which waited for: 10 -> 8; matrix products, arithmetic and copies ran while one was open for 0% -> 0% of each run, Pallas kernels for 19% -> 19%
where the time goes in v2:
time: 51.1 us; the launch traced here: 50.7 us
  starting transfers between devices  15.6 us (31%)
  Pallas kernels  14.4 us (28%)
  waiting for transfers between devices  10 us (20%)
  blocking collectives  9.87 us (19%)
  between operations  0.79 us (2%)
    pallas_call x15, Pallas kernels, kernel(): pl.pallas_call(body, out_shape=outs, in_specs=[here] * len(near) + [there...  13.6 us
    all_to_all x2, starting transfers between devices, everywhere(): lax.all_to_all(message, ('sub', 'coarse'), 0, 0, tiled=len(message.shape)...  10.2 us
    all_to_all x1, blocking collectives, everywhere(): lax.all_to_all(message, ('sub', 'coarse'), 0, 0, tiled=len(message.shape)...  9.87 us
    all_to_all x2, waiting for transfers between devices, everywhere(): lax.all_to_all(message, ('sub', 'coarse'), 0, 0, tiled=len(message.shape)...  6.41 us
    ppermute x6, starting transfers between devices, apply(): lax.ppermute(part, 'sub', swap(subs, 1 << bit))  3.75 us
    ppermute x6, waiting for transfers between devices, apply(): lax.ppermute(part, 'sub', swap(subs, 1 << bit))  2.21 us
    ppermute x6, starting transfers between devices, gathered(): return lax.ppermute(array, 'coarse', swap(2, 1))[None]  1.62 us
    ppermute x6, waiting for transfers between devices, gathered(): return lax.ppermute(array, 'coarse', swap(2, 1))[None]  1.41 us
  transfers between devices with their start and end apart: 14, of which 8 were waited for; matrix products, arithmetic and copies ran while one was open for 0% of the time, Pallas kernels for 19%

profile of v2, /device:TPU:0, one launch (start us, length us, event | category | flops | bytes accessed | tf_op | source)
XLA Modules:
  0.0 50.7 jit_solution(11330076507285384637)
XLA Ops:
  0.6 2.1 %shard_map.86 = (f32[64,128]{1,0:T(8,128)S(1)}, bf16[64,64,128]{2,1,0:T(8,128)(2,1)S(1)}, f32[64,128]{1,0:T(8,128)S(1)}, f32[32,3,128]{2,1,0:T(4,128)}) custom-call(f32[64,128]{1,0:T(8,128)} %bitcast.52, bf16[32,64,128]{2,1,0:T(8,128)(2,1)} %bitcast.47, bf16[64,64,128]{2,1,0:T(8,128)(2,1)} %bitcast.44), custom_call_target="tpu_custom_call" | custom-call | tf_op jit(solution)/shard_map/pallas_call | solution.py:23
  2.7 7.3 %all-to-all-start = ((f32[32,3,128]{2,1,0:T(4,128)}), f32[32,3,128]{2,1,0:T(4,128)S(1)}, u32[]{:S(2)}, u32[]{:S(2)}) async-start(f32[32,3,128]{2,1,0:T(4,128)} %get-tuple-element.42), calls=%async_computation | async-start | bytes 131072 | tf_op jit(solution)/shard_map/all_to_all | solution.py:375
  10.0 0.3 collective-permute-start
  10.3 0.2 shard_map.87
  10.6 0.7 %collective-permute-done = f32[64,128]{1,0:T(8,128)S(1)} collective-permute-done((f32[64,128]{1,0:T(8,128)S(1)}, f32[64,128]{1,0:T(8,128)S(1)}, u32[]{:S(2)}, u32[]{:S(2)}) %collective-permute-start) | collective-permute-done | bytes 32800 | tf_op jit(solution)/shard_map/ppermute | solution.py:356
  11.3 0.8 %shard_map.88.vec.state = f32[64,128]{1,0:T(8,128)S(1)} custom-call(f32[64,128]{1,0:T(8,128)S(1)} %get-tuple-element.36.vec.state, f32[1,64,128]{2,1,0:T(8,128)S(1)} %bitcast.39, f32[64,128]{1,0:T(8,128)S(1)} %get-tuple-element.38.own, f32[64,128]{1,0:T(8,128)S(1)} %get-tuple-element.39.resid, bf16[64,64,128]{2,1,0:T(8,128)(2,1)S(1)} %get-tuple-element.40.dblock, ...), custom_call_target="tpu_custom_call" | custom-call | tf_op jit(solution)/shard_map/pallas_call | solution.py:23
  12.1 0.3 collective-permute-start.1
  12.4 1.1 %shard_map.89 = (f32[64,128]{1,0:T(8,128)S(1)}, bf16[32,64,128]{2,1,0:T(8,128)(2,1)S(1)}, f32[32,512]{1,0:T(8,128)S(1)}) custom-call(f32[64,128]{1,0:T(8,128)S(1)} %shard_map.88.vec.state, bf16[64,64,128]{2,1,0:T(8,128)(2,1)S(1)} %get-tuple-element.40.dblock, bf16[32,64,128]{2,1,0:T(8,128)(2,1)} %bitcast.48, f32[32,512]{1,0:T(8,128)} %refs_1_.3), custom_call_target="tpu_custom_call" | custom-call | tf_op jit(solution)/shard_map/pallas_call | solution.py:23
  13.5 0.0 copy-start.1
  13.5 0.0 collective-permute-done.1
  13.5 0.8 %shard_map.90.state = f32[64,128]{1,0:T(8,128)S(1)} custom-call(f32[64,128]{1,0:T(8,128)S(1)} %shard_map.88.vec.state, f32[1,64,128]{2,1,0:T(8,128)S(1)} %bitcast.41, f32[64,128]{1,0:T(8,128)S(1)} %get-tuple-element.41.own, f32[64,128]{1,0:T(8,128)S(1)} %get-tuple-element.39.resid, bf16[64,64,128]{2,1,0:T(8,128)(2,1)S(1)} %get-tuple-element.40.dblock, ...), custom_call_target="tpu_custom_call" | custom-call | tf_op jit(solution)/shard_map/pallas_call | solution.py:23
  14.2 3.2 %all-to-all-done = f32[32,3,128]{2,1,0:T(4,128)S(1)} async-done(((f32[32,3,128]{2,1,0:T(4,128)}), f32[32,3,128]{2,1,0:T(4,128)S(1)}, u32[]{:S(2)}, u32[]{:S(2)}) %all-to-all-start) | async-done | bytes 49184 | tf_op jit(solution)/shard_map/all_to_all | solution.py:375
  17.5 0.3 shard_map.91
  17.7 0.2 collective-permute-start.2
  17.9 0.5 collective-permute-start.3
  18.4 0.8 %collective-permute-start.4 = (f32[16,128]{1,0:T(8,128)S(1)}, f32[16,128]{1,0:T(8,128)S(1)}, u32[]{:S(2)}, u32[]{:S(2)}) collective-permute-start(f32[16,128]{1,0:T(8,128)S(1)} %get-tuple-element.48), channel_id=1, source_target_pairs={{0,4},{2,6},{4,0},{6,2},{8,12},{10,14},{12,8},{14,10},{16,20},{18,... | collective-permute-start | bytes 24584 | tf_op jit(solution)/shard_map/ppermute | solution.py:403
  19.2 0.6 %collective-permute-start.5 = (f32[16,128]{1,0:T(8,128)S(1)}, f32[16,128]{1,0:T(8,128)S(1)}, u32[]{:S(2)}, u32[]{:S(2)}) collective-permute-start(f32[16,128]{1,0:T(8,128)S(1)} %get-tuple-element.49), channel_id=1, source_target_pairs={{0,8},{2,10},{4,12},{6,14},{8,0},{10,2},{12,4},{14,6},{16,24},{18,... | collective-permute-start | bytes 24584 | tf_op jit(solution)/shard_map/ppermute | solution.py:403
  19.8 0.0 collective-permute-done.2
  19.8 0.0 copy-done.1
  19.8 1.6 %shard_map.92 = (f32[64,128]{1,0:T(8,128)S(1)}, bf16[64,64,96]{2,1,0:T(8,128)(2,1)S(1)}, bf16[64,64,128]{2,1,0:T(8,128)(2,1)S(1)}) custom-call(f32[64,128]{1,0:T(8,128)S(1)} %get-tuple-element.45.vec.first, f32[1,64,128]{2,1,0:T(8,128)S(1)} %bitcast.37, s32[2,128]{1,0:T(2,128)S(1)} %bitcast.33, bf16[2,64,64,128]{3,2,1,0:T(8,128)(2,1)S(1)} %bitcast.24, ...), custom_call_target="tpu_custom_call" | custom-call | tf_op jit(solution)/shard_map/pallas_call | solution.py:23
  21.4 0.2 collective-permute-done.3.near0
  21.6 0.4 collective-permute-done.4.near1
  22.0 0.8 %collective-permute-done.5.near2 = f32[16,128]{1,0:T(8,128)S(1)} collective-permute-done((f32[16,128]{1,0:T(8,128)S(1)}, f32[16,128]{1,0:T(8,128)S(1)}, u32[]{:S(2)}, u32[]{:S(2)}) %collective-permute-start.5) | collective-permute-done | bytes 8224 | tf_op jit(solution)/shard_map/ppermute | solution.py:403
  22.8 0.0 copy-done.2
  22.8 1.2 %shard_map.93 = (f32[64,128]{1,0:T(8,128)S(1)}, f32[64,128]{1,0:T(8,128)S(1)}, f32[32,3,128]{2,1,0:T(4,128)}) custom-call(f32[64,128]{1,0:T(8,128)S(1)} %get-tuple-element.46.known, f32[16,128]{1,0:T(8,128)S(1)} %collective-permute-done.3.near0, f32[16,128]{1,0:T(8,128)S(1)} %collective-permute-done.4.near1, f32[16,128]{1,0:T(8,128)S(1)} %collective-permute-done.5.near2, ...), custom_call_target="tpu_custom_call" | custom-call | tf_op jit(solution)/shard_map/pallas_call | solution.py:23
  24.0 2.9 %all-to-all-start.1 = ((f32[32,3,128]{2,1,0:T(4,128)}), f32[32,3,128]{2,1,0:T(4,128)S(1)}, u32[]{:S(2)}, u32[]{:S(2)}) async-start(f32[32,3,128]{2,1,0:T(4,128)} %get-tuple-element.57), calls=%async_computation.1 | async-start | bytes 131072 | tf_op jit(solution)/shard_map/all_to_all | solution.py:375
  26.9 0.3 collective-permute-start.6
  27.2 0.2 shard_map.94
  27.5 0.7 %collective-permute-done.6 = f32[64,128]{1,0:T(8,128)S(1)} collective-permute-done((f32[64,128]{1,0:T(8,128)S(1)}, f32[64,128]{1,0:T(8,128)S(1)}, u32[]{:S(2)}, u32[]{:S(2)}) %collective-permute-start.6) | collective-permute-done | bytes 32800 | tf_op jit(solution)/shard_map/ppermute | solution.py:356
  28.2 0.8 %shard_map.95.vec.state = f32[64,128]{1,0:T(8,128)S(1)} custom-call(f32[64,128]{1,0:T(8,128)S(1)} %get-tuple-element.52.vec.state, f32[1,64,128]{2,1,0:T(8,128)S(1)} %bitcast.40, f32[64,128]{1,0:T(8,128)S(1)} %get-tuple-element.53.own, f32[64,128]{1,0:T(8,128)S(1)} %get-tuple-element.54.resid.image, bf16[64,64,128]{2,1,0:T(8,128)(2,1)S(1)} %get-tuple-element.55.dblock, ...), custom_call_target="tpu_custom_call" | custom-call | tf_op jit(solution)/shard_map/pallas_call | solution.py:23
  28.9 0.3 collective-permute-start.7
  29.3 1.1 %shard_map.96 = (f32[64,128]{1,0:T(8,128)S(1)}, bf16[32,64,128]{2,1,0:T(8,128)(2,1)S(1)}, f32[32,512]{1,0:T(8,128)S(1)}) custom-call(f32[64,128]{1,0:T(8,128)S(1)} %shard_map.95.vec.state, bf16[64,64,128]{2,1,0:T(8,128)(2,1)S(1)} %get-tuple-element.55.dblock, bf16[32,64,128]{2,1,0:T(8,128)(2,1)} %bitcast.49, f32[32,512]{1,0:T(8,128)} %refs_1_.3), custom_call_target="tpu_custom_call" | custom-call | tf_op jit(solution)/shard_map/pallas_call | solution.py:23
  30.3 0.0 collective-permute-done.7
  30.3 0.8 %shard_map.97.state = f32[64,128]{1,0:T(8,128)S(1)} custom-call(f32[64,128]{1,0:T(8,128)S(1)} %shard_map.95.vec.state, f32[1,64,128]{2,1,0:T(8,128)S(1)} %bitcast.42, f32[64,128]{1,0:T(8,128)S(1)} %get-tuple-element.56.own, f32[64,128]{1,0:T(8,128)S(1)} %get-tuple-element.54.resid.image, bf16[64,64,128]{2,1,0:T(8,128)(2,1)S(1)} %get-tuple-element.55.dblock, ...), custom_call_target="tpu_custom_call" | custom-call | tf_op jit(solution)/shard_map/pallas_call | solution.py:23
  31.1 3.2 %all-to-all-done.1 = f32[32,3,128]{2,1,0:T(4,128)S(1)} async-done(((f32[32,3,128]{2,1,0:T(4,128)}), f32[32,3,128]{2,1,0:T(4,128)S(1)}, u32[]{:S(2)}, u32[]{:S(2)}) %all-to-all-start.1) | async-done | bytes 49184 | tf_op jit(solution)/shard_map/all_to_all | solution.py:375
  34.3 0.3 shard_map.98
  34.6 0.2 collective-permute-start.8
  34.8 0.5 collective-permute-start.9
  35.3 0.8 %collective-permute-start.10 = (f32[16,128]{1,0:T(8,128)S(1)}, f32[16,128]{1,0:T(8,128)S(1)}, u32[]{:S(2)}, u32[]{:S(2)}) collective-permute-start(f32[16,128]{1,0:T(8,128)S(1)} %get-tuple-element.63), channel_id=1, source_target_pairs={{0,4},{2,6},{4,0},{6,2},{8,12},{10,14},{12,8},{14,10},{16,20},{18,... | collective-permute-start | bytes 24584 | tf_op jit(solution)/shard_map/ppermute | solution.py:403
  36.0 0.6 %collective-permute-start.11 = (f32[16,128]{1,0:T(8,128)S(1)}, f32[16,128]{1,0:T(8,128)S(1)}, u32[]{:S(2)}, u32[]{:S(2)}) collective-permute-start(f32[16,128]{1,0:T(8,128)S(1)} %get-tuple-element.64), channel_id=1, source_target_pairs={{0,8},{2,10},{4,12},{6,14},{8,0},{10,2},{12,4},{14,6},{16,24},{18,... | collective-permute-start | bytes 24584 | tf_op jit(solution)/shard_map/ppermute | solution.py:403
  36.7 0.0 collective-permute-done.8
  36.7 2.2 %shard_map.99 = (f32[64,128]{1,0:T(8,128)S(1)}, bf16[64,64,96]{2,1,0:T(8,128)(2,1)S(1)}) custom-call(f32[64,128]{1,0:T(8,128)S(1)} %get-tuple-element.60.vec.second, f32[1,64,128]{2,1,0:T(8,128)S(1)} %bitcast.38, s32[2,128]{1,0:T(2,128)S(1)} %bitcast.36, bf16[2,64,64,128]{3,2,1,0:T(8,128)(2,1)S(1)} %bitcast.27, bf16[64,64,128]{2,1,0:T(8,128)(2,1)} %bitcast.46, ...), custom_call_target="tpu_custom_call" | custom-call | tf_op jit(solution)/shard_map/pallas_call | solution.py:23
  38.9 0.0 collective-permute-done.9.near0
  38.9 0.0 collective-permute-done.10.near1
  38.9 0.8 %collective-permute-done.11.near2 = f32[16,128]{1,0:T(8,128)S(1)} collective-permute-done((f32[16,128]{1,0:T(8,128)S(1)}, f32[16,128]{1,0:T(8,128)S(1)}, u32[]{:S(2)}, u32[]{:S(2)}) %collective-permute-start.11) | collective-permute-done | bytes 8224 | tf_op jit(solution)/shard_map/ppermute | solution.py:403
  39.7 0.4 shard_map.100
  40.1 9.9 %all_to_all.21 = f32[32,1,128]{2,1,0:T(1,128)S(1)} all-to-all(f32[32,1,128]{2,1,0:T(1,128)S(1)} %bitcast.43), channel_id=1, replica_groups=mesh['sub'=16,'coarse'=2] {'sub','coarse'}, dimensions={0} | all-to-all | bytes 32768 | tf_op jit(solution)/shard_map/all_to_all | solution.py:375
  50.0 0.8 %shard_map.101 = (f32[1,64,128]{2,1,0:T(8,128)}, f32[1,64,128]{2,1,0:T(8,128)}) custom-call(f32[32,128]{1,0:T(8,128)S(1)} %bitcast.29, f32[8,128]{1,0:T(8,128)S(1)} %get-tuple-element.68.alpha, f32[64,128]{1,0:T(8,128)S(1)} %get-tuple-element.45.vec.first, f32[64,128]{1,0:T(8,128)S(1)} %get-tuple-element.60.vec.second, ...), custom_call_target="tpu_custom_call" | custom-call | tf_op jit(solution)/shard_map/pallas_call | solution.py:440
  (7 shorter events, 0.0 us)
Async XLA Ops:
  0.6 10.7 %copy-start.3 = (s32[1,2,128]{2,1,0:T(2,128)S(1)}, s32[1,2,128]{2,1,0:T(2,128)}, u32[]{:S(2)}) copy-start(s32[1,2,128]{2,1,0:T(2,128)} %param.11) | copy-start | bytes 3076
  0.6 10.7 %copy-start = (bf16[1,2,64,64,128]{4,3,2,1,0:T(8,128)(2,1)S(1)}, bf16[1,2,64,64,128]{4,3,2,1,0:T(8,128)(2,1)}, u32[]{:S(2)}) copy-start(bf16[1,2,64,64,128]{4,3,2,1,0:T(8,128)(2,1)} %param.8) | copy-start | bytes 6291460
  2.7 14.7 %all-to-all-start = ((f32[32,3,128]{2,1,0:T(4,128)}), f32[32,3,128]{2,1,0:T(4,128)S(1)}, u32[]{:S(2)}, u32[]{:S(2)}) async-start(f32[32,3,128]{2,1,0:T(4,128)} %get-tuple-element.42), calls=%async_computation | async-start | bytes 131072 | tf_op jit(solution)/shard_map/all_to_all | solution.py:375
  10.0 1.3 %collective-permute-start = (f32[64,128]{1,0:T(8,128)S(1)}, f32[64,128]{1,0:T(8,128)S(1)}, u32[]{:S(2)}, u32[]{:S(2)}) collective-permute-start(f32[64,128]{1,0:T(8,128)S(1)} %get-tuple-element.36.vec.state), channel_id=1, source_target_pairs={{0,1},{1,0},{2,3},{3,2},{4,5},{5,4},{6,7},{7,6},{8,9},{9,8},{10,11... | collective-permute-start | bytes 98312 | tf_op jit(solution)/shard_map/ppermute | solution.py:356
  12.1 1.4 %collective-permute-start.1 = (f32[64,128]{1,0:T(8,128)S(1)}, f32[64,128]{1,0:T(8,128)S(1)}, u32[]{:S(2)}, u32[]{:S(2)}) collective-permute-start(f32[64,128]{1,0:T(8,128)S(1)} %shard_map.88.vec.state), channel_id=1, source_target_pairs={{0,1},{1,0},{2,3},{3,2},{4,5},{5,4},{6,7},{7,6},{8,9},{9,8},{10,11... | collective-permute-start | bytes 98312 | tf_op jit(solution)/shard_map/ppermute | solution.py:356
  13.5 6.3 %copy-start.1 = (bf16[32,64,128]{2,1,0:T(8,128)(2,1)}, bf16[32,64,128]{2,1,0:T(8,128)(2,1)S(1)}, u32[]{:S(2)}) copy-start(bf16[32,64,128]{2,1,0:T(8,128)(2,1)S(1)} %get-tuple-element.43.zvec) | copy-start | bytes 1572868
  17.7 2.1 %collective-permute-start.2 = (f32[64,128]{1,0:T(8,128)S(1)}, f32[64,128]{1,0:T(8,128)S(1)}, u32[]{:S(2)}, u32[]{:S(2)}) collective-permute-start(f32[64,128]{1,0:T(8,128)S(1)} %get-tuple-element.45.vec.first), channel_id=1, source_target_pairs={{0,1},{1,0},{2,3},{3,2},{4,5},{5,4},{6,7},{7,6},{8,9},{9,8},{10,11... | collective-permute-start | bytes 98312 | tf_op jit(solution)/shard_map/ppermute | solution.py:356
  17.9 3.7 %collective-permute-start.3 = (f32[16,128]{1,0:T(8,128)S(1)}, f32[16,128]{1,0:T(8,128)S(1)}, u32[]{:S(2)}, u32[]{:S(2)}) collective-permute-start(f32[16,128]{1,0:T(8,128)S(1)} %get-tuple-element.47), channel_id=1, source_target_pairs={{0,2},{2,0},{4,6},{6,4},{8,10},{10,8},{12,14},{14,12},{16,18},{18,... | collective-permute-start | bytes 24584 | tf_op jit(solution)/shard_map/ppermute | solution.py:403
  18.4 3.7 %collective-permute-start.4 = (f32[16,128]{1,0:T(8,128)S(1)}, f32[16,128]{1,0:T(8,128)S(1)}, u32[]{:S(2)}, u32[]{:S(2)}) collective-permute-start(f32[16,128]{1,0:T(8,128)S(1)} %get-tuple-element.48), channel_id=1, source_target_pairs={{0,4},{2,6},{4,0},{6,2},{8,12},{10,14},{12,8},{14,10},{16,20},{18,... | collective-permute-start | bytes 24584 | tf_op jit(solution)/shard_map/ppermute | solution.py:403
  19.2 3.7 %collective-permute-start.5 = (f32[16,128]{1,0:T(8,128)S(1)}, f32[16,128]{1,0:T(8,128)S(1)}, u32[]{:S(2)}, u32[]{:S(2)}) collective-permute-start(f32[16,128]{1,0:T(8,128)S(1)} %get-tuple-element.49), channel_id=1, source_target_pairs={{0,8},{2,10},{4,12},{6,14},{8,0},{10,2},{12,4},{14,6},{16,24},{18,... | collective-permute-start | bytes 24584 | tf_op jit(solution)/shard_map/ppermute | solution.py:403
  19.8 3.0 %copy-start.2 = (bf16[32,64,128]{2,1,0:T(8,128)(2,1)S(1)}, bf16[32,64,128]{2,1,0:T(8,128)(2,1)}, u32[]{:S(2)}) copy-start(bf16[32,64,128]{2,1,0:T(8,128)(2,1)} %copy-done.1) | copy-start | bytes 1572868
  24.0 10.3 %all-to-all-start.1 = ((f32[32,3,128]{2,1,0:T(4,128)}), f32[32,3,128]{2,1,0:T(4,128)S(1)}, u32[]{:S(2)}, u32[]{:S(2)}) async-start(f32[32,3,128]{2,1,0:T(4,128)} %get-tuple-element.57), calls=%async_computation.1 | async-start | bytes 131072 | tf_op jit(solution)/shard_map/all_to_all | solution.py:375
  26.9 1.3 %collective-permute-start.6 = (f32[64,128]{1,0:T(8,128)S(1)}, f32[64,128]{1,0:T(8,128)S(1)}, u32[]{:S(2)}, u32[]{:S(2)}) collective-permute-start(f32[64,128]{1,0:T(8,128)S(1)} %get-tuple-element.52.vec.state), channel_id=1, source_target_pairs={{0,1},{1,0},{2,3},{3,2},{4,5},{5,4},{6,7},{7,6},{8,9},{9,8},{10,11... | collective-permute-start | bytes 98312 | tf_op jit(solution)/shard_map/ppermute | solution.py:356
  28.9 1.4 %collective-permute-start.7 = (f32[64,128]{1,0:T(8,128)S(1)}, f32[64,128]{1,0:T(8,128)S(1)}, u32[]{:S(2)}, u32[]{:S(2)}) collective-permute-start(f32[64,128]{1,0:T(8,128)S(1)} %shard_map.95.vec.state), channel_id=1, source_target_pairs={{0,1},{1,0},{2,3},{3,2},{4,5},{5,4},{6,7},{7,6},{8,9},{9,8},{10,11... | collective-permute-start | bytes 98312 | tf_op jit(solution)/shard_map/ppermute | solution.py:356
  34.6 2.1 %collective-permute-start.8 = (f32[64,128]{1,0:T(8,128)S(1)}, f32[64,128]{1,0:T(8,128)S(1)}, u32[]{:S(2)}, u32[]{:S(2)}) collective-permute-start(f32[64,128]{1,0:T(8,128)S(1)} %get-tuple-element.60.vec.second), channel_id=1, source_target_pairs={{0,1},{1,0},{2,3},{3,2},{4,5},{5,4},{6,7},{7,6},{8,9},{9,8},{10,11... | collective-permute-start | bytes 98312 | tf_op jit(solution)/shard_map/ppermute | solution.py:356
  34.8 4.1 %collective-permute-start.9 = (f32[16,128]{1,0:T(8,128)S(1)}, f32[16,128]{1,0:T(8,128)S(1)}, u32[]{:S(2)}, u32[]{:S(2)}) collective-permute-start(f32[16,128]{1,0:T(8,128)S(1)} %get-tuple-element.62), channel_id=1, source_target_pairs={{0,2},{2,0},{4,6},{6,4},{8,10},{10,8},{12,14},{14,12},{16,18},{18,... | collective-permute-start | bytes 24584 | tf_op jit(solution)/shard_map/ppermute | solution.py:403
  35.3 3.7 %collective-permute-start.10 = (f32[16,128]{1,0:T(8,128)S(1)}, f32[16,128]{1,0:T(8,128)S(1)}, u32[]{:S(2)}, u32[]{:S(2)}) collective-permute-start(f32[16,128]{1,0:T(8,128)S(1)} %get-tuple-element.63), channel_id=1, source_target_pairs={{0,4},{2,6},{4,0},{6,2},{8,12},{10,14},{12,8},{14,10},{16,20},{18,... | collective-permute-start | bytes 24584 | tf_op jit(solution)/shard_map/ppermute | solution.py:403
  36.0 3.7 %collective-permute-start.11 = (f32[16,128]{1,0:T(8,128)S(1)}, f32[16,128]{1,0:T(8,128)S(1)}, u32[]{:S(2)}, u32[]{:S(2)}) collective-permute-start(f32[16,128]{1,0:T(8,128)S(1)} %get-tuple-element.64), channel_id=1, source_target_pairs={{0,8},{2,10},{4,12},{6,14},{8,0},{10,2},{12,4},{14,6},{16,24},{18,... | collective-permute-start | bytes 24584 | tf_op jit(solution)/shard_map/ppermute | solution.py:403

commit v3 on v2

--- a/solution.py
+++ b/solution.py
@@ -11,12 +11,12 @@
 ITERS = 2
 BITS = 3
 ROWS = 8
-WIDE = 3
 SCOPED = 6 << 20
+BESIDE = 1 << 30
 HIGH = lax.Precision.HIGHEST
 
 
-def kernel(body, outs, near, far=(), scratch=()):
+def kernel(body, outs, near, far=(), scratch=(), cost=0):
     near = [pltpu.with_memory_space_constraint(a, pltpu.VMEM) for a in near]
     far = [pltpu.with_memory_space_constraint(a, pltpu.HBM) for a in far]
     there, here = pl.BlockSpec(memory_space=pl.ANY), pl.BlockSpec(memory_space=pltpu.VMEM)
@@ -26,7 +26,7 @@
         in_specs=[here] * len(near) + [there] * len(far),
         out_specs=[there if o.memory_space == pltpu.HBM else here for o in outs],
         scratch_shapes=scratch,
-        cost_estimate=pl.CostEstimate(flops=0, bytes_accessed=0, transcendentals=0),
+        cost_estimate=pl.CostEstimate(flops=cost, bytes_accessed=cost, transcendentals=0),
         compiler_params=pltpu.CompilerParams(vmem_limit_bytes=SCOPED),
     )(*near, *far)
 
@@ -89,13 +89,15 @@
     by_rows(blocks.shape[0], body)
 
 
-def relaxed(dblock, vec, out, base=None):
+def relaxed(dblock, vec, out, base=None, copied=None):
     whole = vec[...]
 
     def body(start):
         here = pl.ds(start, ROWS)
         part = 0.25 * (2.0 * vec[here, :] - 0.25 * rows_times(start, (dblock, whole)))
         out[here, :] = part if base is None else base[here, :] + part
+        if copied is not None:
+            copied[here] = dblock[here]
 
     by_rows(dblock.shape[0], body)
 
@@ -114,10 +116,7 @@
     row = lax.broadcasted_iota(jnp.int32, scratch.shape, 0)
     place = lax.rem(sub + row // nvec, groups) * nvec + lax.rem(row, nvec)
     line = jnp.sum(jnp.where(lane == place, sums, 0.0), axis=0, keepdims=True)
-    if len(message.shape) == 3:
-        message[...] = jnp.broadcast_to(line[None], message.shape)
-    else:
-        message[...] = jnp.broadcast_to(line, message.shape)
+    message[...] = jnp.broadcast_to(line, message.shape)
 
 
 def inner_products(scratch, resid, image):
@@ -230,21 +229,6 @@
     wait_all(copies)
 
 
-def diag_copy_kernel(vec, dblock, *refs):
-    count = (len(refs) - 3) // 2
-    copies = start_all(refs[:count], refs[count + 2 : -1], refs[-1])
-    out, copied = refs[count : count + 2]
-    whole = vec[...]
-
-    def body(start):
-        rows = pl.ds(start, ROWS)
-        out[rows, :] = rows_times(start, (dblock, whole))
-        copied[rows] = dblock[rows]
-
-    by_rows(out.shape[0], body)
-    wait_all(copies)
-
-
 def apply_kernel(vec, others, cols, lblocks, dblock_far, fblock_far, out, fblock, dblock, done):
     copies = start_all((dblock_far, fblock_far), (dblock, fblock), done)
     chosen = [picked(vec, others, cols, part) for part in range(lblocks.shape[0])]
@@ -263,7 +247,8 @@
     copies[1].wait()
 
 
-def sweep_kernel(state, others, own, resid, dblock, lblocks, cols, out, rest):
+def sweep_kernel(state, others, own, resid, dblock, lblocks, cols, out, *refs):
+    *copied, rest = refs
     chosen = [picked(state, others, cols, part) for part in range(lblocks.shape[0])]
 
     def body(start):
@@ -271,7 +256,7 @@
         rest[here, :] = resid[here, :] - (own[here, :] + off_rows(lblocks, chosen, start))
 
     by_rows(dblock.shape[0], body)
-    relaxed(dblock, rest, out, state)
+    relaxed(dblock, rest, out, state, *copied)
 
 
 def direction_kernel(count, state, arrived, zvec, inverse, out, *parts):
@@ -334,7 +319,7 @@
     alpha[...] = jnp.broadcast_to(size, alpha.shape)
 
 
-def last_image_kernel(known, near0, near1, near2, fblock, resid, image, message, scratch):
+def last_image_kernel(known, near0, near1, near2, fblock, resid, dblock, image, message, scratch):
     with_interface(known, near_lanes((near0, near1, near2), known.shape[0]), fblock, image)
     scratch[...] = jnp.zeros(scratch.shape, jnp.float32)
     inner_products(scratch, resid[...], image[...])
@@ -363,7 +348,6 @@
     shape = right_side.shape[1:]
     nvec, lanes = zfar.shape[0], shape[1]
     flat, small, parcel = vmem(shape), vmem((nvec + ROWS, lanes)), vmem((subs * count, lanes))
-    wide = vmem((subs * count, WIDE, lanes))
 
     def sems(number):
         return pltpu.SemaphoreType.DMA((number,))
@@ -372,70 +356,60 @@
         return space(array.shape, array.dtype)
 
     def everywhere(message):
-        return lax.all_to_all(message, ("sub", "coarse"), 0, 0, tiled=len(message.shape) == 2)
-
-    def sweep(state, others, own, resid, dblock, lblocks, cols):
-        (out,) = kernel(sweep_kernel, [flat], [state, others, own, resid, dblock, lblocks, cols], (), [flat])
-        return out
-
-    def diag(vec, dblock, *far):
-        return kernel(diag_kernel, [flat, *map(like, far)], [vec, dblock], far, [sems(max(len(far), 1))])
-
-    def smooth(state, resid, dblock, lblocks, cols, *far):
+        return lax.all_to_all(message, ("sub", "coarse"), 0, 0, tiled=True)
+
+    def sweep(*args, copy=False):
+        return kernel(sweep_kernel, [flat, like(dfar)] if copy else [flat], args, (), [flat])
+
+    def diag(vec, dblock, far=(), cost=0):
+        return kernel(diag_kernel, [flat, *map(like, far)], [vec, dblock], far, [sems(max(len(far), 1))], cost)
+
+    def smooth(state, resid, dblock, lblocks, cols, cost=0):
         others = gathered(state, count)
-        own, dblock, *more = kernel(
-            diag_copy_kernel,
-            [flat, like(dblock), *map(like, far)],
-            [state, dblock],
-            far,
-            [sems(max(len(far), 1))],
-        )
-        lblocks, cols = more or (lblocks, cols)
-        state = sweep(state, others, own, resid, dblock, lblocks, cols)
+        (own,) = diag(state, dblock, (), cost)
+        state, dblock = sweep(state, others, own, resid, dblock, lblocks, cols, copy=True)
         for at in range(SWEEPS - 2):
             others = gathered(state, count)
-            own, *held = diag(state, dblock, *((zfar, coarse_inverse) if at == SWEEPS - 3 else ()))
-            state = sweep(state, others, own, resid, dblock, lblocks, cols)
-        return state, held, lblocks, cols
-
-    def apply(vec, parts, lblocks, cols, last=False):
+            own, *held = diag(state, dblock, (zfar, coarse_inverse) if at == SWEEPS - 3 else (), BESIDE)
+            (state,) = sweep(state, others, own, resid, dblock, lblocks, cols)
+        return state, held
+
+    def apply(vec, parts, lblocks, cols):
         others = gathered(vec, count)
         near = [lax.ppermute(part, "sub", swap(subs, 1 << bit)) for bit, part in enumerate(parts)]
-        outs, scratch = [flat, like(ffar)], [like(dfar)]
-        if not last:
-            outs, scratch = outs + scratch, []
-        known, fblock, *brought = kernel(
-            apply_kernel, outs, [vec, others, cols, lblocks], [dfar, ffar], [*scratch, sems(2)]
+        known, fblock, dblock = kernel(
+            apply_kernel, [flat, like(ffar), like(dfar)], [vec, others, cols, lblocks], [dfar, ffar], [sems(2)]
         )
-        return [known, *near, fblock], brought
-
-    wide_far = pltpu.HBM(wide.shape, jnp.float32)
+        return [known, *near, fblock], dblock
+
+    parcel_far = pltpu.HBM(parcel.shape, jnp.float32)
     resid, dblock, state, message = kernel(
         first_kernel,
-        [flat, like(dfar), flat, wide_far],
+        [flat, like(dfar), flat, parcel_far],
         [],
         [right_side[0], zfar, dfar],
-        [like(zfar), small, wide, sems(3 + nvec // ROWS)],
-    )
-    arrived = everywhere(message)[:, 0, :]
-    state, held, lblocks, cols = smooth(state, resid, dblock, lfar, cfar)
+        [like(zfar), small, parcel, sems(3 + nvec // ROWS)],
+    )
+    arrived = everywhere(message)
+    lblocks, cols = lfar, cfar
+    state, held = smooth(state, resid, dblock, lblocks, cols, BESIDE)
     packed = [vmem((shape[0] * ffar.shape[2] // (BITS * lanes), lanes))] * BITS
     first, *parts = kernel(
         functools.partial(direction_kernel, count), [flat, *packed], [state, arrived, *held]
     )
-    terms, (dblock,) = apply(first, parts, lblocks, cols)
+    terms, dblock = apply(first, parts, lblocks, cols)
     first_image, state, message = kernel(
-        image_kernel, [flat, flat, wide_far], [*terms, resid, held[0], dblock], [], [small, wide, sems(1)]
-    )
-    arrived = everywhere(message)[:, 0, :]
-    state, held, _, _ = smooth(state, first_image, dblock, lblocks, cols)
+        image_kernel, [flat, flat, parcel_far], [*terms, resid, held[0], dblock], [], [small, parcel, sems(1)]
+    )
+    arrived = everywhere(message)
+    state, held = smooth(state, first_image, dblock, lblocks, cols)
     second, rest, alpha, *parts = kernel(
         functools.partial(next_direction_kernel, count),
         [flat, flat, vmem((ROWS, lanes)), *packed],
         [state, arrived, *held, first, resid, first_image],
     )
-    terms, _ = apply(second, parts, lblocks, cols, True)
-    image, message = kernel(last_image_kernel, [flat, parcel], [*terms, rest], [], [small])
+    terms, dblock = apply(second, parts, lblocks, cols)
+    image, message = kernel(last_image_kernel, [flat, parcel], [*terms, rest, dblock], [], [small])
     arrived = everywhere(message)
     return pl.pallas_call(
         functools.partial(final_kernel, nvec, count),

time: 51.1 us -> 50.4 us (0.986)
  Pallas kernels: 14.4 us -> 13.6 us
    pallas_call x15, Pallas kernels: 13.6 us -> 12.9 us  [kernel(): pl.pallas_call(body, out_shape=outs, in_specs=[here] * len(near) + [there...]
    ppermute x6, waiting for transfers between devices: 1.41 us -> 0.71 us  [gathered(): return lax.ppermute(array, 'coarse', swap(2, 1))[None]]
    all_to_all x2, waiting for transfers between devices: 6.41 us -> 6.99 us  [everywhere(): return lax.all_to_all(message, ('sub', 'coarse'), 0, 0, tiled=True)]
  transfers between devices with their start and end apart: 14 -> 14, of which waited for: 8 -> 8; matrix products, arithmetic and copies ran while one was open for 0% -> 0% of each run, Pallas kernels for 19% -> 18%
where the time goes in v3:
time: 50.4 us; the launch traced here: 50.1 us
  starting transfers between devices  15.6 us (31%)
  Pallas kernels  13.6 us (27%)
  waiting for transfers between devices  10.3 us (20%)
  blocking collectives  9.67 us (19%)
  between operations  0.81 us (2%)
    pallas_call x15, Pallas kernels, kernel(): pl.pallas_call(body, out_shape=outs, in_specs=[here] * len(near) + [there...  12.9 us
    all_to_all x2, starting transfers between devices, everywhere(): return lax.all_to_all(message, ('sub', 'coarse'), 0, 0, tiled=True)  10.5 us
    all_to_all x1, blocking collectives, everywhere(): return lax.all_to_all(message, ('sub', 'coarse'), 0, 0, tiled=True)  9.67 us
    all_to_all x2, waiting for transfers between devices, everywhere(): return lax.all_to_all(message, ('sub', 'coarse'), 0, 0, tiled=True)  6.99 us
    ppermute x6, starting transfers between devices, apply(): lax.ppermute(part, 'sub', swap(subs, 1 << bit))  3.91 us
    ppermute x6, waiting for transfers between devices, apply(): lax.ppermute(part, 'sub', swap(subs, 1 << bit))  2.63 us
    ppermute x6, starting transfers between devices, gathered(): return lax.ppermute(array, 'coarse', swap(2, 1))[None]  1.16 us
  transfers between devices with their start and end apart: 14, of which 8 were waited for; matrix products, arithmetic and copies ran while one was open for 0% of the time, Pallas kernels for 18%

profile of v3, /device:TPU:0, one launch (start us, length us, event | category | flops | bytes accessed | tf_op | source)
XLA Modules:
  0.0 50.1 jit_solution(9693329263210687678)
XLA Ops:
  0.6 1.9 %shard_map.86 = (f32[64,128]{1,0:T(8,128)S(1)}, bf16[64,64,128]{2,1,0:T(8,128)(2,1)S(1)}, f32[64,128]{1,0:T(8,128)S(1)}, f32[32,128]{1,0:T(8,128)}) custom-call(f32[64,128]{1,0:T(8,128)} %bitcast.54, bf16[32,64,128]{2,1,0:T(8,128)(2,1)} %bitcast.51, bf16[64,64,128]{2,1,0:T(8,128)(2,1)} %bitcast.46), custom_call_target="tpu_custom_call" | custom-call | tf_op jit(solution)/shard_map/pallas_call | solution.py:23
  2.5 0.0 copy-start
  2.5 0.0 copy-start.3
  2.6 7.3 %all-to-all-start = ((f32[32,1,128]{2,1,0:T(1,128)}), f32[32,1,128]{2,1,0:T(1,128)S(1)}, u32[]{:S(2)}, u32[]{:S(2)}) async-start(f32[32,1,128]{2,1,0:T(1,128)} %bitcast.56), calls=%async_computation | async-start | bytes 32768 | tf_op jit(solution)/shard_map/all_to_all | solution.py:359
  9.9 0.3 collective-permute-start
  10.2 0.2 shard_map.87.own
  10.4 0.7 %collective-permute-done = f32[64,128]{1,0:T(8,128)S(1)} collective-permute-done((f32[64,128]{1,0:T(8,128)S(1)}, f32[64,128]{1,0:T(8,128)S(1)}, u32[]{:S(2)}, u32[]{:S(2)}) %collective-permute-start) | collective-permute-done | bytes 32800 | tf_op jit(solution)/shard_map/ppermute | solution.py:341
  11.1 0.0 copy-done.3
  11.2 0.8 %shard_map.88 = (f32[64,128]{1,0:T(8,128)S(1)}, bf16[64,64,128]{2,1,0:T(8,128)(2,1)S(1)}) custom-call(f32[64,128]{1,0:T(8,128)S(1)} %get-tuple-element.37.vec.state, f32[1,64,128]{2,1,0:T(8,128)S(1)} %bitcast.44, f32[64,128]{1,0:T(8,128)S(1)} %shard_map.87.own, f32[64,128]{1,0:T(8,128)S(1)} %get-tuple-element.39.resid, ...), custom_call_target="tpu_custom_call" | custom-call | tf_op jit(solution)/shard_map/pallas_call | solution.py:23
  11.9 0.3 collective-permute-start.1
  12.2 1.1 %shard_map.89 = (f32[64,128]{1,0:T(8,128)S(1)}, bf16[32,64,128]{2,1,0:T(8,128)(2,1)S(1)}, f32[32,512]{1,0:T(8,128)S(1)}) custom-call(f32[64,128]{1,0:T(8,128)S(1)} %get-tuple-element.40.vec.state, bf16[64,64,128]{2,1,0:T(8,128)(2,1)S(1)} %get-tuple-element.41.dblock, bf16[32,64,128]{2,1,0:T(8,128)(2,1)} %bitcast.52, f32[32,512]{1,0:T(8,128)} %refs_1_.3), custom_call_target="tpu_custom_call" | custom-call | flops 1073741824 | bytes 1073741824 | tf_op jit(solution)/shard_map/pallas_call | solution.py:23
  13.3 0.0 collective-permute-done.1
  13.3 0.8 %shard_map.90.state = f32[64,128]{1,0:T(8,128)S(1)} custom-call(f32[64,128]{1,0:T(8,128)S(1)} %get-tuple-element.40.vec.state, f32[1,64,128]{2,1,0:T(8,128)S(1)} %bitcast.42, f32[64,128]{1,0:T(8,128)S(1)} %get-tuple-element.42.own, f32[64,128]{1,0:T(8,128)S(1)} %get-tuple-element.39.resid, bf16[64,64,128]{2,1,0:T(8,128)(2,1)S(1)} %get-tuple-element.41.dblock, ...), custom_call_target="tpu_custom_call" | custom-call | tf_op jit(solution)/shard_map/pallas_call | solution.py:23
  14.1 2.9 %all-to-all-done = f32[32,1,128]{2,1,0:T(1,128)S(1)} async-done(((f32[32,1,128]{2,1,0:T(1,128)}), f32[32,1,128]{2,1,0:T(1,128)S(1)}, u32[]{:S(2)}, u32[]{:S(2)}) %all-to-all-start) | async-done | bytes 16416 | tf_op jit(solution)/shard_map/all_to_all | solution.py:359
  16.9 0.3 shard_map.91
  17.2 0.1 collective-permute-start.2
  17.3 0.6 %collective-permute-start.3 = (f32[16,128]{1,0:T(8,128)S(1)}, f32[16,128]{1,0:T(8,128)S(1)}, u32[]{:S(2)}, u32[]{:S(2)}) collective-permute-start(f32[16,128]{1,0:T(8,128)S(1)} %get-tuple-element.48), channel_id=1, source_target_pairs={{0,2},{2,0},{4,6},{6,4},{8,10},{10,8},{12,14},{14,12},{16,18},{18,... | collective-permute-start | bytes 24584 | tf_op jit(solution)/shard_map/ppermute | solution.py:379
  17.9 0.6 %collective-permute-start.4 = (f32[16,128]{1,0:T(8,128)S(1)}, f32[16,128]{1,0:T(8,128)S(1)}, u32[]{:S(2)}, u32[]{:S(2)}) collective-permute-start(f32[16,128]{1,0:T(8,128)S(1)} %get-tuple-element.49), channel_id=1, source_target_pairs={{0,4},{2,6},{4,0},{6,2},{8,12},{10,14},{12,8},{14,10},{16,20},{18,... | collective-permute-start | bytes 24584 | tf_op jit(solution)/shard_map/ppermute | solution.py:379
  18.5 0.9 %collective-permute-start.5 = (f32[16,128]{1,0:T(8,128)S(1)}, f32[16,128]{1,0:T(8,128)S(1)}, u32[]{:S(2)}, u32[]{:S(2)}) collective-permute-start(f32[16,128]{1,0:T(8,128)S(1)} %get-tuple-element.50), channel_id=1, source_target_pairs={{0,8},{2,10},{4,12},{6,14},{8,0},{10,2},{12,4},{14,6},{16,24},{18,... | collective-permute-start | bytes 24584 | tf_op jit(solution)/shard_map/ppermute | solution.py:379
  19.4 0.0 collective-permute-done.2
  19.4 1.6 %shard_map.92 = (f32[64,128]{1,0:T(8,128)S(1)}, bf16[64,64,96]{2,1,0:T(8,128)(2,1)S(1)}, bf16[64,64,128]{2,1,0:T(8,128)(2,1)S(1)}) custom-call(f32[64,128]{1,0:T(8,128)S(1)} %get-tuple-element.46.vec.first, f32[1,64,128]{2,1,0:T(8,128)S(1)} %bitcast.39, s32[2,128]{1,0:T(2,128)S(1)} %bitcast.35, bf16[2,64,64,128]{3,2,1,0:T(8,128)(2,1)S(1)} %bitcast.26, ...), custom_call_target="tpu_custom_call" | custom-call | tf_op jit(solution)/shard_map/pallas_call | solution.py:23
  21.0 0.0 collective-permute-done.3.near0
  21.1 0.5 collective-permute-done.4.near1
  21.5 0.6 %collective-permute-done.5.near2 = f32[16,128]{1,0:T(8,128)S(1)} collective-permute-done((f32[16,128]{1,0:T(8,128)S(1)}, f32[16,128]{1,0:T(8,128)S(1)}, u32[]{:S(2)}, u32[]{:S(2)}) %collective-permute-start.5) | collective-permute-done | bytes 8224 | tf_op jit(solution)/shard_map/ppermute | solution.py:379
  22.2 1.1 %shard_map.93 = (f32[64,128]{1,0:T(8,128)S(1)}, f32[64,128]{1,0:T(8,128)S(1)}, f32[32,128]{1,0:T(8,128)}) custom-call(f32[64,128]{1,0:T(8,128)S(1)} %get-tuple-element.47.known, f32[16,128]{1,0:T(8,128)S(1)} %collective-permute-done.3.near0, f32[16,128]{1,0:T(8,128)S(1)} %collective-permute-done.4.near1, f32[16,128]{1,0:T(8,128)S(1)} %collective-permute-done.5.near2, ...), custom_call_target="tpu_custom_call" | custom-call | tf_op jit(solution)/shard_map/pallas_call | solution.py:23
  23.3 0.1 collective-permute-start.6
  23.4 0.3 shard_map.94.own
  23.7 3.2 %all-to-all-start.1 = ((f32[32,1,128]{2,1,0:T(1,128)}), f32[32,1,128]{2,1,0:T(1,128)S(1)}, u32[]{:S(2)}, u32[]{:S(2)}) async-start(f32[32,1,128]{2,1,0:T(1,128)} %bitcast.55), calls=%async_computation.1 | async-start | bytes 32768 | tf_op jit(solution)/shard_map/all_to_all | solution.py:359
  26.9 0.0 collective-permute-done.6
  26.9 0.8 %shard_map.95 = (f32[64,128]{1,0:T(8,128)S(1)}, bf16[64,64,128]{2,1,0:T(8,128)(2,1)S(1)}) custom-call(f32[64,128]{1,0:T(8,128)S(1)} %get-tuple-element.53.vec.state, f32[1,64,128]{2,1,0:T(8,128)S(1)} %bitcast.41, f32[64,128]{1,0:T(8,128)S(1)} %shard_map.94.own, f32[64,128]{1,0:T(8,128)S(1)} %get-tuple-element.54.resid.image, ...), custom_call_target="tpu_custom_call" | custom-call | tf_op jit(solution)/shard_map/pallas_call | solution.py:23
  27.7 0.3 collective-permute-start.7
  28.0 1.1 %shard_map.96 = (f32[64,128]{1,0:T(8,128)S(1)}, bf16[32,64,128]{2,1,0:T(8,128)(2,1)S(1)}, f32[32,512]{1,0:T(8,128)S(1)}) custom-call(f32[64,128]{1,0:T(8,128)S(1)} %get-tuple-element.55.vec.state, bf16[64,64,128]{2,1,0:T(8,128)(2,1)S(1)} %get-tuple-element.56.dblock, bf16[32,64,128]{2,1,0:T(8,128)(2,1)} %bitcast.53, f32[32,512]{1,0:T(8,128)} %refs_1_.3), custom_call_target="tpu_custom_call" | custom-call | flops 1073741824 | bytes 1073741824 | tf_op jit(solution)/shard_map/pallas_call | solution.py:23
  29.1 0.0 collective-permute-done.7
  29.1 0.8 %shard_map.97.state = f32[64,128]{1,0:T(8,128)S(1)} custom-call(f32[64,128]{1,0:T(8,128)S(1)} %get-tuple-element.55.vec.state, f32[1,64,128]{2,1,0:T(8,128)S(1)} %bitcast.43, f32[64,128]{1,0:T(8,128)S(1)} %get-tuple-element.57.own, f32[64,128]{1,0:T(8,128)S(1)} %get-tuple-element.54.resid.image, bf16[64,64,128]{2,1,0:T(8,128)(2,1)S(1)} %get-tuple-element.56.dblock, ...), custom_call_target="tpu_custom_call" | custom-call | tf_op jit(solution)/shard_map/pallas_call | solution.py:23
  29.9 4.1 %all-to-all-done.1 = f32[32,1,128]{2,1,0:T(1,128)S(1)} async-done(((f32[32,1,128]{2,1,0:T(1,128)}), f32[32,1,128]{2,1,0:T(1,128)S(1)}, u32[]{:S(2)}, u32[]{:S(2)}) %all-to-all-start.1) | async-done | bytes 16416 | tf_op jit(solution)/shard_map/all_to_all | solution.py:359
  34.0 0.3 shard_map.98
  34.3 0.1 collective-permute-start.8
  34.4 0.6 %collective-permute-start.9 = (f32[16,128]{1,0:T(8,128)S(1)}, f32[16,128]{1,0:T(8,128)S(1)}, u32[]{:S(2)}, u32[]{:S(2)}) collective-permute-start(f32[16,128]{1,0:T(8,128)S(1)} %get-tuple-element.63), channel_id=1, source_target_pairs={{0,2},{2,0},{4,6},{6,4},{8,10},{10,8},{12,14},{14,12},{16,18},{18,... | collective-permute-start | bytes 24584 | tf_op jit(solution)/shard_map/ppermute | solution.py:379
  35.0 0.6 %collective-permute-start.10 = (f32[16,128]{1,0:T(8,128)S(1)}, f32[16,128]{1,0:T(8,128)S(1)}, u32[]{:S(2)}, u32[]{:S(2)}) collective-permute-start(f32[16,128]{1,0:T(8,128)S(1)} %get-tuple-element.64), channel_id=1, source_target_pairs={{0,4},{2,6},{4,0},{6,2},{8,12},{10,14},{12,8},{14,10},{16,20},{18,... | collective-permute-start | bytes 24584 | tf_op jit(solution)/shard_map/ppermute | solution.py:379
  35.6 0.6 %collective-permute-start.11 = (f32[16,128]{1,0:T(8,128)S(1)}, f32[16,128]{1,0:T(8,128)S(1)}, u32[]{:S(2)}, u32[]{:S(2)}) collective-permute-start(f32[16,128]{1,0:T(8,128)S(1)} %get-tuple-element.65), channel_id=1, source_target_pairs={{0,8},{2,10},{4,12},{6,14},{8,0},{10,2},{12,4},{14,6},{16,24},{18,... | collective-permute-start | bytes 24584 | tf_op jit(solution)/shard_map/ppermute | solution.py:379
  36.2 0.0 collective-permute-done.8
  36.2 1.6 %shard_map.99 = (f32[64,128]{1,0:T(8,128)S(1)}, bf16[64,64,96]{2,1,0:T(8,128)(2,1)S(1)}, bf16[64,64,128]{2,1,0:T(8,128)(2,1)S(1)}) custom-call(f32[64,128]{1,0:T(8,128)S(1)} %get-tuple-element.61.vec.second, f32[1,64,128]{2,1,0:T(8,128)S(1)} %bitcast.40, s32[2,128]{1,0:T(2,128)S(1)} %bitcast.38, bf16[2,64,64,128]{3,2,1,0:T(8,128)(2,1)S(1)} %bitcast.29, ...), custom_call_target="tpu_custom_call" | custom-call | tf_op jit(solution)/shard_map/pallas_call | solution.py:23
  37.7 0.3 collective-permute-done.9.near0
  38.1 0.5 %collective-permute-done.10.near1 = f32[16,128]{1,0:T(8,128)S(1)} collective-permute-done((f32[16,128]{1,0:T(8,128)S(1)}, f32[16,128]{1,0:T(8,128)S(1)}, u32[]{:S(2)}, u32[]{:S(2)}) %collective-permute-start.10) | collective-permute-done | bytes 8224 | tf_op jit(solution)/shard_map/ppermute | solution.py:379
  38.6 0.6 %collective-permute-done.11.near2 = f32[16,128]{1,0:T(8,128)S(1)} collective-permute-done((f32[16,128]{1,0:T(8,128)S(1)}, f32[16,128]{1,0:T(8,128)S(1)}, u32[]{:S(2)}, u32[]{:S(2)}) %collective-permute-start.11) | collective-permute-done | bytes 8224 | tf_op jit(solution)/shard_map/ppermute | solution.py:379
  39.2 0.4 shard_map.100
  39.6 9.7 %all_to_all.33 = f32[32,1,128]{2,1,0:T(1,128)S(1)} all-to-all(f32[32,1,128]{2,1,0:T(1,128)S(1)} %bitcast.45), channel_id=1, replica_groups=mesh['sub'=16,'coarse'=2] {'sub','coarse'}, dimensions={0} | all-to-all | bytes 32768 | tf_op jit(solution)/shard_map/all_to_all | solution.py:359
  49.3 0.8 %shard_map.101 = (f32[1,64,128]{2,1,0:T(8,128)}, f32[1,64,128]{2,1,0:T(8,128)}) custom-call(f32[32,128]{1,0:T(8,128)S(1)} %bitcast.32, f32[8,128]{1,0:T(8,128)S(1)} %get-tuple-element.70.alpha, f32[64,128]{1,0:T(8,128)S(1)} %get-tuple-element.46.vec.first, f32[64,128]{1,0:T(8,128)S(1)} %get-tuple-element.61.vec.second, ...), custom_call_target="tpu_custom_call" | custom-call | tf_op jit(solution)/shard_map/pallas_call | solution.py:414
  (5 shorter events, 0.0 us)
Async XLA Ops:
  2.5 8.6 %copy-start = (bf16[1,2,64,64,128]{4,3,2,1,0:T(8,128)(2,1)S(1)}, bf16[1,2,64,64,128]{4,3,2,1,0:T(8,128)(2,1)}, u32[]{:S(2)}) copy-start(bf16[1,2,64,64,128]{4,3,2,1,0:T(8,128)(2,1)} %param.8) | copy-start | bytes 6291460
  2.5 8.6 %copy-start.3 = (s32[1,2,128]{2,1,0:T(2,128)S(1)}, s32[1,2,128]{2,1,0:T(2,128)}, u32[]{:S(2)}) copy-start(s32[1,2,128]{2,1,0:T(2,128)} %param.11) | copy-start | bytes 3076
  2.6 14.4 %all-to-all-start = ((f32[32,1,128]{2,1,0:T(1,128)}), f32[32,1,128]{2,1,0:T(1,128)S(1)}, u32[]{:S(2)}, u32[]{:S(2)}) async-start(f32[32,1,128]{2,1,0:T(1,128)} %bitcast.56), calls=%async_computation | async-start | bytes 32768 | tf_op jit(solution)/shard_map/all_to_all | solution.py:359
  9.9 1.3 %collective-permute-start = (f32[64,128]{1,0:T(8,128)S(1)}, f32[64,128]{1,0:T(8,128)S(1)}, u32[]{:S(2)}, u32[]{:S(2)}) collective-permute-start(f32[64,128]{1,0:T(8,128)S(1)} %get-tuple-element.37.vec.state), channel_id=1, source_target_pairs={{0,1},{1,0},{2,3},{3,2},{4,5},{5,4},{6,7},{7,6},{8,9},{9,8},{10,11... | collective-permute-start | bytes 98312 | tf_op jit(solution)/shard_map/ppermute | solution.py:341
  11.9 1.4 %collective-permute-start.1 = (f32[64,128]{1,0:T(8,128)S(1)}, f32[64,128]{1,0:T(8,128)S(1)}, u32[]{:S(2)}, u32[]{:S(2)}) collective-permute-start(f32[64,128]{1,0:T(8,128)S(1)} %get-tuple-element.40.vec.state), channel_id=1, source_target_pairs={{0,1},{1,0},{2,3},{3,2},{4,5},{5,4},{6,7},{7,6},{8,9},{9,8},{10,11... | collective-permute-start | bytes 98312 | tf_op jit(solution)/shard_map/ppermute | solution.py:341
  13.3 6.1 %copy-start.1 = (bf16[32,64,128]{2,1,0:T(8,128)(2,1)}, bf16[32,64,128]{2,1,0:T(8,128)(2,1)S(1)}, u32[]{:S(2)}) copy-start(bf16[32,64,128]{2,1,0:T(8,128)(2,1)S(1)} %get-tuple-element.44.zvec) | copy-start | bytes 1572868
  17.2 2.2 %collective-permute-start.2 = (f32[64,128]{1,0:T(8,128)S(1)}, f32[64,128]{1,0:T(8,128)S(1)}, u32[]{:S(2)}, u32[]{:S(2)}) collective-permute-start(f32[64,128]{1,0:T(8,128)S(1)} %get-tuple-element.46.vec.first), channel_id=1, source_target_pairs={{0,1},{1,0},{2,3},{3,2},{4,5},{5,4},{6,7},{7,6},{8,9},{9,8},{10,11... | collective-permute-start | bytes 98312 | tf_op jit(solution)/shard_map/ppermute | solution.py:341
  17.3 3.7 %collective-permute-start.3 = (f32[16,128]{1,0:T(8,128)S(1)}, f32[16,128]{1,0:T(8,128)S(1)}, u32[]{:S(2)}, u32[]{:S(2)}) collective-permute-start(f32[16,128]{1,0:T(8,128)S(1)} %get-tuple-element.48), channel_id=1, source_target_pairs={{0,2},{2,0},{4,6},{6,4},{8,10},{10,8},{12,14},{14,12},{16,18},{18,... | collective-permute-start | bytes 24584 | tf_op jit(solution)/shard_map/ppermute | solution.py:379
  17.9 3.7 %collective-permute-start.4 = (f32[16,128]{1,0:T(8,128)S(1)}, f32[16,128]{1,0:T(8,128)S(1)}, u32[]{:S(2)}, u32[]{:S(2)}) collective-permute-start(f32[16,128]{1,0:T(8,128)S(1)} %get-tuple-element.49), channel_id=1, source_target_pairs={{0,4},{2,6},{4,0},{6,2},{8,12},{10,14},{12,8},{14,10},{16,20},{18,... | collective-permute-start | bytes 24584 | tf_op jit(solution)/shard_map/ppermute | solution.py:379
  18.5 3.7 %collective-permute-start.5 = (f32[16,128]{1,0:T(8,128)S(1)}, f32[16,128]{1,0:T(8,128)S(1)}, u32[]{:S(2)}, u32[]{:S(2)}) collective-permute-start(f32[16,128]{1,0:T(8,128)S(1)} %get-tuple-element.50), channel_id=1, source_target_pairs={{0,8},{2,10},{4,12},{6,14},{8,0},{10,2},{12,4},{14,6},{16,24},{18,... | collective-permute-start | bytes 24584 | tf_op jit(solution)/shard_map/ppermute | solution.py:379
  19.4 2.8 %copy-start.2 = (bf16[32,64,128]{2,1,0:T(8,128)(2,1)S(1)}, bf16[32,64,128]{2,1,0:T(8,128)(2,1)}, u32[]{:S(2)}) copy-start(bf16[32,64,128]{2,1,0:T(8,128)(2,1)} %copy-done.1) | copy-start | bytes 1572868
  23.3 3.6 %collective-permute-start.6 = (f32[64,128]{1,0:T(8,128)S(1)}, f32[64,128]{1,0:T(8,128)S(1)}, u32[]{:S(2)}, u32[]{:S(2)}) collective-permute-start(f32[64,128]{1,0:T(8,128)S(1)} %get-tuple-element.53.vec.state), channel_id=1, source_target_pairs={{0,1},{1,0},{2,3},{3,2},{4,5},{5,4},{6,7},{7,6},{8,9},{9,8},{10,11... | collective-permute-start | bytes 98312 | tf_op jit(solution)/shard_map/ppermute | solution.py:341
  23.7 10.3 %all-to-all-start.1 = ((f32[32,1,128]{2,1,0:T(1,128)}), f32[32,1,128]{2,1,0:T(1,128)S(1)}, u32[]{:S(2)}, u32[]{:S(2)}) async-start(f32[32,1,128]{2,1,0:T(1,128)} %bitcast.55), calls=%async_computation.1 | async-start | bytes 32768 | tf_op jit(solution)/shard_map/all_to_all | solution.py:359
  27.7 1.4 %collective-permute-start.7 = (f32[64,128]{1,0:T(8,128)S(1)}, f32[64,128]{1,0:T(8,128)S(1)}, u32[]{:S(2)}, u32[]{:S(2)}) collective-permute-start(f32[64,128]{1,0:T(8,128)S(1)} %get-tuple-element.55.vec.state), channel_id=1, source_target_pairs={{0,1},{1,0},{2,3},{3,2},{4,5},{5,4},{6,7},{7,6},{8,9},{9,8},{10,11... | collective-permute-start | bytes 98312 | tf_op jit(solution)/shard_map/ppermute | solution.py:341
  34.3 1.9 %collective-permute-start.8 = (f32[64,128]{1,0:T(8,128)S(1)}, f32[64,128]{1,0:T(8,128)S(1)}, u32[]{:S(2)}, u32[]{:S(2)}) collective-permute-start(f32[64,128]{1,0:T(8,128)S(1)} %get-tuple-element.61.vec.second), channel_id=1, source_target_pairs={{0,1},{1,0},{2,3},{3,2},{4,5},{5,4},{6,7},{7,6},{8,9},{9,8},{10,11... | collective-permute-start | bytes 98312 | tf_op jit(solution)/shard_map/ppermute | solution.py:341
  34.4 3.7 %collective-permute-start.9 = (f32[16,128]{1,0:T(8,128)S(1)}, f32[16,128]{1,0:T(8,128)S(1)}, u32[]{:S(2)}, u32[]{:S(2)}) collective-permute-start(f32[16,128]{1,0:T(8,128)S(1)} %get-tuple-element.63), channel_id=1, source_target_pairs={{0,2},{2,0},{4,6},{6,4},{8,10},{10,8},{12,14},{14,12},{16,18},{18,... | collective-permute-start | bytes 24584 | tf_op jit(solution)/shard_map/ppermute | solution.py:379
  35.0 3.7 %collective-permute-start.10 = (f32[16,128]{1,0:T(8,128)S(1)}, f32[16,128]{1,0:T(8,128)S(1)}, u32[]{:S(2)}, u32[]{:S(2)}) collective-permute-start(f32[16,128]{1,0:T(8,128)S(1)} %get-tuple-element.64), channel_id=1, source_target_pairs={{0,4},{2,6},{4,0},{6,2},{8,12},{10,14},{12,8},{14,10},{16,20},{18,... | collective-permute-start | bytes 24584 | tf_op jit(solution)/shard_map/ppermute | solution.py:379
  35.6 3.7 %collective-permute-start.11 = (f32[16,128]{1,0:T(8,128)S(1)}, f32[16,128]{1,0:T(8,128)S(1)}, u32[]{:S(2)}, u32[]{:S(2)}) collective-permute-start(f32[16,128]{1,0:T(8,128)S(1)} %get-tuple-element.65), channel_id=1, source_target_pairs={{0,8},{2,10},{4,12},{6,14},{8,0},{10,2},{12,4},{14,6},{16,24},{18,... | collective-permute-start | bytes 24584 | tf_op jit(solution)/shard_map/ppermute | solution.py:379

commit v4 on v3

--- a/solution.py
+++ b/solution.py
@@ -298,7 +298,7 @@
     return jnp.concatenate(pieces, axis=0)
 
 
-def image_kernel(known, near0, near1, near2, fblock, resid, zvec, dblock, image, state, message_far, scratch, message, done):
+def image_kernel(known, near0, near1, near2, fblock, resid, zvec, dblock, image, state, own, message_far, scratch, message, done):
     with_interface(known, near_lanes((near0, near1, near2), known.shape[0]), fblock, image)
     value = image[...]
     block_product(zvec, value, scratch)
@@ -306,6 +306,7 @@
     post(message, scratch)
     copies = start_all((message,), (message_far,), done)
     relaxed(dblock, image, state)
+    block_product(dblock, state[...], own)
     wait_all(copies)
 
 
@@ -364,9 +365,10 @@
     def diag(vec, dblock, far=(), cost=0):
         return kernel(diag_kernel, [flat, *map(like, far)], [vec, dblock], far, [sems(max(len(far), 1))], cost)
 
-    def smooth(state, resid, dblock, lblocks, cols, cost=0):
+    def smooth(state, resid, dblock, lblocks, cols, own=None):
         others = gathered(state, count)
-        (own,) = diag(state, dblock, (), cost)
+        if own is None:
+            (own,) = diag(state, dblock, (), BESIDE)
         state, dblock = sweep(state, others, own, resid, dblock, lblocks, cols, copy=True)
         for at in range(SWEEPS - 2):
             others = gathered(state, count)
@@ -392,17 +394,17 @@
     )
     arrived = everywhere(message)
     lblocks, cols = lfar, cfar
-    state, held = smooth(state, resid, dblock, lblocks, cols, BESIDE)
+    state, held = smooth(state, resid, dblock, lblocks, cols)
     packed = [vmem((shape[0] * ffar.shape[2] // (BITS * lanes), lanes))] * BITS
     first, *parts = kernel(
         functools.partial(direction_kernel, count), [flat, *packed], [state, arrived, *held]
     )
     terms, dblock = apply(first, parts, lblocks, cols)
-    first_image, state, message = kernel(
-        image_kernel, [flat, flat, parcel_far], [*terms, resid, held[0], dblock], [], [small, parcel, sems(1)]
+    first_image, state, own, message = kernel(
+        image_kernel, [flat, flat, flat, parcel_far], [*terms, resid, held[0], dblock], [], [small, parcel, sems(1)]
     )
     arrived = everywhere(message)
-    state, held = smooth(state, first_image, dblock, lblocks, cols)
+    state, held = smooth(state, first_image, dblock, lblocks, cols, own)
     second, rest, alpha, *parts = kernel(
         functools.partial(next_direction_kernel, count),
         [flat, flat, vmem((ROWS, lanes)), *packed],

time: 50.4 us -> 50.2 us (level)
    pallas_call x15 -> x14, Pallas kernels: 12.9 us -> 12.6 us  [kernel(): pl.pallas_call(body, out_shape=outs, in_specs=[here] * len(near) + [there...]
  transfers between devices with their start and end apart: 14 -> 14, of which waited for: 8 -> 8; matrix products, arithmetic and copies ran while one was open for 0% -> 0% of each run, Pallas kernels for 18% -> 17%
where the time goes in v4:
time: 50.2 us; the launch traced here: 49.8 us
  starting transfers between devices  15.6 us (31%)
  Pallas kernels  13.4 us (27%)
  waiting for transfers between devices  10.3 us (21%)
  blocking collectives  9.67 us (19%)
  between operations  0.8 us (2%)
    pallas_call x14, Pallas kernels, kernel(): pl.pallas_call(body, out_shape=outs, in_specs=[here] * len(near) + [there...  12.6 us
    all_to_all x2, starting transfers between devices, everywhere(): return lax.all_to_all(message, ('sub', 'coarse'), 0, 0, tiled=True)  10.5 us
    all_to_all x1, blocking collectives, everywhere(): return lax.all_to_all(message, ('sub', 'coarse'), 0, 0, tiled=True)  9.67 us
    all_to_all x2, waiting for transfers between devices, everywhere(): return lax.all_to_all(message, ('sub', 'coarse'), 0, 0, tiled=True)  6.99 us
    ppermute x6, starting transfers between devices, apply(): lax.ppermute(part, 'sub', swap(subs, 1 << bit))  3.91 us
    ppermute x6, waiting for transfers between devices, apply(): lax.ppermute(part, 'sub', swap(subs, 1 << bit))  2.63 us
    ppermute x6, starting transfers between devices, gathered(): return lax.ppermute(array, 'coarse', swap(2, 1))[None]  1.16 us
  transfers between devices with their start and end apart: 14, of which 8 were waited for; matrix products, arithmetic and copies ran while one was open for 0% of the time, Pallas kernels for 17%

profile of v4, /device:TPU:0, one launch (start us, length us, event | category | flops | bytes accessed | tf_op | source)
XLA Modules:
  0.0 49.8 jit_solution(11940741743808252668)
XLA Ops:
  0.6 1.9 %shard_map.86 = (f32[64,128]{1,0:T(8,128)S(1)}, bf16[64,64,128]{2,1,0:T(8,128)(2,1)S(1)}, f32[64,128]{1,0:T(8,128)S(1)}, f32[32,128]{1,0:T(8,128)}) custom-call(f32[64,128]{1,0:T(8,128)} %bitcast.54, bf16[32,64,128]{2,1,0:T(8,128)(2,1)} %bitcast.51, bf16[64,64,128]{2,1,0:T(8,128)(2,1)} %bitcast.46), custom_call_target="tpu_custom_call" | custom-call | tf_op jit(solution)/shard_map/pallas_call | solution.py:23
  2.5 0.0 copy-start
  2.5 0.0 copy-start.3
  2.6 7.3 %all-to-all-start = ((f32[32,1,128]{2,1,0:T(1,128)}), f32[32,1,128]{2,1,0:T(1,128)S(1)}, u32[]{:S(2)}, u32[]{:S(2)}) async-start(f32[32,1,128]{2,1,0:T(1,128)} %bitcast.56), calls=%async_computation | async-start | bytes 32768 | tf_op jit(solution)/shard_map/all_to_all | solution.py:360
  9.9 0.3 collective-permute-start
  10.2 0.2 shard_map.87.own
  10.4 0.7 %collective-permute-done = f32[64,128]{1,0:T(8,128)S(1)} collective-permute-done((f32[64,128]{1,0:T(8,128)S(1)}, f32[64,128]{1,0:T(8,128)S(1)}, u32[]{:S(2)}, u32[]{:S(2)}) %collective-permute-start) | collective-permute-done | bytes 32800 | tf_op jit(solution)/shard_map/ppermute | solution.py:342
  11.1 0.0 copy-done.3
  11.2 0.8 %shard_map.88 = (f32[64,128]{1,0:T(8,128)S(1)}, bf16[64,64,128]{2,1,0:T(8,128)(2,1)S(1)}) custom-call(f32[64,128]{1,0:T(8,128)S(1)} %get-tuple-element.38.vec.state, f32[1,64,128]{2,1,0:T(8,128)S(1)} %bitcast.44, f32[64,128]{1,0:T(8,128)S(1)} %shard_map.87.own, f32[64,128]{1,0:T(8,128)S(1)} %get-tuple-element.40.resid, ...), custom_call_target="tpu_custom_call" | custom-call | tf_op jit(solution)/shard_map/pallas_call | solution.py:23
  11.9 0.3 collective-permute-start.1
  12.2 1.1 %shard_map.89 = (f32[64,128]{1,0:T(8,128)S(1)}, bf16[32,64,128]{2,1,0:T(8,128)(2,1)S(1)}, f32[32,512]{1,0:T(8,128)S(1)}) custom-call(f32[64,128]{1,0:T(8,128)S(1)} %get-tuple-element.41.vec.state, bf16[64,64,128]{2,1,0:T(8,128)(2,1)S(1)} %get-tuple-element.42.dblock, bf16[32,64,128]{2,1,0:T(8,128)(2,1)} %bitcast.52, f32[32,512]{1,0:T(8,128)} %refs_1_.3), custom_call_target="tpu_custom_call" | custom-call | flops 1073741824 | bytes 1073741824 | tf_op jit(solution)/shard_map/pallas_call | solution.py:23
  13.3 0.0 collective-permute-done.1
  13.3 0.8 %shard_map.90.state = f32[64,128]{1,0:T(8,128)S(1)} custom-call(f32[64,128]{1,0:T(8,128)S(1)} %get-tuple-element.41.vec.state, f32[1,64,128]{2,1,0:T(8,128)S(1)} %bitcast.42, f32[64,128]{1,0:T(8,128)S(1)} %get-tuple-element.43.own, f32[64,128]{1,0:T(8,128)S(1)} %get-tuple-element.40.resid, bf16[64,64,128]{2,1,0:T(8,128)(2,1)S(1)} %get-tuple-element.42.dblock, ...), custom_call_target="tpu_custom_call" | custom-call | tf_op jit(solution)/shard_map/pallas_call | solution.py:23
  14.1 2.9 %all-to-all-done = f32[32,1,128]{2,1,0:T(1,128)S(1)} async-done(((f32[32,1,128]{2,1,0:T(1,128)}), f32[32,1,128]{2,1,0:T(1,128)S(1)}, u32[]{:S(2)}, u32[]{:S(2)}) %all-to-all-start) | async-done | bytes 16416 | tf_op jit(solution)/shard_map/all_to_all | solution.py:360
  16.9 0.3 shard_map.91
  17.2 0.1 collective-permute-start.2
  17.3 0.6 %collective-permute-start.3 = (f32[16,128]{1,0:T(8,128)S(1)}, f32[16,128]{1,0:T(8,128)S(1)}, u32[]{:S(2)}, u32[]{:S(2)}) collective-permute-start(f32[16,128]{1,0:T(8,128)S(1)} %get-tuple-element.49), channel_id=1, source_target_pairs={{0,2},{2,0},{4,6},{6,4},{8,10},{10,8},{12,14},{14,12},{16,18},{18,... | collective-permute-start | bytes 24584 | tf_op jit(solution)/shard_map/ppermute | solution.py:381
  17.9 0.6 %collective-permute-start.4 = (f32[16,128]{1,0:T(8,128)S(1)}, f32[16,128]{1,0:T(8,128)S(1)}, u32[]{:S(2)}, u32[]{:S(2)}) collective-permute-start(f32[16,128]{1,0:T(8,128)S(1)} %get-tuple-element.50), channel_id=1, source_target_pairs={{0,4},{2,6},{4,0},{6,2},{8,12},{10,14},{12,8},{14,10},{16,20},{18,... | collective-permute-start | bytes 24584 | tf_op jit(solution)/shard_map/ppermute | solution.py:381
  18.5 0.9 %collective-permute-start.5 = (f32[16,128]{1,0:T(8,128)S(1)}, f32[16,128]{1,0:T(8,128)S(1)}, u32[]{:S(2)}, u32[]{:S(2)}) collective-permute-start(f32[16,128]{1,0:T(8,128)S(1)} %get-tuple-element.51), channel_id=1, source_target_pairs={{0,8},{2,10},{4,12},{6,14},{8,0},{10,2},{12,4},{14,6},{16,24},{18,... | collective-permute-start | bytes 24584 | tf_op jit(solution)/shard_map/ppermute | solution.py:381
  19.4 0.0 collective-permute-done.2
  19.4 0.0 copy-done.1
  19.4 1.6 %shard_map.92 = (f32[64,128]{1,0:T(8,128)S(1)}, bf16[64,64,96]{2,1,0:T(8,128)(2,1)S(1)}, bf16[64,64,128]{2,1,0:T(8,128)(2,1)S(1)}) custom-call(f32[64,128]{1,0:T(8,128)S(1)} %get-tuple-element.47.vec.first, f32[1,64,128]{2,1,0:T(8,128)S(1)} %bitcast.39, s32[2,128]{1,0:T(2,128)S(1)} %bitcast.35, bf16[2,64,64,128]{3,2,1,0:T(8,128)(2,1)S(1)} %bitcast.26, ...), custom_call_target="tpu_custom_call" | custom-call | tf_op jit(solution)/shard_map/pallas_call | solution.py:23
  21.0 0.0 collective-permute-done.3.near0
  21.1 0.5 %collective-permute-done.4.near1 = f32[16,128]{1,0:T(8,128)S(1)} collective-permute-done((f32[16,128]{1,0:T(8,128)S(1)}, f32[16,128]{1,0:T(8,128)S(1)}, u32[]{:S(2)}, u32[]{:S(2)}) %collective-permute-start.4) | collective-permute-done | bytes 8224 | tf_op jit(solution)/shard_map/ppermute | solution.py:381
  21.5 0.6 %collective-permute-done.5.near2 = f32[16,128]{1,0:T(8,128)S(1)} collective-permute-done((f32[16,128]{1,0:T(8,128)S(1)}, f32[16,128]{1,0:T(8,128)S(1)}, u32[]{:S(2)}, u32[]{:S(2)}) %collective-permute-start.5) | collective-permute-done | bytes 8224 | tf_op jit(solution)/shard_map/ppermute | solution.py:381
  22.2 1.1 %shard_map.93 = (f32[64,128]{1,0:T(8,128)S(1)}, f32[64,128]{1,0:T(8,128)S(1)}, f32[64,128]{1,0:T(8,128)S(1)}, f32[32,128]{1,0:T(8,128)}) custom-call(f32[64,128]{1,0:T(8,128)S(1)} %get-tuple-element.48.known, f32[16,128]{1,0:T(8,128)S(1)} %collective-permute-done.3.near0, f32[16,128]{1,0:T(8,128)S(1)} %collective-permute-done.4.near1, ...), custom_call_target="tpu_custom_call" | custom-call | tf_op jit(solution)/shard_map/pallas_call | solution.py:23
  23.3 0.1 collective-permute-start.6
  23.4 3.2 %all-to-all-start.1 = ((f32[32,1,128]{2,1,0:T(1,128)}), f32[32,1,128]{2,1,0:T(1,128)S(1)}, u32[]{:S(2)}, u32[]{:S(2)}) async-start(f32[32,1,128]{2,1,0:T(1,128)} %bitcast.55), calls=%async_computation.1 | async-start | bytes 32768 | tf_op jit(solution)/shard_map/all_to_all | solution.py:360
  26.6 0.0 collective-permute-done.6
  26.7 0.8 %shard_map.94 = (f32[64,128]{1,0:T(8,128)S(1)}, bf16[64,64,128]{2,1,0:T(8,128)(2,1)S(1)}) custom-call(f32[64,128]{1,0:T(8,128)S(1)} %get-tuple-element.54.state, f32[1,64,128]{2,1,0:T(8,128)S(1)} %bitcast.41, f32[64,128]{1,0:T(8,128)S(1)} %get-tuple-element.55.own, f32[64,128]{1,0:T(8,128)S(1)} %get-tuple-element.56.resid.image, ...), custom_call_target="tpu_custom_call" | custom-call | tf_op jit(solution)/shard_map/pallas_call | solution.py:23
  27.4 0.3 collective-permute-start.7
  27.7 1.1 %shard_map.95 = (f32[64,128]{1,0:T(8,128)S(1)}, bf16[32,64,128]{2,1,0:T(8,128)(2,1)S(1)}, f32[32,512]{1,0:T(8,128)S(1)}) custom-call(f32[64,128]{1,0:T(8,128)S(1)} %get-tuple-element.57.vec.state, bf16[64,64,128]{2,1,0:T(8,128)(2,1)S(1)} %get-tuple-element.58.dblock, bf16[32,64,128]{2,1,0:T(8,128)(2,1)} %bitcast.53, f32[32,512]{1,0:T(8,128)} %refs_1_.3), custom_call_target="tpu_custom_call" | custom-call | flops 1073741824 | bytes 1073741824 | tf_op jit(solution)/shard_map/pallas_call | solution.py:23
  28.8 0.0 collective-permute-done.7
  28.8 0.8 %shard_map.96.state = f32[64,128]{1,0:T(8,128)S(1)} custom-call(f32[64,128]{1,0:T(8,128)S(1)} %get-tuple-element.57.vec.state, f32[1,64,128]{2,1,0:T(8,128)S(1)} %bitcast.43, f32[64,128]{1,0:T(8,128)S(1)} %get-tuple-element.59.own, f32[64,128]{1,0:T(8,128)S(1)} %get-tuple-element.56.resid.image, bf16[64,64,128]{2,1,0:T(8,128)(2,1)S(1)} %get-tuple-element.58.dblock, ...), custom_call_target="tpu_custom_call" | custom-call | tf_op jit(solution)/shard_map/pallas_call | solution.py:23
  29.6 4.1 %all-to-all-done.1 = f32[32,1,128]{2,1,0:T(1,128)S(1)} async-done(((f32[32,1,128]{2,1,0:T(1,128)}), f32[32,1,128]{2,1,0:T(1,128)S(1)}, u32[]{:S(2)}, u32[]{:S(2)}) %all-to-all-start.1) | async-done | bytes 16416 | tf_op jit(solution)/shard_map/all_to_all | solution.py:360
  33.7 0.3 shard_map.97
  34.0 0.1 collective-permute-start.8
  34.1 0.6 %collective-permute-start.9 = (f32[16,128]{1,0:T(8,128)S(1)}, f32[16,128]{1,0:T(8,128)S(1)}, u32[]{:S(2)}, u32[]{:S(2)}) collective-permute-start(f32[16,128]{1,0:T(8,128)S(1)} %get-tuple-element.65), channel_id=1, source_target_pairs={{0,2},{2,0},{4,6},{6,4},{8,10},{10,8},{12,14},{14,12},{16,18},{18,... | collective-permute-start | bytes 24584 | tf_op jit(solution)/shard_map/ppermute | solution.py:381
  34.7 0.6 %collective-permute-start.10 = (f32[16,128]{1,0:T(8,128)S(1)}, f32[16,128]{1,0:T(8,128)S(1)}, u32[]{:S(2)}, u32[]{:S(2)}) collective-permute-start(f32[16,128]{1,0:T(8,128)S(1)} %get-tuple-element.66), channel_id=1, source_target_pairs={{0,4},{2,6},{4,0},{6,2},{8,12},{10,14},{12,8},{14,10},{16,20},{18,... | collective-permute-start | bytes 24584 | tf_op jit(solution)/shard_map/ppermute | solution.py:381
  35.3 0.6 %collective-permute-start.11 = (f32[16,128]{1,0:T(8,128)S(1)}, f32[16,128]{1,0:T(8,128)S(1)}, u32[]{:S(2)}, u32[]{:S(2)}) collective-permute-start(f32[16,128]{1,0:T(8,128)S(1)} %get-tuple-element.67), channel_id=1, source_target_pairs={{0,8},{2,10},{4,12},{6,14},{8,0},{10,2},{12,4},{14,6},{16,24},{18,... | collective-permute-start | bytes 24584 | tf_op jit(solution)/shard_map/ppermute | solution.py:381
  35.9 0.0 collective-permute-done.8
  35.9 1.6 %shard_map.98 = (f32[64,128]{1,0:T(8,128)S(1)}, bf16[64,64,96]{2,1,0:T(8,128)(2,1)S(1)}, bf16[64,64,128]{2,1,0:T(8,128)(2,1)S(1)}) custom-call(f32[64,128]{1,0:T(8,128)S(1)} %get-tuple-element.63.vec.second, f32[1,64,128]{2,1,0:T(8,128)S(1)} %bitcast.40, s32[2,128]{1,0:T(2,128)S(1)} %bitcast.38, bf16[2,64,64,128]{3,2,1,0:T(8,128)(2,1)S(1)} %bitcast.29, ...), custom_call_target="tpu_custom_call" | custom-call | tf_op jit(solution)/shard_map/pallas_call | solution.py:23
  37.5 0.3 collective-permute-done.9.near0
  37.8 0.5 %collective-permute-done.10.near1 = f32[16,128]{1,0:T(8,128)S(1)} collective-permute-done((f32[16,128]{1,0:T(8,128)S(1)}, f32[16,128]{1,0:T(8,128)S(1)}, u32[]{:S(2)}, u32[]{:S(2)}) %collective-permute-start.10) | collective-permute-done | bytes 8224 | tf_op jit(solution)/shard_map/ppermute | solution.py:381
  38.3 0.6 %collective-permute-done.11.near2 = f32[16,128]{1,0:T(8,128)S(1)} collective-permute-done((f32[16,128]{1,0:T(8,128)S(1)}, f32[16,128]{1,0:T(8,128)S(1)}, u32[]{:S(2)}, u32[]{:S(2)}) %collective-permute-start.11) | collective-permute-done | bytes 8224 | tf_op jit(solution)/shard_map/ppermute | solution.py:381
  39.0 0.4 shard_map.99
  39.4 9.7 %all_to_all.33 = f32[32,1,128]{2,1,0:T(1,128)S(1)} all-to-all(f32[32,1,128]{2,1,0:T(1,128)S(1)} %bitcast.45), channel_id=1, replica_groups=mesh['sub'=16,'coarse'=2] {'sub','coarse'}, dimensions={0} | all-to-all | bytes 32768 | tf_op jit(solution)/shard_map/all_to_all | solution.py:360
  49.0 0.8 %shard_map.100 = (f32[1,64,128]{2,1,0:T(8,128)}, f32[1,64,128]{2,1,0:T(8,128)}) custom-call(f32[32,128]{1,0:T(8,128)S(1)} %bitcast.32, f32[8,128]{1,0:T(8,128)S(1)} %get-tuple-element.72.alpha, f32[64,128]{1,0:T(8,128)S(1)} %get-tuple-element.47.vec.first, f32[64,128]{1,0:T(8,128)S(1)} %get-tuple-element.63.vec.second, ...), custom_call_target="tpu_custom_call" | custom-call | tf_op jit(solution)/shard_map/pallas_call | solution.py:416
  (4 shorter events, 0.0 us)
Async XLA Ops:
  2.5 8.6 %copy-start = (bf16[1,2,64,64,128]{4,3,2,1,0:T(8,128)(2,1)S(1)}, bf16[1,2,64,64,128]{4,3,2,1,0:T(8,128)(2,1)}, u32[]{:S(2)}) copy-start(bf16[1,2,64,64,128]{4,3,2,1,0:T(8,128)(2,1)} %param.8) | copy-start | bytes 6291460
  2.5 8.6 %copy-start.3 = (s32[1,2,128]{2,1,0:T(2,128)S(1)}, s32[1,2,128]{2,1,0:T(2,128)}, u32[]{:S(2)}) copy-start(s32[1,2,128]{2,1,0:T(2,128)} %param.11) | copy-start | bytes 3076
  2.6 14.4 %all-to-all-start = ((f32[32,1,128]{2,1,0:T(1,128)}), f32[32,1,128]{2,1,0:T(1,128)S(1)}, u32[]{:S(2)}, u32[]{:S(2)}) async-start(f32[32,1,128]{2,1,0:T(1,128)} %bitcast.56), calls=%async_computation | async-start | bytes 32768 | tf_op jit(solution)/shard_map/all_to_all | solution.py:360
  9.9 1.3 %collective-permute-start = (f32[64,128]{1,0:T(8,128)S(1)}, f32[64,128]{1,0:T(8,128)S(1)}, u32[]{:S(2)}, u32[]{:S(2)}) collective-permute-start(f32[64,128]{1,0:T(8,128)S(1)} %get-tuple-element.38.vec.state), channel_id=1, source_target_pairs={{0,1},{1,0},{2,3},{3,2},{4,5},{5,4},{6,7},{7,6},{8,9},{9,8},{10,11... | collective-permute-start | bytes 98312 | tf_op jit(solution)/shard_map/ppermute | solution.py:342
  11.9 1.4 %collective-permute-start.1 = (f32[64,128]{1,0:T(8,128)S(1)}, f32[64,128]{1,0:T(8,128)S(1)}, u32[]{:S(2)}, u32[]{:S(2)}) collective-permute-start(f32[64,128]{1,0:T(8,128)S(1)} %get-tuple-element.41.vec.state), channel_id=1, source_target_pairs={{0,1},{1,0},{2,3},{3,2},{4,5},{5,4},{6,7},{7,6},{8,9},{9,8},{10,11... | collective-permute-start | bytes 98312 | tf_op jit(solution)/shard_map/ppermute | solution.py:342
  13.3 6.1 %copy-start.1 = (bf16[32,64,128]{2,1,0:T(8,128)(2,1)}, bf16[32,64,128]{2,1,0:T(8,128)(2,1)S(1)}, u32[]{:S(2)}) copy-start(bf16[32,64,128]{2,1,0:T(8,128)(2,1)S(1)} %get-tuple-element.45.zvec) | copy-start | bytes 1572868
  17.2 2.2 %collective-permute-start.2 = (f32[64,128]{1,0:T(8,128)S(1)}, f32[64,128]{1,0:T(8,128)S(1)}, u32[]{:S(2)}, u32[]{:S(2)}) collective-permute-start(f32[64,128]{1,0:T(8,128)S(1)} %get-tuple-element.47.vec.first), channel_id=1, source_target_pairs={{0,1},{1,0},{2,3},{3,2},{4,5},{5,4},{6,7},{7,6},{8,9},{9,8},{10,11... | collective-permute-start | bytes 98312 | tf_op jit(solution)/shard_map/ppermute | solution.py:342
  17.3 3.7 %collective-permute-start.3 = (f32[16,128]{1,0:T(8,128)S(1)}, f32[16,128]{1,0:T(8,128)S(1)}, u32[]{:S(2)}, u32[]{:S(2)}) collective-permute-start(f32[16,128]{1,0:T(8,128)S(1)} %get-tuple-element.49), channel_id=1, source_target_pairs={{0,2},{2,0},{4,6},{6,4},{8,10},{10,8},{12,14},{14,12},{16,18},{18,... | collective-permute-start | bytes 24584 | tf_op jit(solution)/shard_map/ppermute | solution.py:381
  17.9 3.7 %collective-permute-start.4 = (f32[16,128]{1,0:T(8,128)S(1)}, f32[16,128]{1,0:T(8,128)S(1)}, u32[]{:S(2)}, u32[]{:S(2)}) collective-permute-start(f32[16,128]{1,0:T(8,128)S(1)} %get-tuple-element.50), channel_id=1, source_target_pairs={{0,4},{2,6},{4,0},{6,2},{8,12},{10,14},{12,8},{14,10},{16,20},{18,... | collective-permute-start | bytes 24584 | tf_op jit(solution)/shard_map/ppermute | solution.py:381
  18.5 3.7 %collective-permute-start.5 = (f32[16,128]{1,0:T(8,128)S(1)}, f32[16,128]{1,0:T(8,128)S(1)}, u32[]{:S(2)}, u32[]{:S(2)}) collective-permute-start(f32[16,128]{1,0:T(8,128)S(1)} %get-tuple-element.51), channel_id=1, source_target_pairs={{0,8},{2,10},{4,12},{6,14},{8,0},{10,2},{12,4},{14,6},{16,24},{18,... | collective-permute-start | bytes 24584 | tf_op jit(solution)/shard_map/ppermute | solution.py:381
  19.4 2.8 %copy-start.2 = (bf16[32,64,128]{2,1,0:T(8,128)(2,1)S(1)}, bf16[32,64,128]{2,1,0:T(8,128)(2,1)}, u32[]{:S(2)}) copy-start(bf16[32,64,128]{2,1,0:T(8,128)(2,1)} %copy-done.1) | copy-start | bytes 1572868
  23.3 3.3 %collective-permute-start.6 = (f32[64,128]{1,0:T(8,128)S(1)}, f32[64,128]{1,0:T(8,128)S(1)}, u32[]{:S(2)}, u32[]{:S(2)}) collective-permute-start(f32[64,128]{1,0:T(8,128)S(1)} %get-tuple-element.54.state), channel_id=1, source_target_pairs={{0,1},{1,0},{2,3},{3,2},{4,5},{5,4},{6,7},{7,6},{8,9},{9,8},{10,11... | collective-permute-start | bytes 98312 | tf_op jit(solution)/shard_map/ppermute | solution.py:342
  23.4 10.3 %all-to-all-start.1 = ((f32[32,1,128]{2,1,0:T(1,128)}), f32[32,1,128]{2,1,0:T(1,128)S(1)}, u32[]{:S(2)}, u32[]{:S(2)}) async-start(f32[32,1,128]{2,1,0:T(1,128)} %bitcast.55), calls=%async_computation.1 | async-start | bytes 32768 | tf_op jit(solution)/shard_map/all_to_all | solution.py:360
  27.4 1.4 %collective-permute-start.7 = (f32[64,128]{1,0:T(8,128)S(1)}, f32[64,128]{1,0:T(8,128)S(1)}, u32[]{:S(2)}, u32[]{:S(2)}) collective-permute-start(f32[64,128]{1,0:T(8,128)S(1)} %get-tuple-element.57.vec.state), channel_id=1, source_target_pairs={{0,1},{1,0},{2,3},{3,2},{4,5},{5,4},{6,7},{7,6},{8,9},{9,8},{10,11... | collective-permute-start | bytes 98312 | tf_op jit(solution)/shard_map/ppermute | solution.py:342
  34.0 1.9 %collective-permute-start.8 = (f32[64,128]{1,0:T(8,128)S(1)}, f32[64,128]{1,0:T(8,128)S(1)}, u32[]{:S(2)}, u32[]{:S(2)}) collective-permute-start(f32[64,128]{1,0:T(8,128)S(1)} %get-tuple-element.63.vec.second), channel_id=1, source_target_pairs={{0,1},{1,0},{2,3},{3,2},{4,5},{5,4},{6,7},{7,6},{8,9},{9,8},{10,11... | collective-permute-start | bytes 98312 | tf_op jit(solution)/shard_map/ppermute | solution.py:342
  34.1 3.7 %collective-permute-start.9 = (f32[16,128]{1,0:T(8,128)S(1)}, f32[16,128]{1,0:T(8,128)S(1)}, u32[]{:S(2)}, u32[]{:S(2)}) collective-permute-start(f32[16,128]{1,0:T(8,128)S(1)} %get-tuple-element.65), channel_id=1, source_target_pairs={{0,2},{2,0},{4,6},{6,4},{8,10},{10,8},{12,14},{14,12},{16,18},{18,... | collective-permute-start | bytes 24584 | tf_op jit(solution)/shard_map/ppermute | solution.py:381
  34.7 3.7 %collective-permute-start.10 = (f32[16,128]{1,0:T(8,128)S(1)}, f32[16,128]{1,0:T(8,128)S(1)}, u32[]{:S(2)}, u32[]{:S(2)}) collective-permute-start(f32[16,128]{1,0:T(8,128)S(1)} %get-tuple-element.66), channel_id=1, source_target_pairs={{0,4},{2,6},{4,0},{6,2},{8,12},{10,14},{12,8},{14,10},{16,20},{18,... | collective-permute-start | bytes 24584 | tf_op jit(solution)/shard_map/ppermute | solution.py:381
  35.3 3.7 %collective-permute-start.11 = (f32[16,128]{1,0:T(8,128)S(1)}, f32[16,128]{1,0:T(8,128)S(1)}, u32[]{:S(2)}, u32[]{:S(2)}) collective-permute-start(f32[16,128]{1,0:T(8,128)S(1)} %get-tuple-element.67), channel_id=1, source_target_pairs={{0,8},{2,10},{4,12},{6,14},{8,0},{10,2},{12,4},{14,6},{16,24},{18,... | collective-permute-start | bytes 24584 | tf_op jit(solution)/shard_map/ppermute | solution.py:381

commit v5 on v4

--- a/solution.py
+++ b/solution.py
@@ -135,10 +135,10 @@
     sender = lax.broadcasted_iota(jnp.int32, arrived.shape, 0)
     groups = arrived.shape[1] // nvec
     values = jnp.where(lane // nvec == lax.rem(sender // count + 1, groups), arrived[...], 0.0)
-    place = lax.rem(lane, nvec)
-    cross = total(jnp.where(place == 0, values, 0.0))
-    square = total(jnp.where(place == 1, values, 0.0))
-    return cross / (square + 1e-06)
+    line = jnp.sum(values, axis=0, keepdims=True)
+    place = lax.rem(lane[:ROWS], nvec)
+    pair = jnp.sum(jnp.where(place == sender[:ROWS], line, 0.0), axis=1, keepdims=True)
+    return pair[0:1] / (pair[1:2] + 1e-06)
 
 
 def restriction_rows(arrived, nvec, count):

time: 50.2 us -> 50.1 us (level)
  no operation moved by 1% of the time
where the time goes in v5:
time: 50.1 us; the launch traced here: 49.8 us
  starting transfers between devices  15.6 us (31%)
  Pallas kernels  13.4 us (27%)
  waiting for transfers between devices  10.3 us (21%)
  blocking collectives  9.67 us (19%)
  between operations  0.8 us (2%)
    pallas_call x14, Pallas kernels, kernel(): pl.pallas_call(body, out_shape=outs, in_specs=[here] * len(near) + [there...  12.6 us
    all_to_all x2, starting transfers between devices, everywhere(): return lax.all_to_all(message, ('sub', 'coarse'), 0, 0, tiled=True)  10.5 us
    all_to_all x1, blocking collectives, everywhere(): return lax.all_to_all(message, ('sub', 'coarse'), 0, 0, tiled=True)  9.67 us
    all_to_all x2, waiting for transfers between devices, everywhere(): return lax.all_to_all(message, ('sub', 'coarse'), 0, 0, tiled=True)  6.99 us
    ppermute x6, starting transfers between devices, apply(): lax.ppermute(part, 'sub', swap(subs, 1 << bit))  3.91 us
    ppermute x6, waiting for transfers between devices, apply(): lax.ppermute(part, 'sub', swap(subs, 1 << bit))  2.63 us
    ppermute x6, starting transfers between devices, gathered(): return lax.ppermute(array, 'coarse', swap(2, 1))[None]  1.16 us
  transfers between devices with their start and end apart: 14, of which 8 were waited for; matrix products, arithmetic and copies ran while one was open for 0% of the time, Pallas kernels for 17%

profile of v5, /device:TPU:0, one launch (start us, length us, event | category | flops | bytes accessed | tf_op | source)
XLA Modules:
  0.0 49.8 jit_solution(4132651352371659608)
XLA Ops:
  0.6 1.9 %shard_map.86 = (f32[64,128]{1,0:T(8,128)S(1)}, bf16[64,64,128]{2,1,0:T(8,128)(2,1)S(1)}, f32[64,128]{1,0:T(8,128)S(1)}, f32[32,128]{1,0:T(8,128)}) custom-call(f32[64,128]{1,0:T(8,128)} %bitcast.54, bf16[32,64,128]{2,1,0:T(8,128)(2,1)} %bitcast.51, bf16[64,64,128]{2,1,0:T(8,128)(2,1)} %bitcast.46), custom_call_target="tpu_custom_call" | custom-call | tf_op jit(solution)/shard_map/pallas_call | solution.py:23
  2.5 0.0 copy-start
  2.5 0.0 copy-start.3
  2.6 7.3 %all-to-all-start = ((f32[32,1,128]{2,1,0:T(1,128)}), f32[32,1,128]{2,1,0:T(1,128)S(1)}, u32[]{:S(2)}, u32[]{:S(2)}) async-start(f32[32,1,128]{2,1,0:T(1,128)} %bitcast.56), calls=%async_computation | async-start | bytes 32768 | tf_op jit(solution)/shard_map/all_to_all | solution.py:360
  9.9 0.3 collective-permute-start
  10.2 0.2 shard_map.87.own
  10.4 0.7 %collective-permute-done = f32[64,128]{1,0:T(8,128)S(1)} collective-permute-done((f32[64,128]{1,0:T(8,128)S(1)}, f32[64,128]{1,0:T(8,128)S(1)}, u32[]{:S(2)}, u32[]{:S(2)}) %collective-permute-start) | collective-permute-done | bytes 32800 | tf_op jit(solution)/shard_map/ppermute | solution.py:342
  11.1 0.0 copy-done.3
  11.2 0.8 %shard_map.88 = (f32[64,128]{1,0:T(8,128)S(1)}, bf16[64,64,128]{2,1,0:T(8,128)(2,1)S(1)}) custom-call(f32[64,128]{1,0:T(8,128)S(1)} %get-tuple-element.38.vec.state, f32[1,64,128]{2,1,0:T(8,128)S(1)} %bitcast.44, f32[64,128]{1,0:T(8,128)S(1)} %shard_map.87.own, f32[64,128]{1,0:T(8,128)S(1)} %get-tuple-element.40.resid, ...), custom_call_target="tpu_custom_call" | custom-call | tf_op jit(solution)/shard_map/pallas_call | solution.py:23
  11.9 0.3 collective-permute-start.1
  12.2 1.1 %shard_map.89 = (f32[64,128]{1,0:T(8,128)S(1)}, bf16[32,64,128]{2,1,0:T(8,128)(2,1)S(1)}, f32[32,512]{1,0:T(8,128)S(1)}) custom-call(f32[64,128]{1,0:T(8,128)S(1)} %get-tuple-element.41.vec.state, bf16[64,64,128]{2,1,0:T(8,128)(2,1)S(1)} %get-tuple-element.42.dblock, bf16[32,64,128]{2,1,0:T(8,128)(2,1)} %bitcast.52, f32[32,512]{1,0:T(8,128)} %refs_1_.3), custom_call_target="tpu_custom_call" | custom-call | flops 1073741824 | bytes 1073741824 | tf_op jit(solution)/shard_map/pallas_call | solution.py:23
  13.3 0.0 collective-permute-done.1
  13.3 0.8 %shard_map.90.state = f32[64,128]{1,0:T(8,128)S(1)} custom-call(f32[64,128]{1,0:T(8,128)S(1)} %get-tuple-element.41.vec.state, f32[1,64,128]{2,1,0:T(8,128)S(1)} %bitcast.42, f32[64,128]{1,0:T(8,128)S(1)} %get-tuple-element.43.own, f32[64,128]{1,0:T(8,128)S(1)} %get-tuple-element.40.resid, bf16[64,64,128]{2,1,0:T(8,128)(2,1)S(1)} %get-tuple-element.42.dblock, ...), custom_call_target="tpu_custom_call" | custom-call | tf_op jit(solution)/shard_map/pallas_call | solution.py:23
  14.1 2.9 %all-to-all-done = f32[32,1,128]{2,1,0:T(1,128)S(1)} async-done(((f32[32,1,128]{2,1,0:T(1,128)}), f32[32,1,128]{2,1,0:T(1,128)S(1)}, u32[]{:S(2)}, u32[]{:S(2)}) %all-to-all-start) | async-done | bytes 16416 | tf_op jit(solution)/shard_map/all_to_all | solution.py:360
  16.9 0.3 shard_map.91
  17.2 0.1 collective-permute-start.2
  17.3 0.6 %collective-permute-start.3 = (f32[16,128]{1,0:T(8,128)S(1)}, f32[16,128]{1,0:T(8,128)S(1)}, u32[]{:S(2)}, u32[]{:S(2)}) collective-permute-start(f32[16,128]{1,0:T(8,128)S(1)} %get-tuple-element.49), channel_id=1, source_target_pairs={{0,2},{2,0},{4,6},{6,4},{8,10},{10,8},{12,14},{14,12},{16,18},{18,... | collective-permute-start | bytes 24584 | tf_op jit(solution)/shard_map/ppermute | solution.py:381
  17.9 0.6 %collective-permute-start.4 = (f32[16,128]{1,0:T(8,128)S(1)}, f32[16,128]{1,0:T(8,128)S(1)}, u32[]{:S(2)}, u32[]{:S(2)}) collective-permute-start(f32[16,128]{1,0:T(8,128)S(1)} %get-tuple-element.50), channel_id=1, source_target_pairs={{0,4},{2,6},{4,0},{6,2},{8,12},{10,14},{12,8},{14,10},{16,20},{18,... | collective-permute-start | bytes 24584 | tf_op jit(solution)/shard_map/ppermute | solution.py:381
  18.5 0.9 %collective-permute-start.5 = (f32[16,128]{1,0:T(8,128)S(1)}, f32[16,128]{1,0:T(8,128)S(1)}, u32[]{:S(2)}, u32[]{:S(2)}) collective-permute-start(f32[16,128]{1,0:T(8,128)S(1)} %get-tuple-element.51), channel_id=1, source_target_pairs={{0,8},{2,10},{4,12},{6,14},{8,0},{10,2},{12,4},{14,6},{16,24},{18,... | collective-permute-start | bytes 24584 | tf_op jit(solution)/shard_map/ppermute | solution.py:381
  19.4 0.0 collective-permute-done.2
  19.4 0.0 copy-done.1
  19.4 1.6 %shard_map.92 = (f32[64,128]{1,0:T(8,128)S(1)}, bf16[64,64,96]{2,1,0:T(8,128)(2,1)S(1)}, bf16[64,64,128]{2,1,0:T(8,128)(2,1)S(1)}) custom-call(f32[64,128]{1,0:T(8,128)S(1)} %get-tuple-element.47.vec.first, f32[1,64,128]{2,1,0:T(8,128)S(1)} %bitcast.39, s32[2,128]{1,0:T(2,128)S(1)} %bitcast.35, bf16[2,64,64,128]{3,2,1,0:T(8,128)(2,1)S(1)} %bitcast.26, ...), custom_call_target="tpu_custom_call" | custom-call | tf_op jit(solution)/shard_map/pallas_call | solution.py:23
  21.0 0.0 collective-permute-done.3.near0
  21.1 0.5 %collective-permute-done.4.near1 = f32[16,128]{1,0:T(8,128)S(1)} collective-permute-done((f32[16,128]{1,0:T(8,128)S(1)}, f32[16,128]{1,0:T(8,128)S(1)}, u32[]{:S(2)}, u32[]{:S(2)}) %collective-permute-start.4) | collective-permute-done | bytes 8224 | tf_op jit(solution)/shard_map/ppermute | solution.py:381
  21.5 0.6 %collective-permute-done.5.near2 = f32[16,128]{1,0:T(8,128)S(1)} collective-permute-done((f32[16,128]{1,0:T(8,128)S(1)}, f32[16,128]{1,0:T(8,128)S(1)}, u32[]{:S(2)}, u32[]{:S(2)}) %collective-permute-start.5) | collective-permute-done | bytes 8224 | tf_op jit(solution)/shard_map/ppermute | solution.py:381
  22.2 1.1 %shard_map.93 = (f32[64,128]{1,0:T(8,128)S(1)}, f32[64,128]{1,0:T(8,128)S(1)}, f32[64,128]{1,0:T(8,128)S(1)}, f32[32,128]{1,0:T(8,128)}) custom-call(f32[64,128]{1,0:T(8,128)S(1)} %get-tuple-element.48.known, f32[16,128]{1,0:T(8,128)S(1)} %collective-permute-done.3.near0, f32[16,128]{1,0:T(8,128)S(1)} %collective-permute-done.4.near1, ...), custom_call_target="tpu_custom_call" | custom-call | tf_op jit(solution)/shard_map/pallas_call | solution.py:23
  23.3 0.1 collective-permute-start.6
  23.4 3.2 %all-to-all-start.1 = ((f32[32,1,128]{2,1,0:T(1,128)}), f32[32,1,128]{2,1,0:T(1,128)S(1)}, u32[]{:S(2)}, u32[]{:S(2)}) async-start(f32[32,1,128]{2,1,0:T(1,128)} %bitcast.55), calls=%async_computation.1 | async-start | bytes 32768 | tf_op jit(solution)/shard_map/all_to_all | solution.py:360
  26.6 0.0 collective-permute-done.6
  26.7 0.8 %shard_map.94 = (f32[64,128]{1,0:T(8,128)S(1)}, bf16[64,64,128]{2,1,0:T(8,128)(2,1)S(1)}) custom-call(f32[64,128]{1,0:T(8,128)S(1)} %get-tuple-element.54.state, f32[1,64,128]{2,1,0:T(8,128)S(1)} %bitcast.41, f32[64,128]{1,0:T(8,128)S(1)} %get-tuple-element.55.own, f32[64,128]{1,0:T(8,128)S(1)} %get-tuple-element.56.resid.image, ...), custom_call_target="tpu_custom_call" | custom-call | tf_op jit(solution)/shard_map/pallas_call | solution.py:23
  27.4 0.3 collective-permute-start.7
  27.7 1.1 %shard_map.95 = (f32[64,128]{1,0:T(8,128)S(1)}, bf16[32,64,128]{2,1,0:T(8,128)(2,1)S(1)}, f32[32,512]{1,0:T(8,128)S(1)}) custom-call(f32[64,128]{1,0:T(8,128)S(1)} %get-tuple-element.57.vec.state, bf16[64,64,128]{2,1,0:T(8,128)(2,1)S(1)} %get-tuple-element.58.dblock, bf16[32,64,128]{2,1,0:T(8,128)(2,1)} %bitcast.53, f32[32,512]{1,0:T(8,128)} %refs_1_.3), custom_call_target="tpu_custom_call" | custom-call | flops 1073741824 | bytes 1073741824 | tf_op jit(solution)/shard_map/pallas_call | solution.py:23
  28.8 0.0 collective-permute-done.7
  28.8 0.8 %shard_map.96.state = f32[64,128]{1,0:T(8,128)S(1)} custom-call(f32[64,128]{1,0:T(8,128)S(1)} %get-tuple-element.57.vec.state, f32[1,64,128]{2,1,0:T(8,128)S(1)} %bitcast.43, f32[64,128]{1,0:T(8,128)S(1)} %get-tuple-element.59.own, f32[64,128]{1,0:T(8,128)S(1)} %get-tuple-element.56.resid.image, bf16[64,64,128]{2,1,0:T(8,128)(2,1)S(1)} %get-tuple-element.58.dblock, ...), custom_call_target="tpu_custom_call" | custom-call | tf_op jit(solution)/shard_map/pallas_call | solution.py:23
  29.6 4.1 %all-to-all-done.1 = f32[32,1,128]{2,1,0:T(1,128)S(1)} async-done(((f32[32,1,128]{2,1,0:T(1,128)}), f32[32,1,128]{2,1,0:T(1,128)S(1)}, u32[]{:S(2)}, u32[]{:S(2)}) %all-to-all-start.1) | async-done | bytes 16416 | tf_op jit(solution)/shard_map/all_to_all | solution.py:360
  33.7 0.3 shard_map.97
  34.0 0.1 collective-permute-start.8
  34.1 0.6 %collective-permute-start.9 = (f32[16,128]{1,0:T(8,128)S(1)}, f32[16,128]{1,0:T(8,128)S(1)}, u32[]{:S(2)}, u32[]{:S(2)}) collective-permute-start(f32[16,128]{1,0:T(8,128)S(1)} %get-tuple-element.65), channel_id=1, source_target_pairs={{0,2},{2,0},{4,6},{6,4},{8,10},{10,8},{12,14},{14,12},{16,18},{18,... | collective-permute-start | bytes 24584 | tf_op jit(solution)/shard_map/ppermute | solution.py:381
  34.7 0.6 %collective-permute-start.10 = (f32[16,128]{1,0:T(8,128)S(1)}, f32[16,128]{1,0:T(8,128)S(1)}, u32[]{:S(2)}, u32[]{:S(2)}) collective-permute-start(f32[16,128]{1,0:T(8,128)S(1)} %get-tuple-element.66), channel_id=1, source_target_pairs={{0,4},{2,6},{4,0},{6,2},{8,12},{10,14},{12,8},{14,10},{16,20},{18,... | collective-permute-start | bytes 24584 | tf_op jit(solution)/shard_map/ppermute | solution.py:381
  35.3 0.6 %collective-permute-start.11 = (f32[16,128]{1,0:T(8,128)S(1)}, f32[16,128]{1,0:T(8,128)S(1)}, u32[]{:S(2)}, u32[]{:S(2)}) collective-permute-start(f32[16,128]{1,0:T(8,128)S(1)} %get-tuple-element.67), channel_id=1, source_target_pairs={{0,8},{2,10},{4,12},{6,14},{8,0},{10,2},{12,4},{14,6},{16,24},{18,... | collective-permute-start | bytes 24584 | tf_op jit(solution)/shard_map/ppermute | solution.py:381
  35.9 0.0 collective-permute-done.8
  35.9 1.6 %shard_map.98 = (f32[64,128]{1,0:T(8,128)S(1)}, bf16[64,64,96]{2,1,0:T(8,128)(2,1)S(1)}, bf16[64,64,128]{2,1,0:T(8,128)(2,1)S(1)}) custom-call(f32[64,128]{1,0:T(8,128)S(1)} %get-tuple-element.63.vec.second, f32[1,64,128]{2,1,0:T(8,128)S(1)} %bitcast.40, s32[2,128]{1,0:T(2,128)S(1)} %bitcast.38, bf16[2,64,64,128]{3,2,1,0:T(8,128)(2,1)S(1)} %bitcast.29, ...), custom_call_target="tpu_custom_call" | custom-call | tf_op jit(solution)/shard_map/pallas_call | solution.py:23
  37.5 0.3 collective-permute-done.9.near0
  37.8 0.5 %collective-permute-done.10.near1 = f32[16,128]{1,0:T(8,128)S(1)} collective-permute-done((f32[16,128]{1,0:T(8,128)S(1)}, f32[16,128]{1,0:T(8,128)S(1)}, u32[]{:S(2)}, u32[]{:S(2)}) %collective-permute-start.10) | collective-permute-done | bytes 8224 | tf_op jit(solution)/shard_map/ppermute | solution.py:381
  38.3 0.6 %collective-permute-done.11.near2 = f32[16,128]{1,0:T(8,128)S(1)} collective-permute-done((f32[16,128]{1,0:T(8,128)S(1)}, f32[16,128]{1,0:T(8,128)S(1)}, u32[]{:S(2)}, u32[]{:S(2)}) %collective-permute-start.11) | collective-permute-done | bytes 8224 | tf_op jit(solution)/shard_map/ppermute | solution.py:381
  39.0 0.4 shard_map.99
  39.4 9.7 %all_to_all.33 = f32[32,1,128]{2,1,0:T(1,128)S(1)} all-to-all(f32[32,1,128]{2,1,0:T(1,128)S(1)} %bitcast.45), channel_id=1, replica_groups=mesh['sub'=16,'coarse'=2] {'sub','coarse'}, dimensions={0} | all-to-all | bytes 32768 | tf_op jit(solution)/shard_map/all_to_all | solution.py:360
  49.0 0.8 %shard_map.100 = (f32[1,64,128]{2,1,0:T(8,128)}, f32[1,64,128]{2,1,0:T(8,128)}) custom-call(f32[32,128]{1,0:T(8,128)S(1)} %bitcast.32, f32[8,128]{1,0:T(8,128)S(1)} %get-tuple-element.72.alpha, f32[64,128]{1,0:T(8,128)S(1)} %get-tuple-element.47.vec.first, f32[64,128]{1,0:T(8,128)S(1)} %get-tuple-element.63.vec.second, ...), custom_call_target="tpu_custom_call" | custom-call | tf_op jit(solution)/shard_map/pallas_call | solution.py:416
  (4 shorter events, 0.0 us)
Async XLA Ops:
  2.5 8.6 %copy-start = (bf16[1,2,64,64,128]{4,3,2,1,0:T(8,128)(2,1)S(1)}, bf16[1,2,64,64,128]{4,3,2,1,0:T(8,128)(2,1)}, u32[]{:S(2)}) copy-start(bf16[1,2,64,64,128]{4,3,2,1,0:T(8,128)(2,1)} %param.8) | copy-start | bytes 6291460
  2.5 8.6 %copy-start.3 = (s32[1,2,128]{2,1,0:T(2,128)S(1)}, s32[1,2,128]{2,1,0:T(2,128)}, u32[]{:S(2)}) copy-start(s32[1,2,128]{2,1,0:T(2,128)} %param.11) | copy-start | bytes 3076
  2.6 14.4 %all-to-all-start = ((f32[32,1,128]{2,1,0:T(1,128)}), f32[32,1,128]{2,1,0:T(1,128)S(1)}, u32[]{:S(2)}, u32[]{:S(2)}) async-start(f32[32,1,128]{2,1,0:T(1,128)} %bitcast.56), calls=%async_computation | async-start | bytes 32768 | tf_op jit(solution)/shard_map/all_to_all | solution.py:360
  9.9 1.3 %collective-permute-start = (f32[64,128]{1,0:T(8,128)S(1)}, f32[64,128]{1,0:T(8,128)S(1)}, u32[]{:S(2)}, u32[]{:S(2)}) collective-permute-start(f32[64,128]{1,0:T(8,128)S(1)} %get-tuple-element.38.vec.state), channel_id=1, source_target_pairs={{0,1},{1,0},{2,3},{3,2},{4,5},{5,4},{6,7},{7,6},{8,9},{9,8},{10,11... | collective-permute-start | bytes 98312 | tf_op jit(solution)/shard_map/ppermute | solution.py:342
  11.9 1.4 %collective-permute-start.1 = (f32[64,128]{1,0:T(8,128)S(1)}, f32[64,128]{1,0:T(8,128)S(1)}, u32[]{:S(2)}, u32[]{:S(2)}) collective-permute-start(f32[64,128]{1,0:T(8,128)S(1)} %get-tuple-element.41.vec.state), channel_id=1, source_target_pairs={{0,1},{1,0},{2,3},{3,2},{4,5},{5,4},{6,7},{7,6},{8,9},{9,8},{10,11... | collective-permute-start | bytes 98312 | tf_op jit(solution)/shard_map/ppermute | solution.py:342
  13.3 6.1 %copy-start.1 = (bf16[32,64,128]{2,1,0:T(8,128)(2,1)}, bf16[32,64,128]{2,1,0:T(8,128)(2,1)S(1)}, u32[]{:S(2)}) copy-start(bf16[32,64,128]{2,1,0:T(8,128)(2,1)S(1)} %get-tuple-element.45.zvec) | copy-start | bytes 1572868
  17.2 2.2 %collective-permute-start.2 = (f32[64,128]{1,0:T(8,128)S(1)}, f32[64,128]{1,0:T(8,128)S(1)}, u32[]{:S(2)}, u32[]{:S(2)}) collective-permute-start(f32[64,128]{1,0:T(8,128)S(1)} %get-tuple-element.47.vec.first), channel_id=1, source_target_pairs={{0,1},{1,0},{2,3},{3,2},{4,5},{5,4},{6,7},{7,6},{8,9},{9,8},{10,11... | collective-permute-start | bytes 98312 | tf_op jit(solution)/shard_map/ppermute | solution.py:342
  17.3 3.7 %collective-permute-start.3 = (f32[16,128]{1,0:T(8,128)S(1)}, f32[16,128]{1,0:T(8,128)S(1)}, u32[]{:S(2)}, u32[]{:S(2)}) collective-permute-start(f32[16,128]{1,0:T(8,128)S(1)} %get-tuple-element.49), channel_id=1, source_target_pairs={{0,2},{2,0},{4,6},{6,4},{8,10},{10,8},{12,14},{14,12},{16,18},{18,... | collective-permute-start | bytes 24584 | tf_op jit(solution)/shard_map/ppermute | solution.py:381
  17.9 3.7 %collective-permute-start.4 = (f32[16,128]{1,0:T(8,128)S(1)}, f32[16,128]{1,0:T(8,128)S(1)}, u32[]{:S(2)}, u32[]{:S(2)}) collective-permute-start(f32[16,128]{1,0:T(8,128)S(1)} %get-tuple-element.50), channel_id=1, source_target_pairs={{0,4},{2,6},{4,0},{6,2},{8,12},{10,14},{12,8},{14,10},{16,20},{18,... | collective-permute-start | bytes 24584 | tf_op jit(solution)/shard_map/ppermute | solution.py:381
  18.5 3.7 %collective-permute-start.5 = (f32[16,128]{1,0:T(8,128)S(1)}, f32[16,128]{1,0:T(8,128)S(1)}, u32[]{:S(2)}, u32[]{:S(2)}) collective-permute-start(f32[16,128]{1,0:T(8,128)S(1)} %get-tuple-element.51), channel_id=1, source_target_pairs={{0,8},{2,10},{4,12},{6,14},{8,0},{10,2},{12,4},{14,6},{16,24},{18,... | collective-permute-start | bytes 24584 | tf_op jit(solution)/shard_map/ppermute | solution.py:381
  19.4 2.8 %copy-start.2 = (bf16[32,64,128]{2,1,0:T(8,128)(2,1)S(1)}, bf16[32,64,128]{2,1,0:T(8,128)(2,1)}, u32[]{:S(2)}) copy-start(bf16[32,64,128]{2,1,0:T(8,128)(2,1)} %copy-done.1) | copy-start | bytes 1572868
  23.3 3.3 %collective-permute-start.6 = (f32[64,128]{1,0:T(8,128)S(1)}, f32[64,128]{1,0:T(8,128)S(1)}, u32[]{:S(2)}, u32[]{:S(2)}) collective-permute-start(f32[64,128]{1,0:T(8,128)S(1)} %get-tuple-element.54.state), channel_id=1, source_target_pairs={{0,1},{1,0},{2,3},{3,2},{4,5},{5,4},{6,7},{7,6},{8,9},{9,8},{10,11... | collective-permute-start | bytes 98312 | tf_op jit(solution)/shard_map/ppermute | solution.py:342
  23.4 10.3 %all-to-all-start.1 = ((f32[32,1,128]{2,1,0:T(1,128)}), f32[32,1,128]{2,1,0:T(1,128)S(1)}, u32[]{:S(2)}, u32[]{:S(2)}) async-start(f32[32,1,128]{2,1,0:T(1,128)} %bitcast.55), calls=%async_computation.1 | async-start | bytes 32768 | tf_op jit(solution)/shard_map/all_to_all | solution.py:360
  27.4 1.4 %collective-permute-start.7 = (f32[64,128]{1,0:T(8,128)S(1)}, f32[64,128]{1,0:T(8,128)S(1)}, u32[]{:S(2)}, u32[]{:S(2)}) collective-permute-start(f32[64,128]{1,0:T(8,128)S(1)} %get-tuple-element.57.vec.state), channel_id=1, source_target_pairs={{0,1},{1,0},{2,3},{3,2},{4,5},{5,4},{6,7},{7,6},{8,9},{9,8},{10,11... | collective-permute-start | bytes 98312 | tf_op jit(solution)/shard_map/ppermute | solution.py:342
  34.0 1.9 %collective-permute-start.8 = (f32[64,128]{1,0:T(8,128)S(1)}, f32[64,128]{1,0:T(8,128)S(1)}, u32[]{:S(2)}, u32[]{:S(2)}) collective-permute-start(f32[64,128]{1,0:T(8,128)S(1)} %get-tuple-element.63.vec.second), channel_id=1, source_target_pairs={{0,1},{1,0},{2,3},{3,2},{4,5},{5,4},{6,7},{7,6},{8,9},{9,8},{10,11... | collective-permute-start | bytes 98312 | tf_op jit(solution)/shard_map/ppermute | solution.py:342
  34.1 3.7 %collective-permute-start.9 = (f32[16,128]{1,0:T(8,128)S(1)}, f32[16,128]{1,0:T(8,128)S(1)}, u32[]{:S(2)}, u32[]{:S(2)}) collective-permute-start(f32[16,128]{1,0:T(8,128)S(1)} %get-tuple-element.65), channel_id=1, source_target_pairs={{0,2},{2,0},{4,6},{6,4},{8,10},{10,8},{12,14},{14,12},{16,18},{18,... | collective-permute-start | bytes 24584 | tf_op jit(solution)/shard_map/ppermute | solution.py:381
  34.7 3.7 %collective-permute-start.10 = (f32[16,128]{1,0:T(8,128)S(1)}, f32[16,128]{1,0:T(8,128)S(1)}, u32[]{:S(2)}, u32[]{:S(2)}) collective-permute-start(f32[16,128]{1,0:T(8,128)S(1)} %get-tuple-element.66), channel_id=1, source_target_pairs={{0,4},{2,6},{4,0},{6,2},{8,12},{10,14},{12,8},{14,10},{16,20},{18,... | collective-permute-start | bytes 24584 | tf_op jit(solution)/shard_map/ppermute | solution.py:381
  35.3 3.7 %collective-permute-start.11 = (f32[16,128]{1,0:T(8,128)S(1)}, f32[16,128]{1,0:T(8,128)S(1)}, u32[]{:S(2)}, u32[]{:S(2)}) collective-permute-start(f32[16,128]{1,0:T(8,128)S(1)} %get-tuple-element.67), channel_id=1, source_target_pairs={{0,8},{2,10},{4,12},{6,14},{8,0},{10,2},{12,4},{14,6},{16,24},{18,... | collective-permute-start | bytes 24584 | tf_op jit(solution)/shard_map/ppermute | solution.py:381
